TPU v7x, 512 devices: a whole 4x8x8 slice. The times are simulated.
512 devices in a mesh: view: 8 (over x, core), blk: 64 (over z, y).
Axes of the slice: x: 4, y: 8, z: 8, core: 2. Of those that a mesh axis runs over, the one named last changes fastest.
Arguments:
- estimate: float32 [2, 1024, 1024], P(None, 'blk'), may hold values from 0.5 to 2
- measured: float32 [8, 2, 1024, 1024], P('view', None, 'blk'), may hold values from 0.25 to 4
- psf_z: float32 [8, 3, 31], P('view'), may hold values from 0.05 to 1
- psf_y: float32 [8, 3, 31], P('view'), may hold values from 0.05 to 1
- psf_x: float32 [8, 3, 31], P('view'), may hold values from 0.05 to 1
- psf_mix: float32 [8, 3], P('view'), may hold values from 0.2 to 1
- weight_tiles: float32 [8, 8, 1024], replicated, may hold values from 0.1 to 1
- tile_index: int32 [8, 128], P('view', 'blk'), may hold values from 0 to 7
- src_row: int32 [8, 1024], P('view', 'blk'), may hold values from 0 to 1023, as said below
- dst_row: int32 [8, 1024], P('view', 'blk'), may hold values from 0 to 1023, as said below
- col_shift: int32 [8, 1024], P('view', 'blk'), may hold values from -8 to 8
- back_shift: int32 [8, 1024], P('view', 'blk'), may hold values from -8 to 8, as said below
Outputs:
- estimate_out: float32 [2, 1024, 1024], P(None, 'blk')
Inputs may be any that keep to these rules, and one draw needn't show every extreme that they name: For each view, src_row is a permutation of the 1024 output rows. The slab's rows form device blocks of 16 rows, and for each view the blocks pair up with an adjacent block (or stay alone at an end); a row's source lies in its own block or in its partner's, equally many rows cross each way between partners, at most 8, and exactly 8 for some pair in every view. dst_row[v] is the inverse permutation of src_row[v]. back_shift[v, i] = col_shift[v, dst_row[v, i]].
All inputs are finite; a program needn't handle non-finite values.
Results may differ from a plain program's by a relative error of at most 0.0003.
Values sent between devices are 32-bit elements; how exact they have to be, the bound alone decides.
No kernel may reach another device: no remote copies, remote signals or barrier semaphores. Data moves between devices by JAX's collectives and lax.ppermute only.
A program may use at most 64 MiB of HBM per device.

v0:
```python
import jax
import jax.numpy as jnp
from jax import lax
from jax.sharding import PartitionSpec as P

SHIFT_MAX = 8
ITERS = 2


def extended(block, sides, width):
    for axis, dim in sides:
        count = lax.axis_size(axis)
        forward = [(i, i + 1) for i in range(count - 1)]
        backward = [(target, source) for source, target in forward]
        low = lax.ppermute(
            lax.slice_in_dim(block, block.shape[dim] - width, None, axis=dim), axis, forward
        )
        high = lax.ppermute(lax.slice_in_dim(block, 0, width, axis=dim), axis, backward)
        block = jnp.concatenate([low, block, high], axis=dim)
    return block


def from_behind(block, axis, distance):
    devices = range(lax.axis_size(axis))
    route = [(i - distance, i) for i in devices if i - distance in devices]
    return lax.ppermute(block, axis, route)


def normalized(values):
    return values / jnp.sum(values, axis=-1, keepdims=True)


def band_matrix(taps_vec, size_in, size_out, offset):
    index_in = lax.broadcasted_iota(jnp.int32, (size_in, size_out), 0)
    index_out = lax.broadcasted_iota(jnp.int32, (size_in, size_out), 1)
    spread = index_in - index_out - offset
    valid = (spread >= 0) & (spread < taps_vec.shape[0])
    return jnp.where(valid, taps_vec[jnp.clip(spread, 0, taps_vec.shape[0] - 1)], 0.0)


def along_planes(values, taps_vec):
    radius = taps_vec.shape[0] // 2
    matrix = band_matrix(taps_vec, values.shape[0], values.shape[0], -radius)
    return jnp.einsum("wyx,wo->oyx", values, matrix, precision=lax.Precision.HIGHEST)


def along_rows(values, taps_vec, row_count):
    matrix = band_matrix(taps_vec, values.shape[1], row_count, 0)
    return jnp.einsum("zwx,wo->zox", values, matrix, precision=lax.Precision.HIGHEST)


def along_columns(values, taps_vec):
    planes, row_count, col_count = values.shape
    radius = taps_vec.shape[0] // 2
    block = 128
    blocks = values.reshape(planes, row_count, col_count // block, block)
    matrix = band_matrix(taps_vec, 3 * block, block, block - radius)
    left_part = matrix[:block]
    middle_part = matrix[block : 2 * block]
    right_part = matrix[2 * block :]
    result = jnp.einsum("zrbw,wo->zrbo", blocks, middle_part, precision=lax.Precision.HIGHEST)
    from_left = jnp.einsum(
        "zrbw,wo->zrbo", blocks[:, :, :-1], left_part, precision=lax.Precision.HIGHEST
    )
    from_right = jnp.einsum(
        "zrbw,wo->zrbo", blocks[:, :, 1:], right_part, precision=lax.Precision.HIGHEST
    )
    result = result + jnp.pad(from_left, ((0, 0), (0, 0), (1, 0), (0, 0)))
    result = result + jnp.pad(from_right, ((0, 0), (0, 0), (0, 1), (0, 0)))
    return result.reshape(planes, row_count, col_count)


def blurring(values, depth_taps, row_taps, column_taps, mixing, flipped):
    radius = column_taps.shape[1] // 2
    row_count = values.shape[1]
    padded = extended(values, (("blk", 1),), radius)
    result = jnp.zeros_like(values)
    for term in range(depth_taps.shape[0]):
        first_taps, second_taps, third_taps = (depth_taps[term], row_taps[term], column_taps[term])
        if flipped:
            first_taps, second_taps, third_taps = (
                first_taps[::-1],
                second_taps[::-1],
                third_taps[::-1],
            )
        layer = along_rows(padded, second_taps, row_count)
        layer = along_planes(layer, first_taps)
        layer = along_columns(layer, third_taps)
        result = result + mixing[term] * layer
    return result


def shift_columns(values, offsets):
    col_count = values.shape[2]
    padded = jnp.pad(values, ((0, 0), (0, 0), (SHIFT_MAX, SHIFT_MAX)))
    result = jnp.zeros_like(values)
    for amount in range(-SHIFT_MAX, SHIFT_MAX + 1):
        moved = padded[:, :, amount + SHIFT_MAX : amount + SHIFT_MAX + col_count]
        result = jnp.where((offsets == amount)[None, :, None], moved, result)
    return result


def relayout(values, wanted, first_row):
    row_count = values.shape[1]
    arrived_parts = []
    for direction in (1, -1):
        arrived_parts.append(from_behind(values, "blk", direction))
    stacked = jnp.concatenate([arrived_parts[0], values, arrived_parts[1]], axis=1)
    stack_index = wanted - (first_row - row_count)
    columns_of = lax.broadcasted_iota(jnp.int32, (row_count, 3 * row_count), 1)
    selector = (stack_index[:, None] == columns_of).astype(jnp.float32)
    result = jnp.einsum("iw,zwx->zix", selector, stacked, precision=lax.Precision.HIGHEST)
    return result


def body(
    estimate,
    measured,
    psf_z,
    psf_y,
    psf_x,
    psf_mix,
    weight_tiles,
    tile_index,
    src_row,
    dst_row,
    col_shift,
    back_shift,
):
    planes, row_count, col_count = estimate.shape
    first_row = lax.axis_index("blk") * row_count
    depth_taps = normalized(psf_z[0])
    row_taps = normalized(psf_y[0])
    column_taps = normalized(psf_x[0])
    mixing = normalized(psf_mix[0])
    tile_count = weight_tiles.shape[0]
    tile_ids = lax.broadcasted_iota(jnp.int32, (1, tile_count), 1)
    chooser = (tile_index[0][:, None] == tile_ids).astype(jnp.float32)
    weights = jnp.einsum(
        "bt,twx->bwx", chooser, weight_tiles, precision=lax.Precision.HIGHEST
    ).reshape(row_count, col_count)
    weight_total = lax.psum(weights, "view")
    current = estimate
    for iteration in range(ITERS):
        aligned = shift_columns(relayout(current, src_row[0], first_row), col_shift[0])
        blurred = blurring(aligned, depth_taps, row_taps, column_taps, mixing, False)
        quotient = measured[0] / blurred
        adjoint = blurring(quotient, depth_taps, row_taps, column_taps, mixing, True)
        returned = shift_columns(relayout(adjoint, dst_row[0], first_row), back_shift[0])
        weighted = weights[None] * returned
        combined = lax.psum(weighted, "view")
        current = current * combined / weight_total[None]
    return current


def solution(mesh):
    in_specs = (
        P(None, "blk", None),
        P("view", None, "blk", None),
        P("view", None, None),
        P("view", None, None),
        P("view", None, None),
        P("view", None),
        P(),
        P("view", "blk"),
        P("view", "blk"),
        P("view", "blk"),
        P("view", "blk"),
        P("view", "blk"),
    )
    out_specs = P(None, "blk", None)
    return jax.shard_map(body, mesh=mesh, in_specs=in_specs, out_specs=out_specs, check_vma=False)
```

profile of v0, /device:TPU:8, one launch (start us, length us, event | category | flops | bytes accessed | tf_op | source)
XLA Modules:
  0.0 446.4 jit_solution(6564573955339695543)
XLA Ops:
  6.5 7.9 %collective-permute-start.1 = (f32[2,16,1024]{2,1,0:T(8,128)}, f32[2,16,1024]{2,1,0:T(8,128)S(1)}, u32[]{:S(2)}, u32[]{:S(2)}) collective-permute-start(f32[2,16,1024]{2,1,0:T(8,128)} %param.12), channel_id=1, source_target_pairs={{1,0},{2,1},{3,2},{4,3},{5,4},{6,5},{7,6},{8,7},{9,8},{10,9},{11,1... | collective-permute-start | bytes 393224 | tf_op jit(solution)/shard_map/ppermute | solution.py:26
  14.4 1.9 collective-permute-start
  20.9 19.5 %select_select_fusion.3 = f32[384,128]{1,0:T(8,128)S(1)} fusion(f32[]{:T(128)} %bitcast.169, f32[]{:T(128)} %bitcast.170, f32[]{:T(128)} %bitcast.171, f32[]{:T(128)} %bitcast.172, f32[]{:T(128)} %bitcast.173, f32[]{:T(128)} %bitcast.175, f32[]{:T(128)} %bitcast.174, f32[]{:T(128)} %bitcast.145, f32[]{:T(128)} %bitcast.146, f32[]{:T(128)} %bitcast.147, ...), kind=kLoop, calls=%fused_computation.210 | loop fusion | flops 3538944 | bytes 196732 | tf_op jit(solution)/shard_map/jit(_where)/select_n | solution.py:38
  40.3 19.5 %select_select_fusion = f32[384,128]{1,0:T(8,128)S(1)} fusion(f32[]{:T(128)} %bitcast.151, f32[]{:T(128)} %bitcast.150, f32[]{:T(128)} %bitcast.149, f32[]{:T(128)} %bitcast.148, f32[]{:T(128)} %bitcast.147, f32[]{:T(128)} %bitcast.146, f32[]{:T(128)} %bitcast.145, f32[]{:T(128)} %bitcast.152, f32[]{:T(128)} %bitcast.153, f32[]{:T(128)} %bitcast.154, ...), kind=kLoop, calls=%fused_computation.207 | loop fusion | flops 3538944 | bytes 196732 | tf_op jit(solution)/shard_map/jit(_where)/select_n | solution.py:38
  66.7 19.6 %select_select_fusion.4 = f32[384,128]{1,0:T(8,128)S(1)} fusion(f32[]{:T(128)} %bitcast.125, f32[]{:T(128)} %bitcast.126, f32[]{:T(128)} %bitcast.127, f32[]{:T(128)} %bitcast.128, f32[]{:T(128)} %bitcast.129, f32[]{:T(128)} %bitcast.131, f32[]{:T(128)} %bitcast.130, f32[]{:T(128)} %bitcast.101, f32[]{:T(128)} %bitcast.102, f32[]{:T(128)} %bitcast.103, ...), kind=kLoop, calls=%fused_computation.211 | loop fusion | flops 3538944 | bytes 196732 | tf_op jit(solution)/shard_map/jit(_where)/select_n | solution.py:38
  86.4 4.8 %gather_fusion.7 = f32[736]{0:T(1024)S(1)} fusion(f32[31]{0:T(128)S(1)} %get-tuple-element.136, s32[1024]{0:T(1024)S(1)} %pad_clamp_fusion), kind=kCustom, calls=%fused_computation.7 | custom fusion | bytes 8832 | tf_op jit(solution)/shard_map/gather | solution.py:38
  91.1 4.8 %gather_fusion.5 = f32[736]{0:T(1024)S(1)} fusion(f32[31]{0:T(128)S(1)} %get-tuple-element.137, s32[1024]{0:T(1024)S(1)} %pad_clamp_fusion), kind=kCustom, calls=%fused_computation.5 | custom fusion | bytes 8832 | tf_op jit(solution)/shard_map/gather | solution.py:38
  97.5 4.8 %gather_fusion.3 = f32[736]{0:T(1024)S(1)} fusion(f32[31]{0:T(128)S(1)} %get-tuple-element.135, s32[1024]{0:T(1024)S(1)} %pad_clamp_fusion), kind=kCustom, calls=%fused_computation.3 | custom fusion | bytes 8832 | tf_op jit(solution)/shard_map/gather | solution.py:38
  103.6 4.8 %gather_fusion.11 = f32[736]{0:T(1024)S(1)} fusion(f32[31]{0:T(128)S(1)} %rev.43, s32[1024]{0:T(1024)S(1)} %pad_clamp_fusion), kind=kCustom, calls=%fused_computation.11 | custom fusion | bytes 8832 | tf_op jit(solution)/shard_map/gather | solution.py:38
  109.2 4.8 %gather_fusion.9 = f32[736]{0:T(1024)S(1)} fusion(f32[31]{0:T(128)S(1)} %rev.40, s32[1024]{0:T(1024)S(1)} %pad_clamp_fusion), kind=kCustom, calls=%fused_computation.9 | custom fusion | bytes 8832 | tf_op jit(solution)/shard_map/gather | solution.py:38
  114.8 4.8 %gather_fusion.1 = f32[736]{0:T(1024)S(1)} fusion(f32[31]{0:T(128)S(1)} %rev.37, s32[1024]{0:T(1024)S(1)} %pad_clamp_fusion), kind=kCustom, calls=%fused_computation.1 | custom fusion | bytes 8832 | tf_op jit(solution)/shard_map/gather | solution.py:38
  120.3 19.6 %select_select_fusion.1 = f32[384,128]{1,0:T(8,128)S(1)} fusion(f32[]{:T(128)} %bitcast.107, f32[]{:T(128)} %bitcast.106, f32[]{:T(128)} %bitcast.105, f32[]{:T(128)} %bitcast.104, f32[]{:T(128)} %bitcast.103, f32[]{:T(128)} %bitcast.102, f32[]{:T(128)} %bitcast.101, f32[]{:T(128)} %bitcast.108, f32[]{:T(128)} %bitcast.109, f32[]{:T(128)} %bitcast.110, ...), kind=kLoop, calls=%fused_computation.208 | loop fusion | flops 3538944 | bytes 196732 | tf_op jit(solution)/shard_map/jit(_where)/select_n | solution.py:38
  140.9 3.9 collective-permute-start.3
  144.8 2.1 collective-permute-start.2
  146.9 19.5 %select_select_fusion.5 = f32[384,128]{1,0:T(8,128)S(1)} fusion(f32[]{:T(128)} %bitcast.81, f32[]{:T(128)} %bitcast.82, f32[]{:T(128)} %bitcast.83, f32[]{:T(128)} %bitcast.84, f32[]{:T(128)} %bitcast.85, f32[]{:T(128)} %bitcast.87, f32[]{:T(128)} %bitcast.86, f32[]{:T(128)} %bitcast.34, f32[]{:T(128)} %bitcast.36, f32[]{:T(128)} %bitcast.38, f32[]{:T(128)} %bitcast.40, ...), kind=kLoop, calls=%fused_computation.212 | loop fusion | flops 3538944 | bytes 196732 | tf_op jit(solution)/shard_map/jit(_where)/select_n | solution.py:38
  175.6 3.9 collective-permute-start.5
  179.5 1.9 collective-permute-start.4
  181.6 19.5 %select_select_fusion.2 = f32[384,128]{1,0:T(8,128)S(1)} fusion(f32[]{:T(128)} %bitcast.46, f32[]{:T(128)} %bitcast.44, f32[]{:T(128)} %bitcast.42, f32[]{:T(128)} %bitcast.40, f32[]{:T(128)} %bitcast.38, f32[]{:T(128)} %bitcast.36, f32[]{:T(128)} %bitcast.34, f32[]{:T(128)} %bitcast.48, f32[]{:T(128)} %bitcast.50, f32[]{:T(128)} %bitcast.52, f32[]{:T(128)} %bitcast.54, ...), kind=kLoop, calls=%fused_computation.209 | loop fusion | flops 3538944 | bytes 196732 | tf_op jit(solution)/shard_map/jit(_where)/select_n | solution.py:38
  209.3 4.1 collective-permute-start.7
  216.4 3.9 collective-permute-done.6
  222.0 79.8 %all-reduce.34.cloned.1.call-done = (f32[2,16,1024]{2,1,0:T(8,128)}, f32[16,1024]{1,0:T(8,128)}) async-done(((f32[2,16,1024]{2,1,0:T(8,128)}, f32[16,1024]{1,0:T(8,128)}), (f32[2,16,1024]{2,1,0:T(8,128)}, f32[16,1024]{1,0:T(8,128)})) %all-reduce.34.cloned.1.call-update) | async-done | bytes 196624 | tf_op jit(solution)/shard_map/psum | solution.py:151
  302.7 2.5 collective-permute-start.9
  305.2 3.4 collective-permute-start.8
  309.6 2.5 collective-permute-done.8
  314.9 3.9 collective-permute-start.10
  319.9 1.9 collective-permute-done.10
  332.0 4.2 collective-permute-start.12
  337.0 1.9 collective-permute-done.12
  347.2 2.1 collective-permute-start.15
  349.2 3.9 collective-permute-start.14
  354.2 1.9 collective-permute-done.14
  357.7 80.3 %all-reduce.32.cloned.1.call-done = f32[2,16,1024]{2,1,0:T(8,128)} async-done(((f32[2,16,1024]{2,1,0:T(8,128)}), f32[2,16,1024]{2,1,0:T(8,128)}) %all-reduce.32.cloned.1.call-update) | async-done | bytes 131088 | tf_op jit(solution)/shard_map/psum | solution.py:151
  (228 shorter events, 67.9 us)
Async XLA Ops:
  6.5 59.1 %copy-start = (f32[8,8,1024]{2,1,0:T(8,128)S(1)}, f32[8,8,1024]{2,1,0:T(8,128)}, u32[]{:S(2)}) copy-start(f32[8,8,1024]{2,1,0:T(8,128)} %param.18) | copy-start | bytes 786436
  6.5 295.3 %all-reduce.34.cloned.1.call-start = ((), (), s32[]{:S(2)}) async-start(), calls=%async_computation.1 | async-start | bytes 393216 | tf_op jit(solution)/shard_map/psum | solution.py:151
  6.5 133.3 %collective-permute-start.1 = (f32[2,16,1024]{2,1,0:T(8,128)}, f32[2,16,1024]{2,1,0:T(8,128)S(1)}, u32[]{:S(2)}, u32[]{:S(2)}) collective-permute-start(f32[2,16,1024]{2,1,0:T(8,128)} %param.12), channel_id=1, source_target_pairs={{1,0},{2,1},{3,2},{4,3},{5,4},{6,5},{7,6},{8,7},{9,8},{10,9},{11,1... | collective-permute-start | bytes 393224 | tf_op jit(solution)/shard_map/ppermute | solution.py:26
  14.4 125.5 %collective-permute-start = (f32[2,16,1024]{2,1,0:T(8,128)}, f32[2,16,1024]{2,1,0:T(8,128)S(1)}, u32[]{:S(2)}, u32[]{:S(2)}) collective-permute-start(f32[2,16,1024]{2,1,0:T(8,128)} %param.12), channel_id=1, source_target_pairs={{0,1},{1,2},{2,3},{3,4},{4,5},{5,6},{6,7},{7,8},{8,9},{9,10},{10,1... | collective-permute-start | bytes 393224 | tf_op jit(solution)/shard_map/ppermute | solution.py:26
  16.4 0.7 copy-start.6
  59.8 0.7 copy-start.10
  60.5 0.7 copy-start.7
  61.4 0.7 copy-start.8
  62.3 0.7 copy-start.12
  64.3 0.7 copy-start.11
  65.0 0.7 copy-start.13
  120.3 19.6 %copy-start.3 = (f32[2,16,1024]{2,1,0:T(8,128)S(1)}, f32[2,16,1024]{2,1,0:T(8,128)}, u32[]{:S(2)}) copy-start(f32[2,16,1024]{2,1,0:T(8,128)} %param.12) | copy-start | bytes 393220
  140.9 25.5 %collective-permute-start.3 = (f32[2,15,1024]{2,1,0:T(8,128)S(1)}, f32[2,15,1024]{2,1,0:T(8,128)S(1)}, u32[]{:S(2)}, u32[]{:S(2)}) collective-permute-start(f32[2,15,1024]{2,1,0:T(8,128)S(1)} %get-tuple-element.38), channel_id=1, source_target_pairs={{1,0},{2,1},{3,2},{4,3},{5,4},{6,5},{7,6},{8,7},{9,8},{10,9},{11,1... | collective-permute-start | bytes 368648 | tf_op jit(solution)/shard_map/ppermute | solution.py:18
  144.8 21.6 %collective-permute-start.2 = (f32[2,15,1024]{2,1,0:T(8,128)S(1)}, f32[2,15,1024]{2,1,0:T(8,128)S(1)}, u32[]{:S(2)}, u32[]{:S(2)}) collective-permute-start(f32[2,15,1024]{2,1,0:T(8,128)S(1)} %get-tuple-element.37), channel_id=1, source_target_pairs={{0,1},{1,2},{2,3},{3,4},{4,5},{5,6},{6,7},{7,8},{8,9},{9,10},{10,1... | collective-permute-start | bytes 368648 | tf_op jit(solution)/shard_map/ppermute | solution.py:15
  174.6 0.9 copy-start.4
  175.6 25.5 %collective-permute-start.5 = (f32[2,15,1024]{2,1,0:T(8,128)S(1)}, f32[2,15,1024]{2,1,0:T(8,128)S(1)}, u32[]{:S(2)}, u32[]{:S(2)}) collective-permute-start(f32[2,15,1024]{2,1,0:T(8,128)S(1)} %get-tuple-element.30), channel_id=1, source_target_pairs={{1,0},{2,1},{3,2},{4,3},{5,4},{6,5},{7,6},{8,7},{9,8},{10,9},{11,1... | collective-permute-start | bytes 368648 | tf_op jit(solution)/shard_map/ppermute | solution.py:18
  179.5 21.5 %collective-permute-start.4 = (f32[2,15,1024]{2,1,0:T(8,128)S(1)}, f32[2,15,1024]{2,1,0:T(8,128)S(1)}, u32[]{:S(2)}, u32[]{:S(2)}) collective-permute-start(f32[2,15,1024]{2,1,0:T(8,128)S(1)} %get-tuple-element.29), channel_id=1, source_target_pairs={{0,1},{1,2},{2,3},{3,4},{4,5},{5,6},{6,7},{7,8},{8,9},{9,10},{10,1... | collective-permute-start | bytes 368648 | tf_op jit(solution)/shard_map/ppermute | solution.py:15
  181.6 39.1 %copy-start.1 = (f32[2,8,1024]{2,1,0:T(8,128)}, f32[2,8,1024]{2,1,0:T(8,128)S(1)}, u32[]{:S(2)}) copy-start(f32[2,8,1024]{2,1,0:T(8,128)S(1)} %copy.367) | copy-start | bytes 196612
  209.3 6.1 %copy-start.14 = (s32[1,16]{1,0:T(1,128)S(1)}, s32[1,16]{1,0:T(1,128)}, u32[]{:S(2)}) copy-start(s32[1,16]{1,0:T(1,128)} %param.21) | copy-start | bytes 196
  209.3 7.1 %collective-permute-start.7 = (f32[2,16,1024]{2,1,0:T(8,128)S(1)}, f32[2,16,1024]{2,1,0:T(8,128)S(1)}, u32[]{:S(2)}, u32[]{:S(2)}) collective-permute-start(f32[2,16,1024]{2,1,0:T(8,128)S(1)} %add.304), channel_id=1, source_target_pairs={{1,0},{2,1},{3,2},{4,3},{5,4},{6,5},{7,6},{8,7},{9,8},{10,9},{11,1... | collective-permute-start | bytes 393224 | tf_op jit(solution)/shard_map/ppermute | solution.py:26
  213.5 6.9 %collective-permute-start.6 = (f32[2,16,1024]{2,1,0:T(8,128)S(1)}, f32[2,16,1024]{2,1,0:T(8,128)S(1)}, u32[]{:S(2)}, u32[]{:S(2)}) collective-permute-start(f32[2,16,1024]{2,1,0:T(8,128)S(1)} %add.304), channel_id=1, source_target_pairs={{0,1},{1,2},{2,3},{3,4},{4,5},{5,6},{6,7},{7,8},{8,9},{9,10},{10,1... | collective-permute-start | bytes 393224 | tf_op jit(solution)/shard_map/ppermute | solution.py:26
  222.0 216.1 %all-reduce.32.cloned.1.call-start = ((), (), s32[]{:S(2)}) async-start(), calls=%async_computation | async-start | bytes 262144 | tf_op jit(solution)/shard_map/psum | solution.py:151
  302.7 6.9 %collective-permute-start.9 = (f32[2,16,1024]{2,1,0:T(8,128)S(1)}, f32[2,16,1024]{2,1,0:T(8,128)S(1)}, u32[]{:S(2)}, u32[]{:S(2)}) collective-permute-start(f32[2,16,1024]{2,1,0:T(8,128)S(1)} %multiply_divide_fusion.1), channel_id=1, source_target_pairs={{1,0},{2,1},{3,2},{4,3},{5,4},{6,5},{7,6},{8,7},{9,8},{10,9},{11,1... | collective-permute-start | bytes 393224 | tf_op jit(solution)/shard_map/ppermute | solution.py:26
  305.2 6.9 %collective-permute-start.8 = (f32[2,16,1024]{2,1,0:T(8,128)S(1)}, f32[2,16,1024]{2,1,0:T(8,128)S(1)}, u32[]{:S(2)}, u32[]{:S(2)}) collective-permute-start(f32[2,16,1024]{2,1,0:T(8,128)S(1)} %multiply_divide_fusion.1), channel_id=1, source_target_pairs={{0,1},{1,2},{2,3},{3,4},{4,5},{5,6},{6,7},{7,8},{8,9},{9,10},{10,1... | collective-permute-start | bytes 393224 | tf_op jit(solution)/shard_map/ppermute | solution.py:26
  313.0 6.9 %collective-permute-start.11 = (f32[2,15,1024]{2,1,0:T(8,128)S(1)}, f32[2,15,1024]{2,1,0:T(8,128)S(1)}, u32[]{:S(2)}, u32[]{:S(2)}) collective-permute-start(f32[2,15,1024]{2,1,0:T(8,128)S(1)} %get-tuple-element.22), channel_id=1, source_target_pairs={{1,0},{2,1},{3,2},{4,3},{5,4},{6,5},{7,6},{8,7},{9,8},{10,9},{11,1... | collective-permute-start | bytes 368648 | tf_op jit(solution)/shard_map/ppermute | solution.py:18
  314.9 6.9 %collective-permute-start.10 = (f32[2,15,1024]{2,1,0:T(8,128)S(1)}, f32[2,15,1024]{2,1,0:T(8,128)S(1)}, u32[]{:S(2)}, u32[]{:S(2)}) collective-permute-start(f32[2,15,1024]{2,1,0:T(8,128)S(1)} %get-tuple-element.21), channel_id=1, source_target_pairs={{0,1},{1,2},{2,3},{3,4},{4,5},{5,6},{6,7},{7,8},{8,9},{9,10},{10,1... | collective-permute-start | bytes 368648 | tf_op jit(solution)/shard_map/ppermute | solution.py:15
  330.1 6.9 %collective-permute-start.13 = (f32[2,15,1024]{2,1,0:T(8,128)S(1)}, f32[2,15,1024]{2,1,0:T(8,128)S(1)}, u32[]{:S(2)}, u32[]{:S(2)}) collective-permute-start(f32[2,15,1024]{2,1,0:T(8,128)S(1)} %get-tuple-element.14), channel_id=1, source_target_pairs={{1,0},{2,1},{3,2},{4,3},{5,4},{6,5},{7,6},{8,7},{9,8},{10,9},{11,1... | collective-permute-start | bytes 368648 | tf_op jit(solution)/shard_map/ppermute | solution.py:18
  332.0 6.9 %collective-permute-start.12 = (f32[2,15,1024]{2,1,0:T(8,128)S(1)}, f32[2,15,1024]{2,1,0:T(8,128)S(1)}, u32[]{:S(2)}, u32[]{:S(2)}) collective-permute-start(f32[2,15,1024]{2,1,0:T(8,128)S(1)} %get-tuple-element.13), channel_id=1, source_target_pairs={{0,1},{1,2},{2,3},{3,4},{4,5},{5,6},{6,7},{7,8},{8,9},{9,10},{10,1... | collective-permute-start | bytes 368648 | tf_op jit(solution)/shard_map/ppermute | solution.py:15
  347.1 9.2 %copy-start.2 = (f32[2,8,1024]{2,1,0:T(8,128)S(1)}, f32[2,8,1024]{2,1,0:T(8,128)}, u32[]{:S(2)}) copy-start(f32[2,8,1024]{2,1,0:T(8,128)} %copy-done.1) | copy-start | bytes 196612
  347.2 7.0 %collective-permute-start.15 = (f32[2,16,1024]{2,1,0:T(8,128)S(1)}, f32[2,16,1024]{2,1,0:T(8,128)S(1)}, u32[]{:S(2)}, u32[]{:S(2)}) collective-permute-start(f32[2,16,1024]{2,1,0:T(8,128)S(1)} %add.322), channel_id=1, source_target_pairs={{1,0},{2,1},{3,2},{4,3},{5,4},{6,5},{7,6},{8,7},{9,8},{10,9},{11,1... | collective-permute-start | bytes 393224 | tf_op jit(solution)/shard_map/ppermute | solution.py:26
  349.2 6.9 %collective-permute-start.14 = (f32[2,16,1024]{2,1,0:T(8,128)S(1)}, f32[2,16,1024]{2,1,0:T(8,128)S(1)}, u32[]{:S(2)}, u32[]{:S(2)}) collective-permute-start(f32[2,16,1024]{2,1,0:T(8,128)S(1)} %add.322), channel_id=1, source_target_pairs={{0,1},{1,2},{2,3},{3,4},{4,5},{5,6},{6,7},{7,8},{8,9},{9,10},{10,1... | collective-permute-start | bytes 393224 | tf_op jit(solution)/shard_map/ppermute | solution.py:26
  357.7 80.4 %copy-start.5 = (f32[16,1024]{1,0:T(8,128)S(1)}, f32[16,1024]{1,0:T(8,128)}, u32[]{:S(2)}) copy-start(f32[16,1024]{1,0:T(8,128)} %get-tuple-element.6) | copy-start | bytes 196612
  (1 other events, 0.7 us)
Sparse Core Ops, SparseCore 0:
  222.1 79.6 all-reduce.33
  357.8 80.1 all-reduce.31
where the time goes:
time: 449 us; the launch traced here: 446 us
  waiting for transfers between devices  177 us (39%)
  other arithmetic  125 us (28%)
  starting transfers between devices  51.5 us (11%)
  local copies, waits for them, and re-layouts  46.7 us (10%)
  matrix products  30.9 us (7%)
  between operations  14.8 us (3%)
    psum x2, waiting for transfers between devices, body(): combined = lax.psum(weighted, 'view')  160 us
    select_n x6, other arithmetic, band_matrix(): jnp.where(valid, taps_vec[jnp.clip(spread, 0, taps_vec.shape[0] - 1)], 0.0)  117 us
    gather x29, local copies, waits for them, and re-layouts, band_matrix(): taps_vec[jnp.clip(spread, 0, taps_vec.shape[0] - 1)]  37.1 us
    ppermute x8, starting transfers between devices, from_behind(): return lax.ppermute(block, axis, route)  27.7 us
    ppermute x4, starting transfers between devices, extended(): lax.ppermute(lax.slice_in_dim(block, block.shape[dim] - width, None, axis...  12.1 us
    ppermute x4, starting transfers between devices, extended(): lax.ppermute(lax.slice_in_dim(block, 0, width, axis=dim), axis, backward)  11.7 us
    ppermute x8, waiting for transfers between devices, from_behind(): return lax.ppermute(block, axis, route)  11.3 us
    dot_general x12, matrix products, along_columns(): jnp.einsum('zrbw,wo->zrbo', blocks, middle_part, precision=lax.Precision....  10.7 us
  transfers between devices with their start and end apart: 18, of which 12 were waited for; matrix products, arithmetic and copies ran while one was open for 35% of the time, Pallas kernels for 0%

commit v1 on v0

v1 whole, which is shorter than its diff:
```python
import jax
import jax.numpy as jnp
from jax import lax
from jax.experimental import pallas as pl
from jax.experimental.pallas import tpu as pltpu
from jax.sharding import PartitionSpec as P

ITERS = 2
LANE = 128
HALF = 64
TAPS = 31
RADIUS = 15
RANK = 3
ROWS = 16
VIEWS = 8
TAP_LANE = 8
ROW_MARK = 1024
Q_FIRST, Q_LAST = 41, 214
STEPS = (1, -1, 2, -2, 3, -3, 0, 0)
OWN = 6
F32 = jnp.float32
BF16 = jnp.bfloat16
VMEM_LIMIT = 48 * 1024 * 1024


def lanes_of(shape):
    return lax.broadcasted_iota(jnp.int32, shape, len(shape) - 1)


def rows_of(shape):
    return lax.broadcasted_iota(jnp.int32, shape, len(shape) - 2)


def pick_lane(values, lane):
    index = jnp.full(values.shape, lane, jnp.int32)
    return jnp.take_along_axis(values, index, axis=1, mode="promise_in_bounds")


def look_up(values, index):
    return jnp.take_along_axis(values, index, axis=1, mode="promise_in_bounds")


def halves(values):
    high = values.astype(BF16)
    low = (values - high.astype(F32)).astype(BF16)
    return high, low


def dot(left, right):
    return jnp.dot(left, right, preferred_element_type=F32)


def dot_turned(left, right):
    return lax.dot_general(left, right, (((1,), (1,)), ((), ())), preferred_element_type=F32)


def windows_of(strips):
    count = len(strips)
    turned = [pltpu.roll(strip, HALF, 1) for strip in strips]
    lower = lanes_of(strips[0].shape) < HALF
    zero = jnp.zeros_like(strips[0])
    tiles = []
    for place in range(count + 1):
        left = turned[place - 1] if place > 0 else zero
        right = turned[place] if place < count else zero
        tiles.append(jnp.where(lower, left, right))
    return tiles


def pack_measured_kernel(
    measured, dst_row, back_shift, tile_index, psf_z, psf_y, psf_x, psf_mix, out, table
):
    rows = 2 * ROWS
    table[...] = jnp.zeros_like(table)
    dst = dst_row[...].astype(F32) + ROW_MARK
    back = back_shift[...].astype(F32)
    tiles = tile_index[...].astype(F32)
    for plane in range(2):
        first = plane * ROWS
        table[0:1, first : first + ROWS] = dst
        table[1:2, first : first + ROWS] = back
        for part in range(2):
            start = first + part * 8
            table[2:3, start : start + 8] = jnp.broadcast_to(tiles[:, part : part + 1], (1, 8))
    upright = jnp.transpose(table[...])[:rows]
    table[...] = jnp.zeros_like(table)
    for place, psf in enumerate((psf_z, psf_y, psf_x)):
        values = psf[0]
        normal = values / jnp.sum(values, axis=1, keepdims=True)
        table[place * RANK : (place + 1) * RANK, TAP_LANE : TAP_LANE + TAPS] = normal
    mix = psf_mix[...]
    table[9:10, TAP_LANE : TAP_LANE + RANK] = mix / jnp.sum(mix, axis=1, keepdims=True)
    lane = lanes_of((rows, LANE))
    stash = jnp.where(lane < TAP_LANE, upright, table[:rows, :])
    values = measured[0].reshape(rows, measured.shape[3])
    strips = [values[:, place * LANE : (place + 1) * LANE] for place in range(VIEWS)]
    tiles = windows_of(strips)
    for place in range(VIEWS):
        out[place, :, :LANE] = jnp.where(lane < Q_FIRST, stash, tiles[place])
        out[place, :, LANE:] = tiles[place + 1]


def pack_measured(measured, dst_row, back_shift, tile_index, psf_z, psf_y, psf_x, psf_mix):
    return pl.pallas_call(
        pack_measured_kernel,
        out_shape=jax.ShapeDtypeStruct((VIEWS, 2 * ROWS, 2 * LANE), F32),
        scratch_shapes=[pltpu.VMEM((LANE, LANE), F32)],
        name="pack_measured",
    )(measured, dst_row, back_shift, tile_index, psf_z, psf_y, psf_x, psf_mix)


def registration_kernel(stash, out):
    lane = lanes_of((2 * ROWS, LANE))
    result = jnp.zeros((2 * ROWS, LANE), F32)
    for view in range(VIEWS):
        values = stash[view]
        result = jnp.where(lane == view, pick_lane(values, 0), result)
        result = jnp.where(lane == VIEWS + view, pick_lane(values, 1), result)
    out[...] = result


def registration(received):
    return pl.pallas_call(
        registration_kernel,
        out_shape=jax.ShapeDtypeStruct((2 * ROWS, LANE), F32),
        grid=(1,),
        in_specs=[pl.BlockSpec((VIEWS, 2 * ROWS, LANE), lambda i: (0, 0, 0))],
        out_specs=pl.BlockSpec((2 * ROWS, LANE), lambda i: (0, 0)),
        name="registration",
    )(received)


def pack_estimate_kernel(field, stash, out):
    rows = 2 * ROWS
    values = field[...].reshape(rows, field.shape[2])
    strips = [values[:, place * LANE : (place + 1) * LANE] for place in range(VIEWS)]
    tiles = windows_of(strips)
    lane = lanes_of((rows, LANE))
    for place in range(VIEWS):
        out[place, :, :LANE] = jnp.where(lane < 2 * VIEWS, stash[...], tiles[place])
        out[place, :, LANE:] = tiles[place + 1]


def pack_estimate(field, stash):
    return pl.pallas_call(
        pack_estimate_kernel,
        out_shape=jax.ShapeDtypeStruct((VIEWS, 2 * ROWS, 2 * LANE), F32),
        name="pack_estimate",
    )(field, stash)


def pack_field_kernel(field, out):
    tiles = windows_of([field[place] for place in range(VIEWS)])
    for place in range(VIEWS):
        out[place, :, :LANE] = tiles[place]
        out[place, :, LANE:] = tiles[place + 1]


def pack_field(field):
    return pl.pallas_call(
        pack_field_kernel,
        out_shape=jax.ShapeDtypeStruct((VIEWS, 2 * ROWS, 2 * LANE), F32),
        name="pack_field",
    )(field)


def column_bands_kernel(stash, high, low):
    shape = (2 * LANE, LANE)
    row = rows_of(shape)
    lane = lanes_of(shape)
    for term in range(RANK):
        taps = jnp.broadcast_to(stash[0, 6 + term : 7 + term, :], shape)
        for part in range(2):
            spread = row - (lane + part * LANE) + RADIUS
            inside = (spread >= 0) & (spread < TAPS)
            index = jnp.where(inside, spread + TAP_LANE, 0)
            band = jnp.where(inside, look_up(taps, index), 0.0)
            band_high, band_low = halves(band)
            high[0, term, :, part * LANE : (part + 1) * LANE] = band_high
            low[0, term, :, part * LANE : (part + 1) * LANE] = band_low


def column_bands(received):
    shape = jax.ShapeDtypeStruct((VIEWS, RANK, 2 * LANE, 2 * LANE), BF16)
    spec = pl.BlockSpec((1, RANK, 2 * LANE, 2 * LANE), lambda v: (v, 0, 0, 0))
    return pl.pallas_call(
        column_bands_kernel,
        out_shape=(shape, shape),
        grid=(VIEWS,),
        in_specs=[pl.BlockSpec((1, 2 * ROWS, LANE), lambda v: (v, 0, 0))],
        out_specs=(spec, spec),
        name="column_bands",
    )(received)


def build_row_bands(view, first_row, stash, rows_lane, own_dst, high, low, turned_high, turned_low):
    taps_rows = [stash[0, 3 + term : 4 + term, :] for term in range(RANK)]
    depth_rows = [stash[0, term : term + 1, :] for term in range(RANK)]
    mix_row = stash[0, 9:10, :]
    centre = TAP_LANE + RADIUS
    dst_lane = rows_lane[pl.ds(view, 1), :]
    shape = (4 * ROWS, LANE)
    row = rows_of(shape)
    lane = lanes_of(shape)
    for part in range(2):
        dst = jnp.broadcast_to(dst_lane[:, part * LANE : (part + 1) * LANE], shape)
        spread = dst.astype(jnp.int32) - ROW_MARK - first_row - row + RADIUS
        inside = (spread >= 0) & (spread < TAPS)
        if part == 1:
            inside = inside & (lane < 3 * 2 * ROWS)
        index = jnp.where(inside, spread + TAP_LANE, 0)
        upper = (lane // ROWS) % 2 == 0
        for term in range(RANK):
            taps = jnp.broadcast_to(taps_rows[term], shape)
            band = jnp.where(inside, look_up(taps, index), 0.0)
            mix = mix_row[:, TAP_LANE + term : TAP_LANE + term + 1]
            depth = depth_rows[term] * mix
            for plane in range(2):
                from_first = depth[:, centre - plane : centre - plane + 1]
                from_second = depth[:, centre + 1 - plane : centre + 2 - plane]
                scaled = band * jnp.where(upper, from_first, from_second)
                band_high, band_low = halves(scaled)
                start = (term * 2 + plane) * 4 * ROWS
                columns = slice(part * LANE, (part + 1) * LANE)
                high[0, start : start + 4 * ROWS, columns] = band_high
                low[0, start : start + 4 * ROWS, columns] = band_low
    shape = (ROWS, LANE)
    lane = lanes_of(shape)
    spread = own_dst.astype(jnp.int32) - ROW_MARK - first_row - lane % (4 * ROWS) + RADIUS
    inside = (spread >= 0) & (spread < TAPS)
    index = jnp.where(inside, spread + TAP_LANE, 0)
    upper = lane < 4 * ROWS
    for term in range(RANK):
        taps = jnp.broadcast_to(taps_rows[term], shape)
        band = jnp.where(inside, look_up(taps, index), 0.0)
        mix = mix_row[:, TAP_LANE + term : TAP_LANE + term + 1]
        depth = depth_rows[term] * mix
        for plane in range(2):
            from_first = depth[:, centre + plane : centre + plane + 1]
            from_second = depth[:, centre + plane - 1 : centre + plane]
            scaled = band * jnp.where(upper, from_first, from_second)
            band_high, band_low = halves(scaled)
            start = (term * 2 + plane) * ROWS
            turned_high[0, start : start + ROWS, :] = band_high
            turned_low[0, start : start + ROWS, :] = band_low


def iteration_kernel(building, *refs):
    refs = list(refs)
    field = refs.pop(0)
    moves = refs.pop(0)
    stash = refs.pop(0)
    measured = [refs.pop(0) for _ in range(5)]
    col_high, col_low = refs.pop(0), refs.pop(0)
    tiles = refs.pop(0)
    if building:
        out = refs.pop(0)
        row_high, row_low, turned_high, turned_low = [refs.pop(0) for _ in range(4)]
        rows_lane = refs.pop(0)
    else:
        row_high, row_low, turned_high, turned_low = [refs.pop(0) for _ in range(4)]
        out = refs.pop(0)
    x_high, x_low, total, weight_total = refs

    view = pl.program_id(0)
    strip = lax.axis_index("view")
    block = lax.axis_index("blk")

    @pl.when(view == 0)
    def _():
        total[...] = jnp.zeros_like(total)
        weight_total[...] = jnp.zeros_like(weight_total)
        x_high[...] = jnp.zeros_like(x_high)
        x_low[...] = jnp.zeros_like(x_low)
        if building:
            rows_lane[...] = jnp.transpose(moves[...].reshape(VIEWS * 2 * ROWS, LANE))

    own_dst = pick_lane(moves[OWN], view)
    last = jnp.max(own_dst) - ROW_MARK
    phase = (last >= ((block + 1) * ROWS).astype(F32)).astype(jnp.int32)
    first_row = (block - 2 + phase) * ROWS
    if building:
        build_row_bands(
            view, first_row, stash, rows_lane, own_dst[:ROWS],
            row_high, row_low, turned_high, turned_low,
        )

    lane = lanes_of((2 * ROWS, LANE))
    column = lane + strip * LANE - HALF
    columns = column.shape[1] * VIEWS
    inside = [
        (column >= 0) & (column < columns),
        (column + LANE >= 0) & (column + LANE < columns),
    ]
    for slot in range(OWN + 1):
        where = lane + pick_lane(moves[slot], VIEWS + view).astype(jnp.int32)
        index = where & (LANE - 1)
        left = look_up(field[slot, :, :LANE], index)
        right = look_up(field[slot, :, LANE:], index)
        moved = (jnp.where(where < LANE, left, right), jnp.where(where < 0, left, right))
        for part in range(2):
            high, low = halves(jnp.where(inside[part], moved[part], 0.0))
            rows = slice(slot * 2 * ROWS, (slot + 1) * 2 * ROWS)
            x_high[rows, part * LANE : (part + 1) * LANE] = high
            x_low[rows, part * LANE : (part + 1) * LANE] = low

    layers = (
        dot(row_high[0], x_high[...]) + dot(row_low[0], x_high[...]) + dot(row_high[0], x_low[...])
    )
    blurred = None
    height = 8 * ROWS
    for term in range(RANK):
        high, low = halves(layers[term * height : (term + 1) * height])
        part = dot(high, col_high[0, term]) + dot(low, col_high[0, term])
        part = part + dot(high, col_low[0, term])
        blurred = part if blurred is None else blurred + part

    shape = (ROWS, 2 * LANE)
    wide = lanes_of(shape)
    wide_column = wide + strip * LANE - HALF
    kept = (wide >= Q_FIRST) & (wide <= Q_LAST) & (wide_column >= 0) & (wide_column < columns)
    quotients = []
    for plane in range(2):
        for place in range(4):
            rows = slice(plane * ROWS, (plane + 1) * ROWS)
            seen = jnp.where(phase == 1, measured[place + 1][0, rows], measured[place][0, rows])
            start = (plane * 4 + place) * ROWS
            row_block = block - 2 + phase + place
            fine = kept & (row_block >= 0) & (row_block < VIEWS * 8)
            quotients.append(jnp.where(fine, seen / blurred[start : start + ROWS], 0.0))
    quotient = jnp.concatenate(quotients, axis=0)
    high, low = halves(quotient)
    layers = dot(turned_high[0], high) + dot(turned_low[0], high) + dot(turned_high[0], low)
    adjoint = None
    height = 2 * ROWS
    for term in range(RANK):
        high, low = halves(layers[term * height : (term + 1) * height])
        part = dot_turned(high, col_high[0, term]) + dot_turned(low, col_high[0, term])
        part = part + dot_turned(high, col_low[0, term])
        adjoint = part if adjoint is None else adjoint + part

    left = jnp.where(inside[0], adjoint[:, :LANE], 0.0)
    right = jnp.where(inside[1], adjoint[:, LANE:], 0.0)
    where = lane + HALF + pick_lane(moves[OWN], VIEWS + view).astype(jnp.int32)
    index = where & (LANE - 1)
    returned = jnp.where(where < LANE, look_up(left, index), look_up(right, index))
    chosen = pick_lane(stash[0], 2)
    weight = jnp.zeros((2 * ROWS, LANE), F32)
    first_column = pl.multiple_of(strip * LANE, LANE)
    for number in range(tiles.shape[0]):
        tile = tiles[number, :, pl.ds(first_column, LANE)]
        tall = jnp.concatenate([tile] * 4, axis=0)
        weight = jnp.where(chosen == number, tall, weight)
    total[...] += weight * returned
    weight_total[...] += weight

    @pl.when(view == VIEWS - 1)
    def _():
        lower = pltpu.roll(field[OWN, :, :LANE], HALF, 1)
        upper = pltpu.roll(field[OWN, :, LANE:], HALF, 1)
        own = jnp.where(lane < HALF, lower, upper)
        result = own * total[...] / weight_total[...]
        for place in range(VIEWS):
            out[place] = result


def iteration(field, moves, received, neighbours, col_bands, weight_tiles, row_bands=None):
    building = row_bands is None
    rows = 2 * ROWS
    whole = pl.BlockSpec((VIEWS, rows, 2 * LANE), lambda v: (0, 0, 0))
    moves_spec = pl.BlockSpec((VIEWS, rows, LANE), lambda v: (0, 0, 0))
    stash_spec = pl.BlockSpec((1, rows, LANE), lambda v: (v, 0, 0))
    measured_spec = pl.BlockSpec((1, rows, 2 * LANE), lambda v: (v, 0, 0))
    col_spec = pl.BlockSpec((1, RANK, 2 * LANE, 2 * LANE), lambda v: (v, 0, 0, 0))
    tiles_spec = pl.BlockSpec(weight_tiles.shape, lambda v: (0, 0, 0))
    row_shape = (VIEWS, RANK * 8 * ROWS, 2 * LANE)
    turned_shape = (VIEWS, RANK * 2 * ROWS, LANE)
    row_spec = pl.BlockSpec((1,) + row_shape[1:], lambda v: (v, 0, 0))
    turned_spec = pl.BlockSpec((1,) + turned_shape[1:], lambda v: (v, 0, 0))
    band_specs = [row_spec, row_spec, turned_spec, turned_spec]
    out_shape = jax.ShapeDtypeStruct((VIEWS, rows, LANE), F32)
    out_spec = pl.BlockSpec((VIEWS, rows, LANE), lambda v: (0, 0, 0))
    in_specs = [whole, moves_spec, stash_spec] + [measured_spec] * 5 + [col_spec] * 2 + [tiles_spec]
    operands = [field, moves, received, *neighbours, *col_bands, weight_tiles]
    scratch = [
        pltpu.VMEM((2 * LANE, 2 * LANE), BF16),
        pltpu.VMEM((2 * LANE, 2 * LANE), BF16),
        pltpu.VMEM((rows, LANE), F32),
        pltpu.VMEM((rows, LANE), F32),
    ]
    if building:
        bands = [
            jax.ShapeDtypeStruct(row_shape, BF16),
            jax.ShapeDtypeStruct(row_shape, BF16),
            jax.ShapeDtypeStruct(turned_shape, BF16),
            jax.ShapeDtypeStruct(turned_shape, BF16),
        ]
        out_shapes = [out_shape] + bands
        out_specs = [out_spec] + band_specs
        scratch = [pltpu.VMEM((LANE, 2 * LANE), F32)] + scratch
    else:
        in_specs += band_specs
        operands += row_bands
        out_shapes = out_shape
        out_specs = out_spec
    result = pl.pallas_call(
        lambda *refs: iteration_kernel(building, *refs),
        out_shape=out_shapes,
        grid=(VIEWS,),
        in_specs=in_specs,
        out_specs=out_specs,
        scratch_shapes=scratch,
        compiler_params=pltpu.CompilerParams(vmem_limit_bytes=VMEM_LIMIT),
        name="iteration_first" if building else "iteration_next",
    )(*operands)
    if building:
        return result[0], list(result[1:])
    return result


def step_by_view(values):
    blocks = lax.axis_size("blk")
    route = []
    for view, step in enumerate(STEPS):
        for block in range(blocks):
            if 0 <= block + step < blocks:
                route.append((view * blocks + block, view * blocks + block + step))
    return lax.ppermute(values, ("view", "blk"), route)


def from_block(values, offset):
    blocks = lax.axis_size("blk")
    route = [(b + offset, b) for b in range(blocks) if 0 <= b + offset < blocks]
    return lax.ppermute(values, "blk", route)


def over_views(values):
    return lax.all_to_all(values, "view", 0, 0)


def body(
    estimate,
    measured,
    psf_z,
    psf_y,
    psf_x,
    psf_mix,
    weight_tiles,
    tile_index,
    src_row,
    dst_row,
    col_shift,
    back_shift,
):
    planes, row_count, col_count = estimate.shape
    stepped = step_by_view(estimate)
    received = over_views(
        pack_measured(measured, dst_row, back_shift, tile_index, psf_z, psf_y, psf_x, psf_mix)
    )
    moves = step_by_view(registration(received))
    neighbours = [
        received if offset == 0 else from_block(received, offset) for offset in (-2, -1, 0, 1, 2)
    ]
    col_bands = column_bands(received)
    field = over_views(pack_estimate(stepped, moves))
    moves = field
    strips, row_bands = iteration(field, moves, received, neighbours, col_bands, weight_tiles)
    for _ in range(ITERS - 1):
        field = over_views(pack_field(step_by_view(over_views(strips))))
        strips = iteration(
            field, moves, received, neighbours, col_bands, weight_tiles, row_bands
        )
    strips = over_views(strips).reshape(VIEWS, planes, row_count, LANE)
    return jnp.transpose(strips, (1, 2, 0, 3)).reshape(planes, row_count, col_count)


def solution(mesh):
    in_specs = (
        P(None, "blk", None),
        P("view", None, "blk", None),
        P("view", None, None),
        P("view", None, None),
        P("view", None, None),
        P("view", None),
        P(),
        P("view", "blk"),
        P("view", "blk"),
        P("view", "blk"),
        P("view", "blk"),
        P("view", "blk"),
    )
    out_specs = P(None, "blk", None)
    return jax.shard_map(body, mesh=mesh, in_specs=in_specs, out_specs=out_specs, check_vma=False)
```

time: 449 us -> 148 us (0.33)
  the two profiles are of different devices: /device:TPU:8 before, /device:TPU:272 now
where the time goes in v1:
time: 148 us; the launch traced here: 147 us
  Pallas kernels  45.4 us (31%)
  blocking collectives  35.5 us (24%)
  starting transfers between devices  34.3 us (23%)
  waiting for transfers between devices  18.1 us (12%)
  local copies, waits for them, and re-layouts  13.4 us (9%)
    all_to_all x3, blocking collectives, over_views(): return lax.all_to_all(values, 'view', 0, 0)  35.5 us
    pallas_call x2, Pallas kernels, iteration(): pl.pallas_call(lambda *refs: iteration_kernel(building, *refs), out_shape...  31.8 us
    ppermute x4, starting transfers between devices, from_block(): return lax.ppermute(values, 'blk', route)  13.8 us
    ppermute x3, waiting for transfers between devices, step_by_view(): return lax.ppermute(values, ('view', 'blk'), route)  13.1 us
    unnamed x31, local copies, waits for them, and re-layouts  12.7 us
    all_to_all x2, starting transfers between devices, over_views(): return lax.all_to_all(values, 'view', 0, 0)  11.6 us
    ppermute x3, starting transfers between devices, step_by_view(): return lax.ppermute(values, ('view', 'blk'), route)  8.86 us
    pallas_call x1, Pallas kernels, column_bands(): pl.pallas_call(column_bands_kernel, out_shape=(shape, shape), grid=(VIEWS...  6.61 us
  transfers between devices with their start and end apart: 9, of which 4 were waited for; matrix products, arithmetic and copies ran while one was open for 0% of the time, Pallas kernels for 7%

profile of v1, /device:TPU:272, one launch (start us, length us, event | category | flops | bytes accessed | tf_op | source)
XLA Modules:
  0.0 146.7 jit_solution(2478344458268289691)
XLA Ops:
  0.0 1.3 copy.11.psf_z
  1.3 1.3 copy.12.psf_y
  2.5 1.3 copy.13.psf_x
  3.8 1.8 %pack_measured.1 = f32[8,32,256]{2,1,0:T(8,128)} custom-call(f32[1,2,16,1024]{3,2,1,0:T(8,128)} %measured.1, s32[1,16]{1,0:T(1,128)} %dst_row.1, s32[1,16]{1,0:T(1,128)} %back_shift.1, s32[1,2]{1,0:T(1,128)} %tile_index.1, f32[1,3,31]{2,1,0:T(4,128)} %copy.11.psf_z, f32[1,3,31]{2,1,0:T(4,128)} %copy.12.psf_y, f32[1,3,31]{2,1,0:T(4,128)} %copy.13.psf_x, ...), custom_call_target="tpu_custom_call" | custom-call | tf_op jit(solution)/shard_map/pack_measured/pallas_call | solution.py:104
  5.6 4.3 %all-to-all-start = ((f32[8,32,256]{2,1,0:T(8,128)}), f32[8,32,256]{2,1,0:T(8,128)S(1)}, u32[]{:S(2)}, u32[]{:S(2)}) async-start(f32[8,32,256]{2,1,0:T(8,128)} %pack_measured.1), calls=%async_computation | async-start | bytes 524288 | tf_op jit(solution)/shard_map/all_to_all | solution.py:438
  9.9 3.5 %collective-permute-start = (f32[2,16,1024]{2,1,0:T(8,128)}, f32[2,16,1024]{2,1,0:T(8,128)S(1)}, u32[]{:S(2)}, u32[]{:S(2)}) collective-permute-start(f32[2,16,1024]{2,1,0:T(8,128)} %param.12), channel_id=1, source_target_pairs={{0,1},{1,2},{2,3},{3,4},{4,5},{5,6},{6,7},{7,8},{8,9},{9,10},{10,1... | collective-permute-start | bytes 393224 | tf_op jit(solution)/shard_map/ppermute | solution.py:428
  13.4 4.1 %all-to-all-done.stash.refs_2_.refs_5_ = f32[8,32,256]{2,1,0:T(8,128)S(1)} async-done(((f32[8,32,256]{2,1,0:T(8,128)}), f32[8,32,256]{2,1,0:T(8,128)S(1)}, u32[]{:S(2)}, u32[]{:S(2)}) %all-to-all-start) | async-done | bytes 262176 | tf_op jit(solution)/shard_map/all_to_all | solution.py:438
  17.5 2.2 %collective-permute-start.5 = (f32[8,32,256]{2,1,0:T(8,128)S(1)}, f32[8,32,256]{2,1,0:T(8,128)S(1)}, u32[]{:S(2)}, u32[]{:S(2)}) collective-permute-start(f32[8,32,256]{2,1,0:T(8,128)S(1)} %all-to-all-done.stash.refs_2_.refs_5_), channel_id=1, source_target_pairs={{2,0},{3,1},{4,2},{5,3},{6,4},{7,5},{8,6},{9,7},{10,8},{11,9},{12,... | collective-permute-start | bytes 786440 | tf_op jit(solution)/shard_map/ppermute | solution.py:434
  19.7 4.5 %collective-permute-start.4 = (f32[8,32,256]{2,1,0:T(8,128)S(1)}, f32[8,32,256]{2,1,0:T(8,128)S(1)}, u32[]{:S(2)}, u32[]{:S(2)}) collective-permute-start(f32[8,32,256]{2,1,0:T(8,128)S(1)} %all-to-all-done.stash.refs_2_.refs_5_), channel_id=1, source_target_pairs={{1,0},{2,1},{3,2},{4,3},{5,4},{6,5},{7,6},{8,7},{9,8},{10,9},{11,1... | collective-permute-start | bytes 786440 | tf_op jit(solution)/shard_map/ppermute | solution.py:434
  24.2 1.9 %collective-permute-start.3 = (f32[8,32,256]{2,1,0:T(8,128)S(1)}, f32[8,32,256]{2,1,0:T(8,128)S(1)}, u32[]{:S(2)}, u32[]{:S(2)}) collective-permute-start(f32[8,32,256]{2,1,0:T(8,128)S(1)} %all-to-all-done.stash.refs_2_.refs_5_), channel_id=1, source_target_pairs={{0,1},{1,2},{2,3},{3,4},{4,5},{5,6},{6,7},{7,8},{8,9},{9,10},{10,1... | collective-permute-start | bytes 786440 | tf_op jit(solution)/shard_map/ppermute | solution.py:434
  26.1 5.2 %collective-permute-start.2 = (f32[8,32,256]{2,1,0:T(8,128)S(1)}, f32[8,32,256]{2,1,0:T(8,128)S(1)}, u32[]{:S(2)}, u32[]{:S(2)}) collective-permute-start(f32[8,32,256]{2,1,0:T(8,128)S(1)} %all-to-all-done.stash.refs_2_.refs_5_), channel_id=1, source_target_pairs={{0,2},{1,3},{2,4},{3,5},{4,6},{5,7},{6,8},{7,9},{8,10},{9,11},{10,... | collective-permute-start | bytes 786440 | tf_op jit(solution)/shard_map/ppermute | solution.py:434
  31.3 1.7 %registration.1 = f32[32,128]{1,0:T(8,128)} custom-call(f32[8,32,256]{2,1,0:T(8,128)} %copy-done), custom_call_target="tpu_custom_call" | custom-call | tf_op jit(solution)/shard_map/registration/pallas_call | solution.py:123
  32.9 3.5 %collective-permute-start.1 = (f32[32,128]{1,0:T(8,128)}, f32[32,128]{1,0:T(8,128)S(1)}, u32[]{:S(2)}, u32[]{:S(2)}) collective-permute-start(f32[32,128]{1,0:T(8,128)} %registration.1), channel_id=1, source_target_pairs={{0,1},{1,2},{2,3},{3,4},{4,5},{5,6},{6,7},{7,8},{8,9},{9,10},{10,1... | collective-permute-start | bytes 49160 | tf_op jit(solution)/shard_map/ppermute | solution.py:428
  36.4 8.2 %collective-permute-done.1.stash = f32[32,128]{1,0:T(8,128)S(1)} collective-permute-done((f32[32,128]{1,0:T(8,128)}, f32[32,128]{1,0:T(8,128)S(1)}, u32[]{:S(2)}, u32[]{:S(2)}) %collective-permute-start.1) | collective-permute-done | bytes 16416 | tf_op jit(solution)/shard_map/ppermute | solution.py:428
  45.2 1.7 %pack_estimate.1 = f32[8,32,256]{2,1,0:T(8,128)} custom-call(f32[2,16,1024]{2,1,0:T(8,128)} %copy-done.11, f32[32,128]{1,0:T(8,128)} %copy-done.13), custom_call_target="tpu_custom_call" | custom-call | tf_op jit(solution)/shard_map/pack_estimate/pallas_call | solution.py:145
  46.9 7.3 %all-to-all-start.1 = ((f32[8,32,256]{2,1,0:T(8,128)}), f32[8,32,256]{2,1,0:T(8,128)S(1)}, u32[]{:S(2)}, u32[]{:S(2)}) async-start(f32[8,32,256]{2,1,0:T(8,128)} %pack_estimate.1), calls=%async_computation.1 | async-start | bytes 524288 | tf_op jit(solution)/shard_map/all_to_all | solution.py:438
  54.3 6.6 %column_bands.1 = (bf16[8,3,256,256]{3,2,1,0:T(8,128)(2,1)}, bf16[8,3,256,256]{3,2,1,0:T(8,128)(2,1)}) custom-call(f32[8,32,256]{2,1,0:T(8,128)} %copy-done), custom_call_target="tpu_custom_call" | custom-call | tf_op jit(solution)/shard_map/column_bands/pallas_call | solution.py:186
  60.9 0.9 all-to-all-done.1.refs_0_.refs_1_
  61.8 0.9 copy-done.1
  62.8 0.9 copy-done.5
  63.7 16.4 %iteration_first.1 = (f32[8,32,128]{2,1,0:T(8,128)S(1)}, bf16[8,384,256]{2,1,0:T(8,128)(2,1)S(1)}, bf16[8,384,256]{2,1,0:T(8,128)(2,1)S(1)}, bf16[8,96,128]{2,1,0:T(8,128)(2,1)S(1)}, bf16[8,96,128]{2,1,0:T(8,128)(2,1)S(1)}) custom-call(f32[8,32,256]{2,1,0:T(8,128)S(1)} %all-to-all-done.1.refs_0_.refs_1_, f32[8,32,256]{2,1,0:T(8,128)S(1)} %all-to-all-done.1.refs_0_.refs_1_, ...), custom_call_target="tpu_custom_call" | custom-call | tf_op jit(solution)/shard_map/iteration_first/pallas_call | solution.py:406
  80.1 1.1 copy-done.3
  82.6 9.8 %all_to_all.25 = f32[8,32,128]{2,1,0:T(8,128)S(1)} all-to-all(f32[8,32,128]{2,1,0:T(8,128)S(1)} %get-tuple-element.14), channel_id=1, replica_groups=mesh['view'=8,'blk'=64] {'view'}, dimensions={0} | all-to-all | bytes 262144 | tf_op jit(solution)/shard_map/all_to_all | solution.py:438
  92.5 1.9 %collective-permute-start.6 = (f32[8,32,128]{2,1,0:T(8,128)S(1)}, f32[8,32,128]{2,1,0:T(8,128)S(1)}, u32[]{:S(2)}, u32[]{:S(2)}) collective-permute-start(f32[8,32,128]{2,1,0:T(8,128)S(1)} %all_to_all.25), channel_id=1, source_target_pairs={{0,1},{1,2},{2,3},{3,4},{4,5},{5,6},{6,7},{7,8},{8,9},{9,10},{10,1... | collective-permute-start | bytes 393224 | tf_op jit(solution)/shard_map/ppermute | solution.py:428
  94.4 4.9 %collective-permute-done.6.field = f32[8,32,128]{2,1,0:T(8,128)S(1)} collective-permute-done((f32[8,32,128]{2,1,0:T(8,128)S(1)}, f32[8,32,128]{2,1,0:T(8,128)S(1)}, u32[]{:S(2)}, u32[]{:S(2)}) %collective-permute-start.6) | collective-permute-done | bytes 131104 | tf_op jit(solution)/shard_map/ppermute | solution.py:428
  100.0 1.8 %pack_field.1 = f32[8,32,256]{2,1,0:T(8,128)} custom-call(f32[8,32,128]{2,1,0:T(8,128)} %copy-done.12), custom_call_target="tpu_custom_call" | custom-call | tf_op jit(solution)/shard_map/pack_field/pallas_call | solution.py:160
  101.7 17.1 %all_to_all.26.refs_0_ = f32[8,32,256]{2,1,0:T(8,128)S(1)} all-to-all(f32[8,32,256]{2,1,0:T(8,128)} %pack_field.1), channel_id=1, replica_groups=mesh['view'=8,'blk'=64] {'view'}, dimensions={0} | all-to-all | bytes 524288 | tf_op jit(solution)/shard_map/all_to_all | solution.py:438
  118.8 1.4 copy-done.4
  120.3 0.9 copy-done.8
  121.2 0.9 copy-done.10
  122.1 15.4 %iteration_next.1 = f32[8,32,128]{2,1,0:T(8,128)S(1)} custom-call(f32[8,32,256]{2,1,0:T(8,128)S(1)} %all_to_all.26.refs_0_, f32[8,32,256]{2,1,0:T(8,128)S(1)} %all-to-all-done.1.refs_0_.refs_1_, f32[8,32,256]{2,1,0:T(8,128)S(1)} %copy-done.2, f32[8,32,256]{2,1,0:T(8,128)S(1)} %collective-permute-done.2.refs_3_, ...), custom_call_target="tpu_custom_call" | custom-call | tf_op jit(solution)/shard_map/iteration_next/pallas_call | solution.py:406
  137.5 8.5 %all_to_all.27 = f32[8,32,128]{2,1,0:T(8,128)S(1)} all-to-all(f32[8,32,128]{2,1,0:T(8,128)S(1)} %iteration_next.1), channel_id=1, replica_groups=mesh['view'=8,'blk'=64] {'view'}, dimensions={0} | all-to-all | bytes 262144 | tf_op jit(solution)/shard_map/all_to_all | solution.py:438
  (28 shorter events, 3.4 us)
Async XLA Ops:
  5.6 11.8 %all-to-all-start = ((f32[8,32,256]{2,1,0:T(8,128)}), f32[8,32,256]{2,1,0:T(8,128)S(1)}, u32[]{:S(2)}, u32[]{:S(2)}) async-start(f32[8,32,256]{2,1,0:T(8,128)} %pack_measured.1), calls=%async_computation | async-start | bytes 524288 | tf_op jit(solution)/shard_map/all_to_all | solution.py:438
  9.9 23.0 %collective-permute-start = (f32[2,16,1024]{2,1,0:T(8,128)}, f32[2,16,1024]{2,1,0:T(8,128)S(1)}, u32[]{:S(2)}, u32[]{:S(2)}) collective-permute-start(f32[2,16,1024]{2,1,0:T(8,128)} %param.12), channel_id=1, source_target_pairs={{0,1},{1,2},{2,3},{3,4},{4,5},{5,6},{6,7},{7,8},{8,9},{9,10},{10,1... | collective-permute-start | bytes 393224 | tf_op jit(solution)/shard_map/ppermute | solution.py:428
  17.5 13.8 %copy-start = (f32[8,32,256]{2,1,0:T(8,128)}, f32[8,32,256]{2,1,0:T(8,128)S(1)}, u32[]{:S(2)}) copy-start(f32[8,32,256]{2,1,0:T(8,128)S(1)} %all-to-all-done.stash.refs_2_.refs_5_) | copy-start | bytes 786436
  17.5 44.4 %collective-permute-start.5 = (f32[8,32,256]{2,1,0:T(8,128)S(1)}, f32[8,32,256]{2,1,0:T(8,128)S(1)}, u32[]{:S(2)}, u32[]{:S(2)}) collective-permute-start(f32[8,32,256]{2,1,0:T(8,128)S(1)} %all-to-all-done.stash.refs_2_.refs_5_), channel_id=1, source_target_pairs={{2,0},{3,1},{4,2},{5,3},{6,4},{7,5},{8,6},{9,7},{10,8},{11,9},{12,... | collective-permute-start | bytes 786440 | tf_op jit(solution)/shard_map/ppermute | solution.py:434
  19.7 42.1 %collective-permute-start.4 = (f32[8,32,256]{2,1,0:T(8,128)S(1)}, f32[8,32,256]{2,1,0:T(8,128)S(1)}, u32[]{:S(2)}, u32[]{:S(2)}) collective-permute-start(f32[8,32,256]{2,1,0:T(8,128)S(1)} %all-to-all-done.stash.refs_2_.refs_5_), channel_id=1, source_target_pairs={{1,0},{2,1},{3,2},{4,3},{5,4},{6,5},{7,6},{8,7},{9,8},{10,9},{11,1... | collective-permute-start | bytes 786440 | tf_op jit(solution)/shard_map/ppermute | solution.py:434
  24.2 37.6 %collective-permute-start.3 = (f32[8,32,256]{2,1,0:T(8,128)S(1)}, f32[8,32,256]{2,1,0:T(8,128)S(1)}, u32[]{:S(2)}, u32[]{:S(2)}) collective-permute-start(f32[8,32,256]{2,1,0:T(8,128)S(1)} %all-to-all-done.stash.refs_2_.refs_5_), channel_id=1, source_target_pairs={{0,1},{1,2},{2,3},{3,4},{4,5},{5,6},{6,7},{7,8},{8,9},{9,10},{10,1... | collective-permute-start | bytes 786440 | tf_op jit(solution)/shard_map/ppermute | solution.py:434
  26.1 35.7 %collective-permute-start.2 = (f32[8,32,256]{2,1,0:T(8,128)S(1)}, f32[8,32,256]{2,1,0:T(8,128)S(1)}, u32[]{:S(2)}, u32[]{:S(2)}) collective-permute-start(f32[8,32,256]{2,1,0:T(8,128)S(1)} %all-to-all-done.stash.refs_2_.refs_5_), channel_id=1, source_target_pairs={{0,2},{1,3},{2,4},{3,5},{4,6},{5,7},{6,8},{7,9},{8,10},{9,11},{10,... | collective-permute-start | bytes 786440 | tf_op jit(solution)/shard_map/ppermute | solution.py:434
  32.9 11.7 %copy-start.11 = (f32[2,16,1024]{2,1,0:T(8,128)}, f32[2,16,1024]{2,1,0:T(8,128)S(1)}, u32[]{:S(2)}) copy-start(f32[2,16,1024]{2,1,0:T(8,128)S(1)} %collective-permute-done.field) | copy-start | bytes 393220
  32.9 11.7 %collective-permute-start.1 = (f32[32,128]{1,0:T(8,128)}, f32[32,128]{1,0:T(8,128)S(1)}, u32[]{:S(2)}, u32[]{:S(2)}) collective-permute-start(f32[32,128]{1,0:T(8,128)} %registration.1), channel_id=1, source_target_pairs={{0,1},{1,2},{2,3},{3,4},{4,5},{5,6},{6,7},{7,8},{8,9},{9,10},{10,1... | collective-permute-start | bytes 49160 | tf_op jit(solution)/shard_map/ppermute | solution.py:428
  44.6 0.6 copy-start.13
  46.9 14.9 %all-to-all-start.1 = ((f32[8,32,256]{2,1,0:T(8,128)}), f32[8,32,256]{2,1,0:T(8,128)S(1)}, u32[]{:S(2)}, u32[]{:S(2)}) async-start(f32[8,32,256]{2,1,0:T(8,128)} %pack_estimate.1), calls=%async_computation.1 | async-start | bytes 524288 | tf_op jit(solution)/shard_map/all_to_all | solution.py:438
  61.8 1.0 copy-start.1
  62.8 0.9 copy-start.5
  63.7 55.1 %copy-start.2 = (f32[8,32,256]{2,1,0:T(8,128)S(1)}, f32[8,32,256]{2,1,0:T(8,128)}, u32[]{:S(2)}) copy-start(f32[8,32,256]{2,1,0:T(8,128)} %copy-done) | copy-start | bytes 786436
  63.7 55.1 %copy-start.6 = (f32[8,8,1024]{2,1,0:T(8,128)S(1)}, f32[8,8,1024]{2,1,0:T(8,128)}, u32[]{:S(2)}) copy-start(f32[8,8,1024]{2,1,0:T(8,128)} %refs_10_.3) | copy-start | bytes 786436
  80.1 1.2 copy-start.3
  81.2 0.7 copy-start.7
  81.9 0.7 copy-start.9
  92.5 6.8 %collective-permute-start.6 = (f32[8,32,128]{2,1,0:T(8,128)S(1)}, f32[8,32,128]{2,1,0:T(8,128)S(1)}, u32[]{:S(2)}, u32[]{:S(2)}) collective-permute-start(f32[8,32,128]{2,1,0:T(8,128)S(1)} %all_to_all.25), channel_id=1, source_target_pairs={{0,1},{1,2},{2,3},{3,4},{4,5},{5,6},{6,7},{7,8},{8,9},{9,10},{10,1... | collective-permute-start | bytes 393224 | tf_op jit(solution)/shard_map/ppermute | solution.py:428
  99.3 0.7 copy-start.12
  118.8 1.4 copy-start.4
  120.3 0.9 copy-start.8
  121.2 0.9 copy-start.10

commit v2 on v1

v2 whole, which is shorter than its diff:
```python
import jax
import jax.numpy as jnp
from jax import lax
from jax.experimental import pallas as pl
from jax.experimental.pallas import tpu as pltpu
from jax.sharding import PartitionSpec as P

ITERS = 2
LANE = 128
HALF = 64
TAPS = 31
RADIUS = 15
RANK = 3
ROWS = 16
VIEWS = 8
TAP_LANE = 96
TILE_LANE = 2 * 8
ROW_MARK = 1024
Q_FIRST, Q_LAST = 41, 214
STEPS = (1, -1, 2, -2, 3, -3, 0, 0)
OWN = 6
F32 = jnp.float32
BF16 = jnp.bfloat16
VMEM_LIMIT = 65_000_000


def whole(shape):
    return pl.BlockSpec(tuple(shape), lambda i: (0,) * len(shape))


def lanes_of(shape):
    return lax.broadcasted_iota(jnp.int32, shape, len(shape) - 1)


def rows_of(shape):
    return lax.broadcasted_iota(jnp.int32, shape, len(shape) - 2)


def pick_lane(values, lane):
    index = jnp.full(values.shape, lane, jnp.int32)
    return jnp.take_along_axis(values, index, axis=1, mode="promise_in_bounds")


def look_up(values, index):
    return jnp.take_along_axis(values, index, axis=1, mode="promise_in_bounds")


def halves(values):
    high = values.astype(BF16)
    low = (values - high.astype(F32)).astype(BF16)
    return high, low


def dot(left, right):
    return jnp.dot(left, right, preferred_element_type=F32)


def dot_turned(left, right):
    return lax.dot_general(left, right, (((1,), (1,)), ((), ())), preferred_element_type=F32)


def triple(high, low, right_high, right_low, multiply):
    both = multiply(jnp.concatenate([high, low], axis=0), right_high)
    height = high.shape[0]
    return both[:height] + both[height:] + multiply(high, right_low)


def windows_of(strips):
    count = len(strips)
    turned = [pltpu.roll(strip, HALF, 1) for strip in strips]
    lower = lanes_of(strips[0].shape) < HALF
    zero = jnp.zeros_like(strips[0])
    tiles = []
    for place in range(count + 1):
        left = turned[place - 1] if place > 0 else zero
        right = turned[place] if place < count else zero
        tiles.append(jnp.where(lower, left, right))
    return tiles


def pack_measured_kernel(
    measured, dst_row, back_shift, tile_index, psf_z, psf_y, psf_x, psf_mix, out, table
):
    rows = 2 * ROWS
    view = lax.axis_index("view")
    table[...] = jnp.zeros_like(table)
    dst = dst_row[...].astype(F32) + ROW_MARK
    back = back_shift[...].astype(F32)
    tiles = tile_index[...].astype(F32)
    for plane in range(2):
        first = plane * ROWS
        table[0:1, first : first + ROWS] = dst
        table[1:2, first : first + ROWS] = back
        for part in range(2):
            start = first + part * 8
            table[2:3, start : start + 8] = jnp.broadcast_to(tiles[:, part : part + 1], (1, 8))
    upright = jnp.transpose(table[...])[:rows]
    lane = lanes_of((rows, LANE))
    moves = jnp.where(lane == view, upright[:, 0:1], 0.0)
    moves = jnp.where(lane == VIEWS + view, upright[:, 1:2], moves)
    moves = jnp.where(lane == TILE_LANE, upright[:, 2:3], moves)
    table[...] = jnp.zeros_like(table)
    for place, psf in enumerate((psf_z, psf_y, psf_x)):
        for term in range(RANK):
            values = psf[term]
            normal = values / jnp.sum(values, axis=1, keepdims=True)
            row = place * RANK + term
            table[row : row + 1, TAP_LANE : TAP_LANE + TAPS] = normal
    mix = psf_mix[...]
    table[9:10, TAP_LANE : TAP_LANE + RANK] = mix / jnp.sum(mix, axis=1, keepdims=True)
    taps = table[:rows, :]
    values = measured[0].reshape(rows, measured.shape[3])
    strips = [values[:, place * LANE : (place + 1) * LANE] for place in range(VIEWS)]
    tiles = windows_of(strips)
    for place in range(VIEWS):
        out[place, :, :LANE] = jnp.where(lane < Q_FIRST, moves, tiles[place])
        out[place, :, LANE:] = jnp.where(lane < TAP_LANE, tiles[place + 1], taps)


def pack_measured(measured, dst_row, back_shift, tile_index, psf_z, psf_y, psf_x, psf_mix):
    turned = [jnp.transpose(psf, (1, 0, 2)) for psf in (psf_z, psf_y, psf_x)]
    operands = (measured, dst_row, back_shift, tile_index, *turned, psf_mix)
    return pl.pallas_call(
        pack_measured_kernel,
        out_shape=jax.ShapeDtypeStruct((VIEWS, 2 * ROWS, 2 * LANE), F32),
        grid=(1,),
        out_specs=whole((VIEWS, 2 * ROWS, 2 * LANE)),
        scratch_shapes=[pltpu.VMEM((LANE, LANE), F32)],
        in_specs=[whole(operand.shape) for operand in operands],
        compiler_params=pltpu.CompilerParams(vmem_limit_bytes=VMEM_LIMIT),
        name="pack_measured",
    )(*operands)


def registration(received):
    return jnp.sum(received[:, :, :LANE], axis=0)


def pack_estimate_kernel(field, stash, out):
    rows = 2 * ROWS
    values = field[...].reshape(rows, field.shape[2])
    strips = [values[:, place * LANE : (place + 1) * LANE] for place in range(VIEWS)]
    tiles = windows_of(strips)
    lane = lanes_of((rows, LANE))
    for place in range(VIEWS):
        out[place, :, :LANE] = jnp.where(lane < 2 * VIEWS, stash[...], tiles[place])
        out[place, :, LANE:] = tiles[place + 1]


def pack_estimate(field, stash):
    return pl.pallas_call(
        pack_estimate_kernel,
        out_shape=jax.ShapeDtypeStruct((VIEWS, 2 * ROWS, 2 * LANE), F32),
        grid=(1,),
        out_specs=whole((VIEWS, 2 * ROWS, 2 * LANE)),
        in_specs=[whole(field.shape), whole(stash.shape)],
        cost_estimate=pl.CostEstimate(flops=40_000_000_000, bytes_accessed=100_000_000, transcendentals=0),
        compiler_params=pltpu.CompilerParams(vmem_limit_bytes=VMEM_LIMIT),
        name="pack_estimate",
    )(field, stash)


def pack_field_kernel(field, out):
    tiles = windows_of([field[place] for place in range(VIEWS)])
    for place in range(VIEWS):
        out[place, :, :LANE] = tiles[place]
        out[place, :, LANE:] = tiles[place + 1]


def pack_field(field):
    return pl.pallas_call(
        pack_field_kernel,
        out_shape=jax.ShapeDtypeStruct((VIEWS, 2 * ROWS, 2 * LANE), F32),
        grid=(1,),
        out_specs=whole((VIEWS, 2 * ROWS, 2 * LANE)),
        in_specs=[whole(field.shape)],
        compiler_params=pltpu.CompilerParams(vmem_limit_bytes=VMEM_LIMIT),
        name="pack_field",
    )(field)


def tap_index(spread):
    inside = (spread >= 0) & (spread < TAPS)
    return jnp.where(inside, spread + TAP_LANE, LANE - 1)


def build_column_bands(received, high, low):
    high[...] = jnp.zeros_like(high)
    low[...] = jnp.zeros_like(low)
    shape = (LANE, LANE)
    square = tap_index(rows_of(shape) - lanes_of(shape) + RADIUS)
    shape = (ROWS, LANE)
    below = tap_index(rows_of(shape) - lanes_of(shape) + RADIUS + LANE)
    above = tap_index(rows_of(shape) - lanes_of(shape) + RADIUS - ROWS)
    for view in range(VIEWS):
        for term in range(RANK):
            taps = received[view, 6 + term : 7 + term, LANE:]
            band = halves(look_up(jnp.broadcast_to(taps, square.shape), square))
            lower = halves(look_up(jnp.broadcast_to(taps, below.shape), below))
            upper = halves(look_up(jnp.broadcast_to(taps, above.shape), above))
            for place, target in enumerate((high, low)):
                target[view, term, :LANE, :LANE] = band[place]
                target[view, term, LANE:, LANE:] = band[place]
                target[view, term, LANE : LANE + ROWS, :LANE] = lower[place]
                target[view, term, LANE - ROWS : LANE, LANE:] = upper[place]


def build_row_bands(view, first_row, stash, rows_lane, own_dst, high, low, turned_high, turned_low):
    taps_rows = [stash[3 + term : 4 + term, :] for term in range(RANK)]
    depth_rows = [stash[term : term + 1, :] for term in range(RANK)]
    mix_row = stash[9:10, :]
    centre = TAP_LANE + RADIUS
    dst_lane = rows_lane[pl.ds(view, 1), :]
    shape = (4 * ROWS, LANE)
    row = rows_of(shape)
    lane = lanes_of(shape)
    for part in range(2):
        dst = jnp.broadcast_to(dst_lane[:, part * LANE : (part + 1) * LANE], shape)
        spread = dst.astype(jnp.int32) - ROW_MARK - first_row - row + RADIUS
        index = tap_index(spread)
        if part == 1:
            index = jnp.where(lane < 3 * 2 * ROWS, index, LANE - 1)
        upper = (lane // ROWS) % 2 == 0
        for term in range(RANK):
            taps = jnp.broadcast_to(taps_rows[term], shape)
            band = look_up(taps, index)
            mix = mix_row[:, TAP_LANE + term : TAP_LANE + term + 1]
            depth = depth_rows[term] * mix
            for plane in range(2):
                from_first = depth[:, centre - plane : centre - plane + 1]
                from_second = depth[:, centre + 1 - plane : centre + 2 - plane]
                scaled = band * jnp.where(upper, from_first, from_second)
                band_high, band_low = halves(scaled)
                start = (term * 2 + plane) * 4 * ROWS
                columns = slice(part * LANE, (part + 1) * LANE)
                high[view, start : start + 4 * ROWS, columns] = band_high
                low[view, start : start + 4 * ROWS, columns] = band_low
    shape = (ROWS, LANE)
    lane = lanes_of(shape)
    spread = own_dst.astype(jnp.int32) - ROW_MARK - first_row - lane % (4 * ROWS) + RADIUS
    index = tap_index(spread)
    upper = lane < 4 * ROWS
    for term in range(RANK):
        taps = jnp.broadcast_to(taps_rows[term], shape)
        band = look_up(taps, index)
        mix = mix_row[:, TAP_LANE + term : TAP_LANE + term + 1]
        depth = depth_rows[term] * mix
        for plane in range(2):
            from_first = depth[:, centre + plane : centre + plane + 1]
            from_second = depth[:, centre + plane - 1 : centre + plane]
            scaled = band * jnp.where(upper, from_first, from_second)
            band_high, band_low = halves(scaled)
            start = (term * 2 + plane) * ROWS
            turned_high[view, start : start + ROWS, :] = band_high
            turned_low[view, start : start + ROWS, :] = band_low


def start_all(copies):
    for copy in copies:
        copy.start()
    return copies


def wait_all(copies):
    for copy in copies:
        copy.wait()


AHEAD = 1


def iteration_kernel(first, *refs):
    refs = list(refs)

    def take(count):
        taken = refs[:count]
        del refs[:count]
        return taken

    received_in, field_in = take(2)
    moves_in = None if first else take(1)[0]
    measured_in = take(5)
    tiles_in, out = take(2)
    received, field, moves, measured, tiles = take(5)
    col_high, col_low, row_high, row_low, turned_high, turned_low = take(6)
    x_high, x_low, result_ref, rows_lane, sems = take(5)

    strip = lax.axis_index("view")
    block = lax.axis_index("blk")
    first_column = pl.multiple_of(strip * LANE, LANE)
    number = 0

    def copy(source, target):
        nonlocal number
        number += 1
        return pltpu.make_async_copy(source, target, sems.at[number - 1])

    for_taps = start_all([copy(received_in, received)])
    others = [copy(field_in, field)]
    if not first:
        others.append(copy(moves_in.at[:, :, pl.ds(0, LANE)], moves))
    for place, source in enumerate(measured_in):
        others.append(copy(source, measured.at[place]))
    others.append(copy(tiles_in.at[:, :, pl.ds(first_column, LANE)], tiles))
    start_all(others)
    wait_all(for_taps)
    build_column_bands(received, col_high, col_low)
    wait_all(others)

    lane = lanes_of((2 * ROWS, LANE))
    column = lane + strip * LANE - HALF
    columns = LANE * VIEWS
    inside = [
        (column >= 0) & (column < columns),
        (column + LANE >= 0) & (column + LANE < columns),
    ]
    wide = lanes_of((ROWS, 2 * LANE))
    wide_column = wide + strip * LANE - HALF
    kept = (wide >= Q_FIRST) & (wide <= Q_LAST) & (wide_column >= 0) & (wide_column < columns)

    if first:
        moves[...] = field[:, :, :LANE]
    rows_lane[...] = jnp.transpose(moves[...].reshape(VIEWS * 2 * ROWS, LANE))
    x_high[:, (OWN + 1) * 2 * ROWS :, :] = jnp.zeros((VIEWS, 2 * ROWS, 2 * LANE), BF16)
    x_low[:, (OWN + 1) * 2 * ROWS :, :] = jnp.zeros((VIEWS, 2 * ROWS, 2 * LANE), BF16)

    def prepare(view):
        own_dst = pick_lane(moves[OWN], view)
        last = jnp.max(own_dst) - ROW_MARK
        phase = (last >= ((block + 1) * ROWS).astype(F32)).astype(jnp.int32)
        build_row_bands(
            view, (block - 2 + phase) * ROWS, received[view, :, LANE:], rows_lane,
            own_dst[:ROWS], row_high, row_low, turned_high, turned_low,
        )
        for slot in range(OWN + 1):
            shift = pick_lane(moves[slot], VIEWS + view).astype(jnp.int32)
            where = lane + shift
            index = where & (LANE - 1)
            left = look_up(field[slot, :, :LANE], index)
            right = look_up(field[slot, :, LANE:], index)
            moved = (jnp.where(where < LANE, left, right), jnp.where(where < 0, left, right))
            for part in range(2):
                high, low = halves(jnp.where(inside[part], moved[part], 0.0))
                rows = slice(slot * 2 * ROWS, (slot + 1) * 2 * ROWS)
                x_high[view, rows, part * LANE : (part + 1) * LANE] = high
                x_low[view, rows, part * LANE : (part + 1) * LANE] = low
        return phase, shift

    def finish(view, phase, shift):
        xh, xl = x_high[view], x_low[view]
        layers = triple(row_high[view], row_low[view], xh, xl, dot)
        blurred = None
        height = 8 * ROWS
        for term in range(RANK):
            high, low = halves(layers[term * height : (term + 1) * height])
            part = triple(high, low, col_high[view, term], col_low[view, term], dot)
            blurred = part if blurred is None else blurred + part

        quotients = []
        for plane in range(2):
            for place in range(4):
                rows = slice(plane * ROWS, (plane + 1) * ROWS)
                seen = jnp.where(
                    phase == 1, measured[place + 1, view, rows], measured[place, view, rows]
                )
                start = (plane * 4 + place) * ROWS
                row_block = block - 2 + phase + place
                fine = kept & (row_block >= 0) & (row_block < VIEWS * 8)
                quotients.append(jnp.where(fine, seen / blurred[start : start + ROWS], 0.0))
        quotient = jnp.concatenate(quotients, axis=0)
        high, low = halves(quotient)
        layers = triple(turned_high[view], turned_low[view], high, low, dot)
        where = lane + shift
        index = where & (LANE - 1)
        adjoint = None
        height = 2 * ROWS
        for term in range(RANK):
            layer = layers[term * height : (term + 1) * height]
            left = look_up(layer[:, :LANE], index)
            right = look_up(layer[:, LANE:], index)
            moved = jnp.concatenate(
                [jnp.where(where < LANE, left, right), jnp.where(where < 0, left, right)], axis=1
            )
            high, low = halves(moved)
            band_high = col_high[view, term, HALF : HALF + LANE, :]
            band_low = col_low[view, term, HALF : HALF + LANE, :]
            part = triple(high, low, band_high, band_low, dot_turned)
            adjoint = part if adjoint is None else adjoint + part
        source = column + HALF + shift
        returned = jnp.where((source >= 0) & (source < columns), adjoint, 0.0)
        chosen = pick_lane(received[view, :, :LANE], TILE_LANE)
        weight = jnp.zeros((2 * ROWS, LANE), F32)
        for tile in range(tiles.shape[0]):
            tall = jnp.concatenate([tiles[tile]] * 4, axis=0)
            weight = jnp.where(chosen == tile, tall, weight)
        return weight * returned, weight


    total = jnp.zeros((2 * ROWS, LANE), F32)
    weight_total = jnp.zeros((2 * ROWS, LANE), F32)
    waiting = [prepare(view) for view in range(AHEAD)]
    for view in range(VIEWS):
        if view + AHEAD < VIEWS:
            waiting.append(prepare(view + AHEAD))
        more, weight = finish(view, *waiting[view])
        total = total + more
        weight_total = weight_total + weight

    lower = pltpu.roll(field[OWN, :, :LANE], HALF, 1)
    upper = pltpu.roll(field[OWN, :, LANE:], HALF, 1)
    own = jnp.where(lane < HALF, lower, upper)
    result_ref[...] = own * total / weight_total
    wait_all(start_all([copy(result_ref, out.at[place]) for place in range(VIEWS)]))


def iteration(field, moves, received, neighbours, weight_tiles):
    rows = 2 * ROWS
    window = (VIEWS, rows, 2 * LANE)
    col_shape = (VIEWS, RANK, 2 * LANE, 2 * LANE)
    row_shape = (VIEWS, RANK * 8 * ROWS, 2 * LANE)
    turned_shape = (VIEWS, RANK * 2 * ROWS, LANE)
    operands = [received, field, *([] if moves is None else [moves]), *neighbours, weight_tiles]
    scratch = [
        pltpu.VMEM(window, F32),
        pltpu.VMEM(window, F32),
        pltpu.VMEM((VIEWS, rows, LANE), F32),
        pltpu.VMEM((5,) + window, F32),
        pltpu.VMEM(weight_tiles.shape[:2] + (LANE,), F32),
        pltpu.VMEM(col_shape, BF16),
        pltpu.VMEM(col_shape, BF16),
        pltpu.VMEM(row_shape, BF16),
        pltpu.VMEM(row_shape, BF16),
        pltpu.VMEM(turned_shape, BF16),
        pltpu.VMEM(turned_shape, BF16),
        pltpu.VMEM((VIEWS, 2 * LANE, 2 * LANE), BF16),
        pltpu.VMEM((VIEWS, 2 * LANE, 2 * LANE), BF16),
        pltpu.VMEM((rows, LANE), F32),
        pltpu.VMEM((LANE, 2 * LANE), F32),
        pltpu.SemaphoreType.DMA((24,)),
    ]
    anywhere = pl.BlockSpec(memory_space=pl.ANY)
    return pl.pallas_call(
        lambda *refs: iteration_kernel(moves is None, *refs),
        out_shape=jax.ShapeDtypeStruct((VIEWS, rows, LANE), F32),
        in_specs=[anywhere] * len(operands),
        out_specs=anywhere,
        scratch_shapes=scratch,
        compiler_params=pltpu.CompilerParams(vmem_limit_bytes=VMEM_LIMIT),
        name="iteration_first" if moves is None else "iteration_next",
    )(*operands)


def step_by_view(values):
    blocks = lax.axis_size("blk")
    route = []
    for view, step in enumerate(STEPS):
        for block in range(blocks):
            if 0 <= block + step < blocks:
                route.append((view * blocks + block, view * blocks + block + step))
    return lax.ppermute(values, ("view", "blk"), route)


def from_block(values, offset):
    blocks = lax.axis_size("blk")
    route = [(b + offset, b) for b in range(blocks) if 0 <= b + offset < blocks]
    return lax.ppermute(values, "blk", route)


def over_views(values):
    return lax.all_to_all(values, "view", 0, 0)


def body(
    estimate,
    measured,
    psf_z,
    psf_y,
    psf_x,
    psf_mix,
    weight_tiles,
    tile_index,
    src_row,
    dst_row,
    col_shift,
    back_shift,
):
    planes, row_count, col_count = estimate.shape
    stepped = step_by_view(estimate)
    received = over_views(
        pack_measured(measured, dst_row, back_shift, tile_index, psf_z, psf_y, psf_x, psf_mix)
    )
    moves, later = lax.optimization_barrier((registration(received), received))
    moves = step_by_view(moves)
    packed = pack_estimate(stepped, moves)
    far = [from_block(later, offset) for offset in (-2, 2)]
    near = [from_block(later, offset) for offset in (-1, 1)]
    neighbours = [far[0], near[0], received, near[1], far[1]]
    field = over_views(packed)
    moves = field
    strips = iteration(field, None, received, neighbours, weight_tiles)
    for _ in range(ITERS - 1):
        field = over_views(pack_field(step_by_view(over_views(strips))))
        strips = iteration(field, moves, received, neighbours, weight_tiles)
    strips = over_views(strips).reshape(VIEWS, planes, row_count, LANE)
    return jnp.transpose(strips, (1, 2, 0, 3)).reshape(planes, row_count, col_count)


def solution(mesh):
    in_specs = (
        P(None, "blk", None),
        P("view", None, "blk", None),
        P("view", None, None),
        P("view", None, None),
        P("view", None, None),
        P("view", None),
        P(),
        P("view", "blk"),
        P("view", "blk"),
        P("view", "blk"),
        P("view", "blk"),
        P("view", "blk"),
    )
    out_specs = P(None, "blk", None)
    return jax.shard_map(body, mesh=mesh, in_specs=in_specs, out_specs=out_specs, check_vma=False)
```

time: 148 us -> 119 us (0.80)
  the two profiles are of different devices: /device:TPU:272 before, /device:TPU:264 now
where the time goes in v2:
time: 119 us
  blocking collectives  47 us (39%)
  Pallas kernels  29.1 us (24%)
  starting transfers between devices  28 us (24%)
  waiting for transfers between devices  11.7 us (10%)
  local copies, waits for them, and re-layouts  2.64 us (2%)
    all_to_all x4, blocking collectives, over_views(): return lax.all_to_all(values, 'view', 0, 0)  47 us
    pallas_call x2, Pallas kernels, iteration(): pl.pallas_call(lambda *refs: iteration_kernel(moves is None, *refs), out_...  23.6 us
    ppermute x4, starting transfers between devices, from_block(): return lax.ppermute(values, 'blk', route)  14.7 us
    ppermute x3, starting transfers between devices, step_by_view(): return lax.ppermute(values, ('view', 'blk'), route)  8.88 us
    ppermute x3, waiting for transfers between devices, step_by_view(): return lax.ppermute(values, ('view', 'blk'), route)  4.94 us
    all_to_all x1, starting transfers between devices, over_views(): return lax.all_to_all(values, 'view', 0, 0)  4.43 us
    all_to_all x1, waiting for transfers between devices, over_views(): return lax.all_to_all(values, 'view', 0, 0)  4.04 us
    ppermute x4, waiting for transfers between devices, from_block(): return lax.ppermute(values, 'blk', route)  2.73 us
  transfers between devices with their start and end apart: 8, of which 3 were waited for; matrix products, arithmetic and copies ran while one was open for 0% of the time, Pallas kernels for 1%

profile of v2, /device:TPU:264, one launch (start us, length us, event | category | flops | bytes accessed | tf_op | source)
XLA Modules:
  0.0 118.6 jit_solution(347625015431250283)
XLA Ops:
  0.0 2.1 %pack_measured.1 = f32[8,32,256]{2,1,0:T(8,128)} custom-call(f32[1,2,16,1024]{3,2,1,0:T(8,128)} %measured.1, s32[1,16]{1,0:T(1,128)} %dst_row.1, s32[1,16]{1,0:T(1,128)} %back_shift.1, s32[1,2]{1,0:T(1,128)} %tile_index.1, f32[3,1,31]{2,1,0:T(1,128)} %bitcast.11, f32[3,1,31]{2,1,0:T(1,128)} %bitcast.12, f32[3,1,31]{2,1,0:T(1,128)} %bitcast.13, f32[1,3]{1,0:T(1,128)} %psf_mix.1), custom_call_target="tpu_custom_call" | custom-call | tf_op jit(solution)/shard_map/pack_measured/pallas_call | solution.py:123
  2.1 4.4 %all-to-all-start = ((f32[8,32,256]{2,1,0:T(8,128)}), f32[8,32,256]{2,1,0:T(8,128)S(1)}, u32[]{:S(2)}, u32[]{:S(2)}) async-start(f32[8,32,256]{2,1,0:T(8,128)} %pack_measured.1), calls=%async_computation | async-start | bytes 524288 | tf_op jit(solution)/shard_map/all_to_all | solution.py:470
  6.5 3.5 %collective-permute-start = (f32[2,16,1024]{2,1,0:T(8,128)S(1)}, f32[2,16,1024]{2,1,0:T(8,128)S(1)}, u32[]{:S(2)}, u32[]{:S(2)}) collective-permute-start(f32[2,16,1024]{2,1,0:T(8,128)S(1)} %copy-done.6), channel_id=1, source_target_pairs={{0,1},{1,2},{2,3},{3,4},{4,5},{5,6},{6,7},{7,8},{8,9},{9,10},{10,1... | collective-permute-start | bytes 393224 | tf_op jit(solution)/shard_map/ppermute | solution.py:460
  10.0 4.0 %all-to-all-done.refs_0_.refs_4_.refs_5_ = f32[8,32,256]{2,1,0:T(8,128)S(1)} async-done(((f32[8,32,256]{2,1,0:T(8,128)}), f32[8,32,256]{2,1,0:T(8,128)S(1)}, u32[]{:S(2)}, u32[]{:S(2)}) %all-to-all-start) | async-done | bytes 262176 | tf_op jit(solution)/shard_map/all_to_all | solution.py:470
  14.1 3.5 %collective-permute-start.1 = (f32[32,128]{1,0:T(8,128)S(1)}, f32[32,128]{1,0:T(8,128)S(1)}, u32[]{:S(2)}, u32[]{:S(2)}) collective-permute-start(f32[32,128]{1,0:T(8,128)S(1)} %slice_reduce_fusion), channel_id=1, source_target_pairs={{0,1},{1,2},{2,3},{3,4},{4,5},{5,6},{6,7},{7,8},{8,9},{9,10},{10,1... | collective-permute-start | bytes 49160 | tf_op jit(solution)/shard_map/ppermute | solution.py:460
  17.6 5.6 %collective-permute-start.5 = (f32[8,32,256]{2,1,0:T(8,128)S(1)}, f32[8,32,256]{2,1,0:T(8,128)S(1)}, u32[]{:S(2)}, u32[]{:S(2)}) collective-permute-start(f32[8,32,256]{2,1,0:T(8,128)S(1)} %all-to-all-done.refs_0_.refs_4_.refs_5_), channel_id=1, source_target_pairs={{2,0},{3,1},{4,2},{5,3},{6,4},{7,5},{8,6},{9,7},{10,8},{11,9},{12,... | collective-permute-start | bytes 786440 | tf_op jit(solution)/shard_map/ppermute | solution.py:466
  23.1 1.9 %collective-permute-start.4 = (f32[8,32,256]{2,1,0:T(8,128)S(1)}, f32[8,32,256]{2,1,0:T(8,128)S(1)}, u32[]{:S(2)}, u32[]{:S(2)}) collective-permute-start(f32[8,32,256]{2,1,0:T(8,128)S(1)} %all-to-all-done.refs_0_.refs_4_.refs_5_), channel_id=1, source_target_pairs={{1,0},{2,1},{3,2},{4,3},{5,4},{6,5},{7,6},{8,7},{9,8},{10,9},{11,1... | collective-permute-start | bytes 786440 | tf_op jit(solution)/shard_map/ppermute | solution.py:466
  25.1 3.9 %collective-permute-start.3 = (f32[8,32,256]{2,1,0:T(8,128)S(1)}, f32[8,32,256]{2,1,0:T(8,128)S(1)}, u32[]{:S(2)}, u32[]{:S(2)}) collective-permute-start(f32[8,32,256]{2,1,0:T(8,128)S(1)} %all-to-all-done.refs_0_.refs_4_.refs_5_), channel_id=1, source_target_pairs={{0,1},{1,2},{2,3},{3,4},{4,5},{5,6},{6,7},{7,8},{8,9},{9,10},{10,1... | collective-permute-start | bytes 786440 | tf_op jit(solution)/shard_map/ppermute | solution.py:466
  29.0 0.0 collective-permute-done.field
  29.0 0.0 copy-start.7
  29.0 3.3 %collective-permute-start.2 = (f32[8,32,256]{2,1,0:T(8,128)S(1)}, f32[8,32,256]{2,1,0:T(8,128)S(1)}, u32[]{:S(2)}, u32[]{:S(2)}) collective-permute-start(f32[8,32,256]{2,1,0:T(8,128)S(1)} %all-to-all-done.refs_0_.refs_4_.refs_5_), channel_id=1, source_target_pairs={{0,2},{1,3},{2,4},{3,5},{4,6},{5,7},{6,8},{7,9},{8,10},{9,11},{10,... | collective-permute-start | bytes 786440 | tf_op jit(solution)/shard_map/ppermute | solution.py:466
  32.3 0.0 collective-permute-done.1.stash
  32.3 0.6 copy-done.8
  32.9 1.7 %pack_estimate.1 = f32[8,32,256]{2,1,0:T(8,128)} custom-call(f32[2,16,1024]{2,1,0:T(8,128)} %copy-done.7, f32[32,128]{1,0:T(8,128)} %copy-done.8), custom_call_target="tpu_custom_call" | custom-call | flops 40000000000 | bytes 100000000 | tf_op jit(solution)/shard_map/pack_estimate/pallas_call | solution.py:151
  34.6 11.6 %all_to_all.25.refs_1_.refs_2_ = f32[8,32,256]{2,1,0:T(8,128)} all-to-all(f32[8,32,256]{2,1,0:T(8,128)} %pack_estimate.1), channel_id=1, replica_groups=mesh['view'=8,'blk'=64] {'view'}, dimensions={0} | all-to-all | bytes 524288 | tf_op jit(solution)/shard_map/all_to_all | solution.py:470
  46.3 0.0 collective-permute-done.5.refs_6_.refs_7_
  46.3 0.0 collective-permute-done.4.refs_5_.refs_6_
  46.3 0.0 collective-permute-done.3.refs_3_.refs_4_
  46.3 0.0 copy-start.3
  46.3 2.7 %collective-permute-done.2.refs_2_.refs_3_ = f32[8,32,256]{2,1,0:T(8,128)S(1)} collective-permute-done((f32[8,32,256]{2,1,0:T(8,128)S(1)}, f32[8,32,256]{2,1,0:T(8,128)S(1)}, u32[]{:S(2)}, u32[]{:S(2)}) %collective-permute-start.2) | collective-permute-done | bytes 262176 | tf_op jit(solution)/shard_map/ppermute | solution.py:466
  49.0 0.0 copy-start.4
  49.1 0.7 copy-done.4
  49.8 11.8 %iteration_first.1 = f32[8,32,128]{2,1,0:T(8,128)} custom-call(f32[8,32,256]{2,1,0:T(8,128)} %copy-done, f32[8,32,256]{2,1,0:T(8,128)} %all_to_all.25.refs_1_.refs_2_, f32[8,32,256]{2,1,0:T(8,128)} %copy-done.4, f32[8,32,256]{2,1,0:T(8,128)} %copy-done.3, f32[8,32,256]{2,1,0:T(8,128)} %copy-done, f32[8,32,256]{2,1,0:T(8,128)} %copy-done.2, ...), custom_call_target="tpu_custom_call" | custom-call | tf_op jit(solution)/shard_map/iteration_first/pallas_call | solution.py:442
  61.6 9.4 %all_to_all.26 = f32[8,32,128]{2,1,0:T(8,128)S(1)} all-to-all(f32[8,32,128]{2,1,0:T(8,128)} %iteration_first.1), channel_id=1, replica_groups=mesh['view'=8,'blk'=64] {'view'}, dimensions={0} | all-to-all | bytes 262144 | tf_op jit(solution)/shard_map/all_to_all | solution.py:470
  71.0 1.9 %collective-permute-start.6 = (f32[8,32,128]{2,1,0:T(8,128)S(1)}, f32[8,32,128]{2,1,0:T(8,128)S(1)}, u32[]{:S(2)}, u32[]{:S(2)}) collective-permute-start(f32[8,32,128]{2,1,0:T(8,128)S(1)} %all_to_all.26), channel_id=1, source_target_pairs={{0,1},{1,2},{2,3},{3,4},{4,5},{5,6},{6,7},{7,8},{8,9},{9,10},{10,1... | collective-permute-start | bytes 393224 | tf_op jit(solution)/shard_map/ppermute | solution.py:460
  72.9 4.9 %collective-permute-done.6.field = f32[8,32,128]{2,1,0:T(8,128)S(1)} collective-permute-done((f32[8,32,128]{2,1,0:T(8,128)S(1)}, f32[8,32,128]{2,1,0:T(8,128)S(1)}, u32[]{:S(2)}, u32[]{:S(2)}) %collective-permute-start.6) | collective-permute-done | bytes 131104 | tf_op jit(solution)/shard_map/ppermute | solution.py:460
  77.9 0.7 copy-done.5
  78.5 1.7 %pack_field.1 = f32[8,32,256]{2,1,0:T(8,128)} custom-call(f32[8,32,128]{2,1,0:T(8,128)} %copy-done.5), custom_call_target="tpu_custom_call" | custom-call | tf_op jit(solution)/shard_map/pack_field/pallas_call | solution.py:171
  80.2 16.5 %all_to_all.27.refs_1_ = f32[8,32,256]{2,1,0:T(8,128)} all-to-all(f32[8,32,256]{2,1,0:T(8,128)} %pack_field.1), channel_id=1, replica_groups=mesh['view'=8,'blk'=64] {'view'}, dimensions={0} | all-to-all | bytes 524288 | tf_op jit(solution)/shard_map/all_to_all | solution.py:470
  96.7 11.8 %iteration_next.1 = f32[8,32,128]{2,1,0:T(8,128)} custom-call(f32[8,32,256]{2,1,0:T(8,128)} %copy-done, f32[8,32,256]{2,1,0:T(8,128)} %all_to_all.27.refs_1_, f32[8,32,256]{2,1,0:T(8,128)} %all_to_all.25.refs_1_.refs_2_, f32[8,32,256]{2,1,0:T(8,128)} %copy-done.4, f32[8,32,256]{2,1,0:T(8,128)} %copy-done.3, f32[8,32,256]{2,1,0:T(8,128)} %copy-done, ...), custom_call_target="tpu_custom_call" | custom-call | tf_op jit(solution)/shard_map/iteration_next/pallas_call | solution.py:442
  108.5 9.4 %all_to_all.28 = f32[8,32,128]{2,1,0:T(8,128)S(1)} all-to-all(f32[8,32,128]{2,1,0:T(8,128)} %iteration_next.1), channel_id=1, replica_groups=mesh['view'=8,'blk'=64] {'view'}, dimensions={0} | all-to-all | bytes 262144 | tf_op jit(solution)/shard_map/all_to_all | solution.py:470
  118.0 0.7 copy.14
  (13 shorter events, 0.0 us)
Async XLA Ops:
  2.1 4.4 %copy-start.6 = (f32[2,16,1024]{2,1,0:T(8,128)S(1)}, f32[2,16,1024]{2,1,0:T(8,128)}, u32[]{:S(2)}) copy-start(f32[2,16,1024]{2,1,0:T(8,128)} %param.12) | copy-start | bytes 393220
  2.1 12.0 %all-to-all-start = ((f32[8,32,256]{2,1,0:T(8,128)}), f32[8,32,256]{2,1,0:T(8,128)S(1)}, u32[]{:S(2)}, u32[]{:S(2)}) async-start(f32[8,32,256]{2,1,0:T(8,128)} %pack_measured.1), calls=%async_computation | async-start | bytes 524288 | tf_op jit(solution)/shard_map/all_to_all | solution.py:470
  6.5 22.5 %collective-permute-start = (f32[2,16,1024]{2,1,0:T(8,128)S(1)}, f32[2,16,1024]{2,1,0:T(8,128)S(1)}, u32[]{:S(2)}, u32[]{:S(2)}) collective-permute-start(f32[2,16,1024]{2,1,0:T(8,128)S(1)} %copy-done.6), channel_id=1, source_target_pairs={{0,1},{1,2},{2,3},{3,4},{4,5},{5,6},{6,7},{7,8},{8,9},{9,10},{10,1... | collective-permute-start | bytes 393224 | tf_op jit(solution)/shard_map/ppermute | solution.py:460
  14.1 20.6 %copy-start = (f32[8,32,256]{2,1,0:T(8,128)}, f32[8,32,256]{2,1,0:T(8,128)S(1)}, u32[]{:S(2)}) copy-start(f32[8,32,256]{2,1,0:T(8,128)S(1)} %all-to-all-done.refs_0_.refs_4_.refs_5_) | copy-start | bytes 786436
  14.1 18.2 %collective-permute-start.1 = (f32[32,128]{1,0:T(8,128)S(1)}, f32[32,128]{1,0:T(8,128)S(1)}, u32[]{:S(2)}, u32[]{:S(2)}) collective-permute-start(f32[32,128]{1,0:T(8,128)S(1)} %slice_reduce_fusion), channel_id=1, source_target_pairs={{0,1},{1,2},{2,3},{3,4},{4,5},{5,6},{6,7},{7,8},{8,9},{9,10},{10,1... | collective-permute-start | bytes 49160 | tf_op jit(solution)/shard_map/ppermute | solution.py:460
  17.6 28.7 %collective-permute-start.5 = (f32[8,32,256]{2,1,0:T(8,128)S(1)}, f32[8,32,256]{2,1,0:T(8,128)S(1)}, u32[]{:S(2)}, u32[]{:S(2)}) collective-permute-start(f32[8,32,256]{2,1,0:T(8,128)S(1)} %all-to-all-done.refs_0_.refs_4_.refs_5_), channel_id=1, source_target_pairs={{2,0},{3,1},{4,2},{5,3},{6,4},{7,5},{8,6},{9,7},{10,8},{11,9},{12,... | collective-permute-start | bytes 786440 | tf_op jit(solution)/shard_map/ppermute | solution.py:466
  23.1 23.1 %collective-permute-start.4 = (f32[8,32,256]{2,1,0:T(8,128)S(1)}, f32[8,32,256]{2,1,0:T(8,128)S(1)}, u32[]{:S(2)}, u32[]{:S(2)}) collective-permute-start(f32[8,32,256]{2,1,0:T(8,128)S(1)} %all-to-all-done.refs_0_.refs_4_.refs_5_), channel_id=1, source_target_pairs={{1,0},{2,1},{3,2},{4,3},{5,4},{6,5},{7,6},{8,7},{9,8},{10,9},{11,1... | collective-permute-start | bytes 786440 | tf_op jit(solution)/shard_map/ppermute | solution.py:466
  25.1 21.2 %collective-permute-start.3 = (f32[8,32,256]{2,1,0:T(8,128)S(1)}, f32[8,32,256]{2,1,0:T(8,128)S(1)}, u32[]{:S(2)}, u32[]{:S(2)}) collective-permute-start(f32[8,32,256]{2,1,0:T(8,128)S(1)} %all-to-all-done.refs_0_.refs_4_.refs_5_), channel_id=1, source_target_pairs={{0,1},{1,2},{2,3},{3,4},{4,5},{5,6},{6,7},{7,8},{8,9},{9,10},{10,1... | collective-permute-start | bytes 786440 | tf_op jit(solution)/shard_map/ppermute | solution.py:466
  29.0 3.3 %copy-start.7 = (f32[2,16,1024]{2,1,0:T(8,128)}, f32[2,16,1024]{2,1,0:T(8,128)S(1)}, u32[]{:S(2)}) copy-start(f32[2,16,1024]{2,1,0:T(8,128)S(1)} %collective-permute-done.field) | copy-start | bytes 393220
  29.0 20.0 %collective-permute-start.2 = (f32[8,32,256]{2,1,0:T(8,128)S(1)}, f32[8,32,256]{2,1,0:T(8,128)S(1)}, u32[]{:S(2)}, u32[]{:S(2)}) collective-permute-start(f32[8,32,256]{2,1,0:T(8,128)S(1)} %all-to-all-done.refs_0_.refs_4_.refs_5_), channel_id=1, source_target_pairs={{0,2},{1,3},{2,4},{3,5},{4,6},{5,7},{6,8},{7,9},{8,10},{9,11},{10,... | collective-permute-start | bytes 786440 | tf_op jit(solution)/shard_map/ppermute | solution.py:466
  32.3 0.6 copy-start.8
  46.3 2.8 %copy-start.1 = (f32[8,32,256]{2,1,0:T(8,128)}, f32[8,32,256]{2,1,0:T(8,128)S(1)}, u32[]{:S(2)}) copy-start(f32[8,32,256]{2,1,0:T(8,128)S(1)} %collective-permute-done.5.refs_6_.refs_7_) | copy-start | bytes 786436
  46.3 2.8 %copy-start.2 = (f32[8,32,256]{2,1,0:T(8,128)}, f32[8,32,256]{2,1,0:T(8,128)S(1)}, u32[]{:S(2)}) copy-start(f32[8,32,256]{2,1,0:T(8,128)S(1)} %collective-permute-done.4.refs_5_.refs_6_) | copy-start | bytes 786436
  46.3 2.7 %copy-start.3 = (f32[8,32,256]{2,1,0:T(8,128)}, f32[8,32,256]{2,1,0:T(8,128)S(1)}, u32[]{:S(2)}) copy-start(f32[8,32,256]{2,1,0:T(8,128)S(1)} %collective-permute-done.3.refs_3_.refs_4_) | copy-start | bytes 786436
  49.0 0.7 copy-start.4
  71.0 6.8 %collective-permute-start.6 = (f32[8,32,128]{2,1,0:T(8,128)S(1)}, f32[8,32,128]{2,1,0:T(8,128)S(1)}, u32[]{:S(2)}, u32[]{:S(2)}) collective-permute-start(f32[8,32,128]{2,1,0:T(8,128)S(1)} %all_to_all.26), channel_id=1, source_target_pairs={{0,1},{1,2},{2,3},{3,4},{4,5},{5,6},{6,7},{7,8},{8,9},{9,10},{10,1... | collective-permute-start | bytes 393224 | tf_op jit(solution)/shard_map/ppermute | solution.py:460
  77.8 0.7 copy-start.5

commit v3 on v2

--- a/solution.py
+++ b/solution.py
@@ -19,13 +19,26 @@
 Q_FIRST, Q_LAST = 41, 214
 STEPS = (1, -1, 2, -2, 3, -3, 0, 0)
 OWN = 6
+SEEN = 3 * LANE
 F32 = jnp.float32
 BF16 = jnp.bfloat16
-VMEM_LIMIT = 65_000_000
+VMEM_LIMIT = 24 * 1024 * 1024
+SMALL_LIMIT = 4 * 1024 * 1024
 
 
 def whole(shape):
     return pl.BlockSpec(tuple(shape), lambda i: (0,) * len(shape))
+
+
+def start_all(copies):
+    for copy in copies:
+        copy.start()
+    return copies
+
+
+def wait_all(copies):
+    for copy in copies:
+        copy.wait()
 
 
 def lanes_of(shape):
@@ -79,7 +92,7 @@
 
 
 def pack_measured_kernel(
-    measured, dst_row, back_shift, tile_index, psf_z, psf_y, psf_x, psf_mix, out, table
+    measured, dst_row, back_shift, tile_index, psf_z, psf_y, psf_x, psf_mix, out_ref, table, out, sems
 ):
     rows = 2 * ROWS
     view = lax.axis_index("view")
@@ -109,72 +122,131 @@
     mix = psf_mix[...]
     table[9:10, TAP_LANE : TAP_LANE + RANK] = mix / jnp.sum(mix, axis=1, keepdims=True)
     taps = table[:rows, :]
-    values = measured[0].reshape(rows, measured.shape[3])
-    strips = [values[:, place * LANE : (place + 1) * LANE] for place in range(VIEWS)]
-    tiles = windows_of(strips)
+    stash = jnp.where(lane < TAP_LANE, moves, taps)[:ROWS]
+    lane = lanes_of((ROWS, LANE))
+    zero = jnp.zeros((ROWS, LANE), F32)
+    strips = []
+    for plane in range(2):
+        values = measured[0, plane]
+        strips.append([values[:, place * LANE : (place + 1) * LANE] for place in range(VIEWS)])
     for place in range(VIEWS):
-        out[place, :, :LANE] = jnp.where(lane < Q_FIRST, moves, tiles[place])
-        out[place, :, LANE:] = jnp.where(lane < TAP_LANE, tiles[place + 1], taps)
+        before = [row[place - 1] if place > 0 else zero for row in strips]
+        after = [row[place + 1] if place < VIEWS - 1 else zero for row in strips]
+        edges = jnp.where(lane < 96, pltpu.roll(after[1], HALF, 1), before[1])
+        edges = jnp.where(lane < HALF, pltpu.roll(before[0], HALF, 1), edges)
+        edges = jnp.where(lane < 32, after[0], edges)
+        turned = [pltpu.roll(row[place], HALF, 1) for row in strips]
+        for number, tile in enumerate((turned[0], turned[1], edges, stash)):
+            out[place, :, number * LANE : (number + 1) * LANE] = tile
+    wait_all(start_all([pltpu.make_async_copy(out, out_ref, sems.at[0])]))
+
+
+ANYWHERE = pl.BlockSpec(memory_space=pl.ANY)
 
 
 def pack_measured(measured, dst_row, back_shift, tile_index, psf_z, psf_y, psf_x, psf_mix):
     turned = [jnp.transpose(psf, (1, 0, 2)) for psf in (psf_z, psf_y, psf_x)]
     operands = (measured, dst_row, back_shift, tile_index, *turned, psf_mix)
+    shape = (VIEWS, ROWS, 4 * LANE)
     return pl.pallas_call(
         pack_measured_kernel,
-        out_shape=jax.ShapeDtypeStruct((VIEWS, 2 * ROWS, 2 * LANE), F32),
+        out_shape=jax.ShapeDtypeStruct(shape, F32),
         grid=(1,),
-        out_specs=whole((VIEWS, 2 * ROWS, 2 * LANE)),
-        scratch_shapes=[pltpu.VMEM((LANE, LANE), F32)],
         in_specs=[whole(operand.shape) for operand in operands],
-        compiler_params=pltpu.CompilerParams(vmem_limit_bytes=VMEM_LIMIT),
+        out_specs=ANYWHERE,
+        scratch_shapes=[
+            pltpu.VMEM((LANE, LANE), F32),
+            pltpu.VMEM(shape, F32),
+            pltpu.SemaphoreType.DMA((1,)),
+        ],
         name="pack_measured",
     )(*operands)
 
 
-def registration(received):
-    return jnp.sum(received[:, :, :LANE], axis=0)
-
-
-def pack_estimate_kernel(field, stash, out):
-    rows = 2 * ROWS
-    values = field[...].reshape(rows, field.shape[2])
-    strips = [values[:, place * LANE : (place + 1) * LANE] for place in range(VIEWS)]
-    tiles = windows_of(strips)
-    lane = lanes_of((rows, LANE))
-    for place in range(VIEWS):
-        out[place, :, :LANE] = jnp.where(lane < 2 * VIEWS, stash[...], tiles[place])
-        out[place, :, LANE:] = tiles[place + 1]
-
-
-def pack_estimate(field, stash):
+def pack_estimate_kernel(field_in, moves_in, out_ref, field, moves, out, sems):
+    fetches = [
+        pltpu.make_async_copy(field_in, field, sems.at[0]),
+        pltpu.make_async_copy(moves_in, moves, sems.at[1]),
+    ]
+    start_all(fetches)
+    wait_all(fetches)
+    lane = lanes_of((ROWS, LANE))
+    for plane in range(2):
+        strips = [field[plane, :, place * LANE : (place + 1) * LANE] for place in range(VIEWS)]
+        tiles = windows_of(strips)
+        for place in range(VIEWS):
+            out[place, plane] = jnp.where(lane < 2 * VIEWS, moves[...], tiles[place])
+            out[place, 2 + plane] = tiles[place + 1]
+    wait_all(start_all([pltpu.make_async_copy(out, out_ref, sems.at[2])]))
+
+
+def pack_estimate(field, moves):
+    shape = (VIEWS, 4, ROWS, LANE)
     return pl.pallas_call(
         pack_estimate_kernel,
-        out_shape=jax.ShapeDtypeStruct((VIEWS, 2 * ROWS, 2 * LANE), F32),
-        grid=(1,),
-        out_specs=whole((VIEWS, 2 * ROWS, 2 * LANE)),
-        in_specs=[whole(field.shape), whole(stash.shape)],
-        cost_estimate=pl.CostEstimate(flops=40_000_000_000, bytes_accessed=100_000_000, transcendentals=0),
-        compiler_params=pltpu.CompilerParams(vmem_limit_bytes=VMEM_LIMIT),
+        out_shape=jax.ShapeDtypeStruct(shape, F32),
+        in_specs=[ANYWHERE] * 2,
+        out_specs=ANYWHERE,
+        scratch_shapes=[
+            pltpu.VMEM(field.shape, F32),
+            pltpu.VMEM(moves.shape, F32),
+            pltpu.VMEM(shape, F32),
+            pltpu.SemaphoreType.DMA((3,)),
+        ],
+        cost_estimate=pl.CostEstimate(
+            flops=40_000_000_000, bytes_accessed=100_000_000, transcendentals=0
+        ),
+        compiler_params=pltpu.CompilerParams(vmem_limit_bytes=SMALL_LIMIT),
         name="pack_estimate",
-    )(field, stash)
-
-
-def pack_field_kernel(field, out):
+    )(field, moves)
+
+
+def hand_on_kernel(*refs):
+    del refs
+
+
+def hand_on(arrays):
+    count = len(arrays)
+    return pl.pallas_call(
+        hand_on_kernel,
+        out_shape=[jax.ShapeDtypeStruct(array.shape, array.dtype) for array in arrays],
+        in_specs=[ANYWHERE] * count,
+        out_specs=[ANYWHERE] * count,
+        input_output_aliases={number: number for number in range(count)},
+        cost_estimate=pl.CostEstimate(
+            flops=2_000_000_000, bytes_accessed=1_000_000, transcendentals=0
+        ),
+        compiler_params=pltpu.CompilerParams(vmem_limit_bytes=SMALL_LIMIT),
+        name="hand_on",
+    )(*arrays)
+
+
+def pack_field_kernel(field_in, out_ref, field, out, sems):
+    fetch = pltpu.make_async_copy(field_in, field, sems.at[0])
+    fetch.start()
+    fetch.wait()
     tiles = windows_of([field[place] for place in range(VIEWS)])
     for place in range(VIEWS):
-        out[place, :, :LANE] = tiles[place]
-        out[place, :, LANE:] = tiles[place + 1]
+        out[place, 0:2] = tiles[place].reshape(2, ROWS, LANE)
+        out[place, 2:4] = tiles[place + 1].reshape(2, ROWS, LANE)
+    send = pltpu.make_async_copy(out, out_ref, sems.at[1])
+    send.start()
+    send.wait()
 
 
 def pack_field(field):
+    shape = (VIEWS, 4, ROWS, LANE)
     return pl.pallas_call(
         pack_field_kernel,
-        out_shape=jax.ShapeDtypeStruct((VIEWS, 2 * ROWS, 2 * LANE), F32),
-        grid=(1,),
-        out_specs=whole((VIEWS, 2 * ROWS, 2 * LANE)),
-        in_specs=[whole(field.shape)],
-        compiler_params=pltpu.CompilerParams(vmem_limit_bytes=VMEM_LIMIT),
+        out_shape=jax.ShapeDtypeStruct(shape, F32),
+        in_specs=[ANYWHERE],
+        out_specs=ANYWHERE,
+        scratch_shapes=[
+            pltpu.VMEM(field.shape, F32),
+            pltpu.VMEM(shape, F32),
+            pltpu.SemaphoreType.DMA((2,)),
+        ],
+        compiler_params=pltpu.CompilerParams(vmem_limit_bytes=SMALL_LIMIT),
         name="pack_field",
     )(field)
 
@@ -194,7 +266,7 @@
     above = tap_index(rows_of(shape) - lanes_of(shape) + RADIUS - ROWS)
     for view in range(VIEWS):
         for term in range(RANK):
-            taps = received[view, 6 + term : 7 + term, LANE:]
+            taps = received[view, 6 + term : 7 + term, :]
             band = halves(look_up(jnp.broadcast_to(taps, square.shape), square))
             lower = halves(look_up(jnp.broadcast_to(taps, below.shape), below))
             upper = halves(look_up(jnp.broadcast_to(taps, above.shape), above))
@@ -205,7 +277,7 @@
                 target[view, term, LANE - ROWS : LANE, LANE:] = upper[place]
 
 
-def build_row_bands(view, first_row, stash, rows_lane, own_dst, high, low, turned_high, turned_low):
+def build_row_bands(view, first_row, stash, rows_lane, high, low):
     taps_rows = [stash[3 + term : 4 + term, :] for term in range(RANK)]
     depth_rows = [stash[term : term + 1, :] for term in range(RANK)]
     mix_row = stash[9:10, :]
@@ -235,6 +307,12 @@
                 columns = slice(part * LANE, (part + 1) * LANE)
                 high[view, start : start + 4 * ROWS, columns] = band_high
                 low[view, start : start + 4 * ROWS, columns] = band_low
+
+def build_turned_bands(view, first_row, stash, own_dst, high, low):
+    taps_rows = [stash[3 + term : 4 + term, :] for term in range(RANK)]
+    depth_rows = [stash[term : term + 1, :] for term in range(RANK)]
+    mix_row = stash[9:10, :]
+    centre = TAP_LANE + RADIUS
     shape = (ROWS, LANE)
     lane = lanes_of(shape)
     spread = own_dst.astype(jnp.int32) - ROW_MARK - first_row - lane % (4 * ROWS) + RADIUS
@@ -251,25 +329,11 @@
             scaled = band * jnp.where(upper, from_first, from_second)
             band_high, band_low = halves(scaled)
             start = (term * 2 + plane) * ROWS
-            turned_high[view, start : start + ROWS, :] = band_high
-            turned_low[view, start : start + ROWS, :] = band_low
-
-
-def start_all(copies):
-    for copy in copies:
-        copy.start()
-    return copies
-
-
-def wait_all(copies):
-    for copy in copies:
-        copy.wait()
-
-
-AHEAD = 1
-
-
-def iteration_kernel(first, *refs):
+            high[view, start : start + ROWS, :] = band_high
+            low[view, start : start + ROWS, :] = band_low
+
+
+def iteration_kernel(mode, *refs):
     refs = list(refs)
 
     def take(count):
@@ -277,13 +341,24 @@
         del refs[:count]
         return taken
 
+    forward = mode != "adjoint"
+    backward = mode != "forward"
     received_in, field_in = take(2)
-    moves_in = None if first else take(1)[0]
-    measured_in = take(5)
-    tiles_in, out = take(2)
-    received, field, moves, measured, tiles = take(5)
-    col_high, col_low, row_high, row_low, turned_high, turned_low = take(6)
-    x_high, x_low, result_ref, rows_lane, sems = take(5)
+    moves_in = take(1)[0] if mode == "both" else None
+    blurred_in = take(1)[0] if mode == "adjoint" else None
+    if backward:
+        sides = take(4)
+        sides.insert(2, received_in.at[:, :, pl.ds(0, SEEN)])
+        (tiles_in,) = take(1)
+    (out,) = take(1)
+    received, field, moves, col_high, col_low = take(5)
+    if forward:
+        row_high, row_low, x_high, x_low, rows_lane = take(5)
+    if backward:
+        turned_high, turned_low, measured, tiles, result_ref = take(5)
+    if mode != "both":
+        (blurred_ref,) = take(1)
+    (sems,) = take(1)
 
     strip = lax.axis_index("view")
     block = lax.axis_index("blk")
@@ -295,13 +370,16 @@
         number += 1
         return pltpu.make_async_copy(source, target, sems.at[number - 1])
 
-    for_taps = start_all([copy(received_in, received)])
+    for_taps = start_all([copy(received_in.at[:, :, pl.ds(SEEN, LANE)], received)])
     others = [copy(field_in, field)]
-    if not first:
-        others.append(copy(moves_in.at[:, :, pl.ds(0, LANE)], moves))
-    for place, source in enumerate(measured_in):
-        others.append(copy(source, measured.at[place]))
-    others.append(copy(tiles_in.at[:, :, pl.ds(first_column, LANE)], tiles))
+    if mode == "both":
+        others.append(copy(moves_in.at[:, pl.ds(0, 2)], moves))
+    if mode == "adjoint":
+        others.append(copy(blurred_in, blurred_ref))
+    if backward:
+        for place, source in enumerate(sides):
+            others.append(copy(source, measured.at[place]))
+        others.append(copy(tiles_in.at[:, :, pl.ds(first_column, LANE)], tiles))
     start_all(others)
     wait_all(for_taps)
     build_column_bands(received, col_high, col_low)
@@ -318,26 +396,33 @@
     wide_column = wide + strip * LANE - HALF
     kept = (wide >= Q_FIRST) & (wide <= Q_LAST) & (wide_column >= 0) & (wide_column < columns)
 
-    if first:
-        moves[...] = field[:, :, :LANE]
-    rows_lane[...] = jnp.transpose(moves[...].reshape(VIEWS * 2 * ROWS, LANE))
-    x_high[:, (OWN + 1) * 2 * ROWS :, :] = jnp.zeros((VIEWS, 2 * ROWS, 2 * LANE), BF16)
-    x_low[:, (OWN + 1) * 2 * ROWS :, :] = jnp.zeros((VIEWS, 2 * ROWS, 2 * LANE), BF16)
+    if mode != "both":
+        moves[...] = field[:, 0:2]
+    if forward:
+        rows_lane[...] = jnp.transpose(moves[...].reshape(VIEWS * 2 * ROWS, LANE))
+        unused = slice((OWN + 1) * 2 * ROWS, VIEWS * 2 * ROWS)
+        x_high[:, unused, :] = jnp.zeros((VIEWS, 2 * ROWS, 2 * LANE), BF16)
+        x_low[:, unused, :] = jnp.zeros((VIEWS, 2 * ROWS, 2 * LANE), BF16)
 
     def prepare(view):
-        own_dst = pick_lane(moves[OWN], view)
+        own_dst = pick_lane(moves[OWN].reshape(2 * ROWS, LANE), view)
         last = jnp.max(own_dst) - ROW_MARK
         phase = (last >= ((block + 1) * ROWS).astype(F32)).astype(jnp.int32)
-        build_row_bands(
-            view, (block - 2 + phase) * ROWS, received[view, :, LANE:], rows_lane,
-            own_dst[:ROWS], row_high, row_low, turned_high, turned_low,
-        )
+        first_row = (block - 2 + phase) * ROWS
+        shift = pick_lane(moves[OWN].reshape(2 * ROWS, LANE), VIEWS + view).astype(jnp.int32)
+        if backward:
+            build_turned_bands(
+                view, first_row, received[view], own_dst[:ROWS], turned_high, turned_low
+            )
+        if not forward:
+            return phase, shift
+        build_row_bands(view, first_row, received[view], rows_lane, row_high, row_low)
         for slot in range(OWN + 1):
-            shift = pick_lane(moves[slot], VIEWS + view).astype(jnp.int32)
-            where = lane + shift
+            step = pick_lane(moves[slot].reshape(2 * ROWS, LANE), VIEWS + view)
+            where = lane + step.astype(jnp.int32)
             index = where & (LANE - 1)
-            left = look_up(field[slot, :, :LANE], index)
-            right = look_up(field[slot, :, LANE:], index)
+            left = look_up(field[slot, 0:2].reshape(2 * ROWS, LANE), index)
+            right = look_up(field[slot, 2:4].reshape(2 * ROWS, LANE), index)
             moved = (jnp.where(where < LANE, left, right), jnp.where(where < 0, left, right))
             for part in range(2):
                 high, low = halves(jnp.where(inside[part], moved[part], 0.0))
@@ -346,7 +431,7 @@
                 x_low[view, rows, part * LANE : (part + 1) * LANE] = low
         return phase, shift
 
-    def finish(view, phase, shift):
+    def blur(view):
         xh, xl = x_high[view], x_low[view]
         layers = triple(row_high[view], row_low[view], xh, xl, dot)
         blurred = None
@@ -355,18 +440,31 @@
             high, low = halves(layers[term * height : (term + 1) * height])
             part = triple(high, low, col_high[view, term], col_low[view, term], dot)
             blurred = part if blurred is None else blurred + part
-
-        quotients = []
-        for plane in range(2):
-            for place in range(4):
-                rows = slice(plane * ROWS, (plane + 1) * ROWS)
-                seen = jnp.where(
-                    phase == 1, measured[place + 1, view, rows], measured[place, view, rows]
+        return blurred
+
+    def finish(view, blurred, phase, shift):
+        quotients = [None] * 8
+        lower = lanes_of((ROWS, LANE)) < HALF
+        for place in range(4):
+            seen = [
+                jnp.where(
+                    phase == 1,
+                    measured[place + 1, view, :, tile * LANE : (tile + 1) * LANE],
+                    measured[place, view, :, tile * LANE : (tile + 1) * LANE],
                 )
+                for tile in range(3)
+            ]
+            edges = (seen[2], pltpu.roll(seen[2], HALF, 1))
+            row_block = block - 2 + phase + place
+            fine = kept & (row_block >= 0) & (row_block < VIEWS * 8)
+            for plane in range(2):
+                middle = seen[plane]
+                left = jnp.where(lower, edges[plane], middle)
+                right = jnp.where(lower, middle, edges[1 - plane])
+                both = jnp.concatenate([left, right], axis=1)
                 start = (plane * 4 + place) * ROWS
-                row_block = block - 2 + phase + place
-                fine = kept & (row_block >= 0) & (row_block < VIEWS * 8)
-                quotients.append(jnp.where(fine, seen / blurred[start : start + ROWS], 0.0))
+                ratio = both / blurred[start : start + ROWS]
+                quotients[plane * 4 + place] = jnp.where(fine, ratio, 0.0)
         quotient = jnp.concatenate(quotients, axis=0)
         high, low = halves(quotient)
         layers = triple(turned_high[view], turned_low[view], high, low, dot)
@@ -388,65 +486,82 @@
             adjoint = part if adjoint is None else adjoint + part
         source = column + HALF + shift
         returned = jnp.where((source >= 0) & (source < columns), adjoint, 0.0)
-        chosen = pick_lane(received[view, :, :LANE], TILE_LANE)
-        weight = jnp.zeros((2 * ROWS, LANE), F32)
+        chosen = pick_lane(received[view], TILE_LANE)
+        weight = jnp.zeros((ROWS, LANE), F32)
         for tile in range(tiles.shape[0]):
-            tall = jnp.concatenate([tiles[tile]] * 4, axis=0)
+            tall = jnp.concatenate([tiles[tile]] * 2, axis=0)
             weight = jnp.where(chosen == tile, tall, weight)
+        weight = jnp.concatenate([weight, weight], axis=0)
         return weight * returned, weight
 
 
     total = jnp.zeros((2 * ROWS, LANE), F32)
     weight_total = jnp.zeros((2 * ROWS, LANE), F32)
-    waiting = [prepare(view) for view in range(AHEAD)]
     for view in range(VIEWS):
-        if view + AHEAD < VIEWS:
-            waiting.append(prepare(view + AHEAD))
-        more, weight = finish(view, *waiting[view])
+        phase, shift = prepare(view)
+        blurred = blur(view) if forward else blurred_ref[view]
+        if not backward:
+            blurred_ref[view] = blurred
+            continue
+        more, weight = finish(view, blurred, phase, shift)
         total = total + more
         weight_total = weight_total + weight
 
-    lower = pltpu.roll(field[OWN, :, :LANE], HALF, 1)
-    upper = pltpu.roll(field[OWN, :, LANE:], HALF, 1)
+    if not backward:
+        wait_all(start_all([copy(blurred_ref, out)]))
+        return
+    lower = pltpu.roll(field[OWN, 0:2].reshape(2 * ROWS, LANE), HALF, 1)
+    upper = pltpu.roll(field[OWN, 2:4].reshape(2 * ROWS, LANE), HALF, 1)
     own = jnp.where(lane < HALF, lower, upper)
     result_ref[...] = own * total / weight_total
     wait_all(start_all([copy(result_ref, out.at[place]) for place in range(VIEWS)]))
 
 
-def iteration(field, moves, received, neighbours, weight_tiles):
+def iteration(mode, operands, weight_tiles=None):
     rows = 2 * ROWS
-    window = (VIEWS, rows, 2 * LANE)
+    strips = (VIEWS, rows, LANE)
+    blurred = (VIEWS, 8 * ROWS, 2 * LANE)
     col_shape = (VIEWS, RANK, 2 * LANE, 2 * LANE)
     row_shape = (VIEWS, RANK * 8 * ROWS, 2 * LANE)
     turned_shape = (VIEWS, RANK * 2 * ROWS, LANE)
-    operands = [received, field, *([] if moves is None else [moves]), *neighbours, weight_tiles]
     scratch = [
-        pltpu.VMEM(window, F32),
-        pltpu.VMEM(window, F32),
-        pltpu.VMEM((VIEWS, rows, LANE), F32),
-        pltpu.VMEM((5,) + window, F32),
-        pltpu.VMEM(weight_tiles.shape[:2] + (LANE,), F32),
+        pltpu.VMEM((VIEWS, ROWS, LANE), F32),
+        pltpu.VMEM((VIEWS, 4, ROWS, LANE), F32),
+        pltpu.VMEM((VIEWS, 2, ROWS, LANE), F32),
         pltpu.VMEM(col_shape, BF16),
         pltpu.VMEM(col_shape, BF16),
-        pltpu.VMEM(row_shape, BF16),
-        pltpu.VMEM(row_shape, BF16),
-        pltpu.VMEM(turned_shape, BF16),
-        pltpu.VMEM(turned_shape, BF16),
-        pltpu.VMEM((VIEWS, 2 * LANE, 2 * LANE), BF16),
-        pltpu.VMEM((VIEWS, 2 * LANE, 2 * LANE), BF16),
-        pltpu.VMEM((rows, LANE), F32),
-        pltpu.VMEM((LANE, 2 * LANE), F32),
-        pltpu.SemaphoreType.DMA((24,)),
     ]
-    anywhere = pl.BlockSpec(memory_space=pl.ANY)
+    if mode != "adjoint":
+        scratch += [
+            pltpu.VMEM(row_shape, BF16),
+            pltpu.VMEM(row_shape, BF16),
+            pltpu.VMEM((VIEWS, 2 * LANE, 2 * LANE), BF16),
+            pltpu.VMEM((VIEWS, 2 * LANE, 2 * LANE), BF16),
+            pltpu.VMEM((LANE, 2 * LANE), F32),
+        ]
+    if mode != "forward":
+        operands = [*operands, weight_tiles]
+        scratch += [
+            pltpu.VMEM(turned_shape, BF16),
+            pltpu.VMEM(turned_shape, BF16),
+            pltpu.VMEM((5, VIEWS, ROWS, SEEN), F32),
+            pltpu.VMEM(weight_tiles.shape[:2] + (LANE,), F32),
+            pltpu.VMEM((rows, LANE), F32),
+        ]
+    if mode != "both":
+        scratch.append(pltpu.VMEM(blurred, F32))
+    scratch.append(pltpu.SemaphoreType.DMA((24,)))
     return pl.pallas_call(
-        lambda *refs: iteration_kernel(moves is None, *refs),
-        out_shape=jax.ShapeDtypeStruct((VIEWS, rows, LANE), F32),
-        in_specs=[anywhere] * len(operands),
-        out_specs=anywhere,
+        lambda *refs: iteration_kernel(mode, *refs),
+        out_shape=jax.ShapeDtypeStruct(blurred if mode == "forward" else strips, F32),
+        in_specs=[ANYWHERE] * len(operands),
+        out_specs=ANYWHERE,
         scratch_shapes=scratch,
         compiler_params=pltpu.CompilerParams(vmem_limit_bytes=VMEM_LIMIT),
-        name="iteration_first" if moves is None else "iteration_next",
+        cost_estimate=pl.CostEstimate(
+            flops=8_000_000_000, bytes_accessed=1_000_000, transcendentals=0
+        ),
+        name=f"iteration_{mode}",
     )(*operands)
 
 
@@ -489,18 +604,20 @@
     received = over_views(
         pack_measured(measured, dst_row, back_shift, tile_index, psf_z, psf_y, psf_x, psf_mix)
     )
-    moves, later = lax.optimization_barrier((registration(received), received))
-    moves = step_by_view(moves)
-    packed = pack_estimate(stepped, moves)
-    far = [from_block(later, offset) for offset in (-2, 2)]
-    near = [from_block(later, offset) for offset in (-1, 1)]
-    neighbours = [far[0], near[0], received, near[1], far[1]]
+    moves = jnp.sum(received[:, :, SEEN:], axis=0)
+    moves, seen = lax.optimization_barrier((moves, received[:, :, :SEEN]))
+    packed = pack_estimate(stepped, step_by_view(moves))
+    far = hand_on([from_block(seen, offset) for offset in (-2, 2)])
+    packed, seen = lax.optimization_barrier((packed, seen))
+    near = [from_block(seen, offset) for offset in (-1, 1)]
+    sides = [far[0], near[0], near[1], far[1]]
     field = over_views(packed)
     moves = field
-    strips = iteration(field, None, received, neighbours, weight_tiles)
+    blurred = iteration("forward", [received, field])
+    strips = iteration("adjoint", [received, field, blurred, *sides], weight_tiles)
     for _ in range(ITERS - 1):
         field = over_views(pack_field(step_by_view(over_views(strips))))
-        strips = iteration(field, moves, received, neighbours, weight_tiles)
+        strips = iteration("both", [received, field, moves, *sides], weight_tiles)
     strips = over_views(strips).reshape(VIEWS, planes, row_count, LANE)
     return jnp.transpose(strips, (1, 2, 0, 3)).reshape(planes, row_count, col_count)
 

time: 119 us -> 112 us (0.941)
  the two profiles are of different devices: /device:TPU:264 before, /device:TPU:256 now
where the time goes in v3:
time: 112 us
  starting transfers between devices  36.1 us (32%)
  blocking collectives  31.3 us (28%)
  Pallas kernels  27.7 us (25%)
  waiting for transfers between devices  15.8 us (14%)
    all_to_all x3, blocking collectives, over_views(): return lax.all_to_all(values, 'view', 0, 0)  31.3 us
    pallas_call x3, Pallas kernels, iteration(): pl.pallas_call(lambda *refs: iteration_kernel(mode, *refs), out_shape=jax...  24.3 us
    ppermute x4, starting transfers between devices, from_block(): return lax.ppermute(values, 'blk', route)  16 us
    all_to_all x2, starting transfers between devices, over_views(): return lax.all_to_all(values, 'view', 0, 0)  11.2 us
    ppermute x3, starting transfers between devices, step_by_view(): return lax.ppermute(values, ('view', 'blk'), route)  8.88 us
    ppermute x3, waiting for transfers between devices, step_by_view(): return lax.ppermute(values, ('view', 'blk'), route)  8.26 us
    all_to_all x2, waiting for transfers between devices, over_views(): return lax.all_to_all(values, 'view', 0, 0)  4.04 us
    ppermute x4, waiting for transfers between devices, from_block(): return lax.ppermute(values, 'blk', route)  3.54 us
  transfers between devices with their start and end apart: 9, of which 3 were waited for; matrix products, arithmetic and copies ran while one was open for 0% of the time, Pallas kernels for 7%

profile of v3, /device:TPU:256, one launch (start us, length us, event | category | flops | bytes accessed | tf_op | source)
XLA Modules:
  0.0 111.8 jit_solution(7694838649027322764)
XLA Ops:
  0.0 2.1 %pack_measured.1 = f32[8,16,512]{2,1,0:T(8,128)} custom-call(f32[1,2,16,1024]{3,2,1,0:T(8,128)} %measured.1, s32[1,16]{1,0:T(1,128)} %dst_row.1, s32[1,16]{1,0:T(1,128)} %back_shift.1, s32[1,2]{1,0:T(1,128)} %tile_index.1, f32[3,1,31]{2,1,0:T(1,128)} %bitcast.11, f32[3,1,31]{2,1,0:T(1,128)} %bitcast.12, f32[3,1,31]{2,1,0:T(1,128)} %bitcast.13, f32[1,3]{1,0:T(1,128)} %psf_mix.1), custom_call_target="tpu_custom_call" | custom-call | tf_op jit(solution)/shard_map/pack_measured/pallas_call | solution.py:151
  2.2 0.0 copy-start.1
  2.2 4.4 %all-to-all-start = ((f32[8,16,512]{2,1,0:T(8,128)}), f32[8,16,512]{2,1,0:T(8,128)S(1)}, u32[]{:S(2)}, u32[]{:S(2)}) async-start(f32[8,16,512]{2,1,0:T(8,128)} %pack_measured.1), calls=%async_computation | async-start | bytes 524288 | tf_op jit(solution)/shard_map/all_to_all | solution.py:585
  6.6 0.0 copy-done.1
  6.6 3.5 %collective-permute-start = (f32[2,16,1024]{2,1,0:T(8,128)S(1)}, f32[2,16,1024]{2,1,0:T(8,128)S(1)}, u32[]{:S(2)}, u32[]{:S(2)}) collective-permute-start(f32[2,16,1024]{2,1,0:T(8,128)S(1)} %copy-done.1), channel_id=1, source_target_pairs={{0,1},{1,2},{2,3},{3,4},{4,5},{5,6},{6,7},{7,8},{8,9},{9,10},{10,1... | collective-permute-start | bytes 393224 | tf_op jit(solution)/shard_map/ppermute | solution.py:575
  10.1 4.0 %all-to-all-done.refs_0_ = f32[8,16,512]{2,1,0:T(8,128)S(1)} async-done(((f32[8,16,512]{2,1,0:T(8,128)}), f32[8,16,512]{2,1,0:T(8,128)S(1)}, u32[]{:S(2)}, u32[]{:S(2)}) %all-to-all-start) | async-done | bytes 262176 | tf_op jit(solution)/shard_map/all_to_all | solution.py:585
  14.2 3.5 %collective-permute-start.1 = (f32[16,128]{1,0:T(8,128)S(1)}, f32[16,128]{1,0:T(8,128)S(1)}, u32[]{:S(2)}, u32[]{:S(2)}) collective-permute-start(f32[16,128]{1,0:T(8,128)S(1)} %slice_reduce_fusion), channel_id=1, source_target_pairs={{0,1},{1,2},{2,3},{3,4},{4,5},{5,6},{6,7},{7,8},{8,9},{9,10},{10,1... | collective-permute-start | bytes 24584 | tf_op jit(solution)/shard_map/ppermute | solution.py:575
  17.7 4.4 %collective-permute-start.3 = (f32[8,16,384]{2,1,0:T(8,128)S(1)}, f32[8,16,384]{2,1,0:T(8,128)S(1)}, u32[]{:S(2)}, u32[]{:S(2)}) collective-permute-start(f32[8,16,384]{2,1,0:T(8,128)S(1)} %slice.9), channel_id=1, source_target_pairs={{2,0},{3,1},{4,2},{5,3},{6,4},{7,5},{8,6},{9,7},{10,8},{11,9},{12,... | collective-permute-start | bytes 589832 | tf_op jit(solution)/shard_map/ppermute | solution.py:581
  22.0 2.4 %collective-permute-start.2 = (f32[8,16,384]{2,1,0:T(8,128)S(1)}, f32[8,16,384]{2,1,0:T(8,128)S(1)}, u32[]{:S(2)}, u32[]{:S(2)}) collective-permute-start(f32[8,16,384]{2,1,0:T(8,128)S(1)} %slice.9), channel_id=1, source_target_pairs={{0,2},{1,3},{2,4},{3,5},{4,6},{5,7},{6,8},{7,9},{8,10},{9,11},{10,... | collective-permute-start | bytes 589832 | tf_op jit(solution)/shard_map/ppermute | solution.py:581
  24.4 0.0 collective-permute-done.field_in
  24.5 0.0 collective-permute-done.1.moves_in
  24.5 1.0 pack_estimate.1
  25.5 6.8 %all-to-all-start.1 = ((f32[8,4,16,128]{3,2,1,0:T(8,128)}), f32[8,4,16,128]{3,2,1,0:T(8,128)S(1)}, u32[]{:S(2)}, u32[]{:S(2)}) async-start(f32[8,4,16,128]{3,2,1,0:T(8,128)} %pack_estimate.1), calls=%async_computation.1 | async-start | bytes 524288 | tf_op jit(solution)/shard_map/all_to_all | solution.py:585
  32.3 7.3 %collective-permute-start.5 = (f32[8,16,384]{2,1,0:T(8,128)S(1)}, f32[8,16,384]{2,1,0:T(8,128)S(1)}, u32[]{:S(2)}, u32[]{:S(2)}) collective-permute-start(f32[8,16,384]{2,1,0:T(8,128)S(1)} %slice.9), channel_id=1, source_target_pairs={{1,0},{2,1},{3,2},{4,3},{5,4},{6,5},{7,6},{8,7},{9,8},{10,9},{11,1... | collective-permute-start | bytes 589832 | tf_op jit(solution)/shard_map/ppermute | solution.py:581
  39.6 1.9 %collective-permute-start.4 = (f32[8,16,384]{2,1,0:T(8,128)S(1)}, f32[8,16,384]{2,1,0:T(8,128)S(1)}, u32[]{:S(2)}, u32[]{:S(2)}) collective-permute-start(f32[8,16,384]{2,1,0:T(8,128)S(1)} %slice.9), channel_id=1, source_target_pairs={{0,1},{1,2},{2,3},{3,4},{4,5},{5,6},{6,7},{7,8},{8,9},{9,10},{10,1... | collective-permute-start | bytes 589832 | tf_op jit(solution)/shard_map/ppermute | solution.py:581
  41.5 0.0 collective-permute-done.3.refs_1_
  41.6 0.0 collective-permute-done.2.refs_0_
  41.6 0.0 copy-start
  41.6 0.0 all-to-all-done.1.refs_1_.refs_2_
  41.6 6.7 %iteration_forward.1.refs_2_ = f32[8,128,256]{2,1,0:T(8,128)S(1)} custom-call(f32[8,16,512]{2,1,0:T(8,128)S(1)} %all-to-all-done.refs_0_, f32[8,4,16,128]{3,2,1,0:T(8,128)S(1)} %all-to-all-done.1.refs_1_.refs_2_), custom_call_target="tpu_custom_call" | custom-call | flops 8000000000 | bytes 1000000 | tf_op jit(solution)/shard_map/iteration_forward/pallas_call | solution.py:554
  48.3 0.0 collective-permute-done.5.refs_5_
  48.3 3.5 %collective-permute-done.4.refs_4_ = f32[8,16,384]{2,1,0:T(8,128)S(1)} collective-permute-done((f32[8,16,384]{2,1,0:T(8,128)S(1)}, f32[8,16,384]{2,1,0:T(8,128)S(1)}, u32[]{:S(2)}, u32[]{:S(2)}) %collective-permute-start.4) | collective-permute-done | bytes 196640 | tf_op jit(solution)/shard_map/ppermute | solution.py:581
  51.9 0.0 copy-done
  51.9 6.1 %iteration_adjoint.1 = f32[8,32,128]{2,1,0:T(8,128)S(1)} custom-call(f32[8,16,512]{2,1,0:T(8,128)S(1)} %all-to-all-done.refs_0_, f32[8,4,16,128]{3,2,1,0:T(8,128)S(1)} %all-to-all-done.1.refs_1_.refs_2_, f32[8,128,256]{2,1,0:T(8,128)S(1)} %iteration_forward.1.refs_2_, f32[8,16,384]{2,1,0:T(8,128)S(1)} %get-tuple-element.14.refs_3_, ...), custom_call_target="tpu_custom_call" | custom-call | flops 8000000000 | bytes 1000000 | tf_op jit(solution)/shard_map/iteration_adjoint/pallas_call | solution.py:554
  58.0 10.4 %all_to_all.25 = f32[8,32,128]{2,1,0:T(8,128)S(1)} all-to-all(f32[8,32,128]{2,1,0:T(8,128)S(1)} %iteration_adjoint.1), channel_id=1, replica_groups=mesh['view'=8,'blk'=64] {'view'}, dimensions={0} | all-to-all | bytes 262144 | tf_op jit(solution)/shard_map/all_to_all | solution.py:585
  68.4 1.9 %collective-permute-start.6 = (f32[8,32,128]{2,1,0:T(8,128)S(1)}, f32[8,32,128]{2,1,0:T(8,128)S(1)}, u32[]{:S(2)}, u32[]{:S(2)}) collective-permute-start(f32[8,32,128]{2,1,0:T(8,128)S(1)} %all_to_all.25), channel_id=1, source_target_pairs={{0,1},{1,2},{2,3},{3,4},{4,5},{5,6},{6,7},{7,8},{8,9},{9,10},{10,1... | collective-permute-start | bytes 393224 | tf_op jit(solution)/shard_map/ppermute | solution.py:575
  70.3 8.3 %collective-permute-done.6.field_in = f32[8,32,128]{2,1,0:T(8,128)S(1)} collective-permute-done((f32[8,32,128]{2,1,0:T(8,128)S(1)}, f32[8,32,128]{2,1,0:T(8,128)S(1)}, u32[]{:S(2)}, u32[]{:S(2)}) %collective-permute-start.6) | collective-permute-done | bytes 131104 | tf_op jit(solution)/shard_map/ppermute | solution.py:575
  78.5 0.3 pack_field.1
  78.8 12.4 %all_to_all.26.refs_1_ = f32[8,4,16,128]{3,2,1,0:T(8,128)S(1)} all-to-all(f32[8,4,16,128]{3,2,1,0:T(8,128)S(1)} %pack_field.1), channel_id=1, replica_groups=mesh['view'=8,'blk'=64] {'view'}, dimensions={0} | all-to-all | bytes 524288 | tf_op jit(solution)/shard_map/all_to_all | solution.py:585
  91.2 11.5 %iteration_both.1 = f32[8,32,128]{2,1,0:T(8,128)S(1)} custom-call(f32[8,16,512]{2,1,0:T(8,128)S(1)} %all-to-all-done.refs_0_, f32[8,4,16,128]{3,2,1,0:T(8,128)S(1)} %all_to_all.26.refs_1_, f32[8,4,16,128]{3,2,1,0:T(8,128)S(1)} %all-to-all-done.1.refs_1_.refs_2_, f32[8,16,384]{2,1,0:T(8,128)S(1)} %get-tuple-element.14.refs_3_, ...), custom_call_target="tpu_custom_call" | custom-call | flops 8000000000 | bytes 1000000 | tf_op jit(solution)/shard_map/iteration_both/pallas_call | solution.py:554
  102.7 8.5 %all_to_all.27 = f32[8,32,128]{2,1,0:T(8,128)S(1)} all-to-all(f32[8,32,128]{2,1,0:T(8,128)S(1)} %iteration_both.1), channel_id=1, replica_groups=mesh['view'=8,'blk'=64] {'view'}, dimensions={0} | all-to-all | bytes 262144 | tf_op jit(solution)/shard_map/all_to_all | solution.py:585
  111.2 0.7 copy.16
  (3 shorter events, 0.0 us)
Async XLA Ops:
  2.2 4.5 %copy-start.1 = (f32[2,16,1024]{2,1,0:T(8,128)S(1)}, f32[2,16,1024]{2,1,0:T(8,128)}, u32[]{:S(2)}) copy-start(f32[2,16,1024]{2,1,0:T(8,128)} %param.12) | copy-start | bytes 393220
  2.2 12.0 %all-to-all-start = ((f32[8,16,512]{2,1,0:T(8,128)}), f32[8,16,512]{2,1,0:T(8,128)S(1)}, u32[]{:S(2)}, u32[]{:S(2)}) async-start(f32[8,16,512]{2,1,0:T(8,128)} %pack_measured.1), calls=%async_computation | async-start | bytes 524288 | tf_op jit(solution)/shard_map/all_to_all | solution.py:585
  6.6 17.8 %collective-permute-start = (f32[2,16,1024]{2,1,0:T(8,128)S(1)}, f32[2,16,1024]{2,1,0:T(8,128)S(1)}, u32[]{:S(2)}, u32[]{:S(2)}) collective-permute-start(f32[2,16,1024]{2,1,0:T(8,128)S(1)} %copy-done.1), channel_id=1, source_target_pairs={{0,1},{1,2},{2,3},{3,4},{4,5},{5,6},{6,7},{7,8},{8,9},{9,10},{10,1... | collective-permute-start | bytes 393224 | tf_op jit(solution)/shard_map/ppermute | solution.py:575
  14.2 10.3 %collective-permute-start.1 = (f32[16,128]{1,0:T(8,128)S(1)}, f32[16,128]{1,0:T(8,128)S(1)}, u32[]{:S(2)}, u32[]{:S(2)}) collective-permute-start(f32[16,128]{1,0:T(8,128)S(1)} %slice_reduce_fusion), channel_id=1, source_target_pairs={{0,1},{1,2},{2,3},{3,4},{4,5},{5,6},{6,7},{7,8},{8,9},{9,10},{10,1... | collective-permute-start | bytes 24584 | tf_op jit(solution)/shard_map/ppermute | solution.py:575
  17.7 23.9 %collective-permute-start.3 = (f32[8,16,384]{2,1,0:T(8,128)S(1)}, f32[8,16,384]{2,1,0:T(8,128)S(1)}, u32[]{:S(2)}, u32[]{:S(2)}) collective-permute-start(f32[8,16,384]{2,1,0:T(8,128)S(1)} %slice.9), channel_id=1, source_target_pairs={{2,0},{3,1},{4,2},{5,3},{6,4},{7,5},{8,6},{9,7},{10,8},{11,9},{12,... | collective-permute-start | bytes 589832 | tf_op jit(solution)/shard_map/ppermute | solution.py:581
  22.0 19.5 %collective-permute-start.2 = (f32[8,16,384]{2,1,0:T(8,128)S(1)}, f32[8,16,384]{2,1,0:T(8,128)S(1)}, u32[]{:S(2)}, u32[]{:S(2)}) collective-permute-start(f32[8,16,384]{2,1,0:T(8,128)S(1)} %slice.9), channel_id=1, source_target_pairs={{0,2},{1,3},{2,4},{3,5},{4,6},{5,7},{6,8},{7,9},{8,10},{9,11},{10,... | collective-permute-start | bytes 589832 | tf_op jit(solution)/shard_map/ppermute | solution.py:581
  25.5 16.1 %all-to-all-start.1 = ((f32[8,4,16,128]{3,2,1,0:T(8,128)}), f32[8,4,16,128]{3,2,1,0:T(8,128)S(1)}, u32[]{:S(2)}, u32[]{:S(2)}) async-start(f32[8,4,16,128]{3,2,1,0:T(8,128)} %pack_estimate.1), calls=%async_computation.1 | async-start | bytes 524288 | tf_op jit(solution)/shard_map/all_to_all | solution.py:585
  32.3 16.1 %collective-permute-start.5 = (f32[8,16,384]{2,1,0:T(8,128)S(1)}, f32[8,16,384]{2,1,0:T(8,128)S(1)}, u32[]{:S(2)}, u32[]{:S(2)}) collective-permute-start(f32[8,16,384]{2,1,0:T(8,128)S(1)} %slice.9), channel_id=1, source_target_pairs={{1,0},{2,1},{3,2},{4,3},{5,4},{6,5},{7,6},{8,7},{9,8},{10,9},{11,1... | collective-permute-start | bytes 589832 | tf_op jit(solution)/shard_map/ppermute | solution.py:581
  39.6 12.2 %collective-permute-start.4 = (f32[8,16,384]{2,1,0:T(8,128)S(1)}, f32[8,16,384]{2,1,0:T(8,128)S(1)}, u32[]{:S(2)}, u32[]{:S(2)}) collective-permute-start(f32[8,16,384]{2,1,0:T(8,128)S(1)} %slice.9), channel_id=1, source_target_pairs={{0,1},{1,2},{2,3},{3,4},{4,5},{5,6},{6,7},{7,8},{8,9},{9,10},{10,1... | collective-permute-start | bytes 589832 | tf_op jit(solution)/shard_map/ppermute | solution.py:581
  41.6 10.3 %copy-start = (f32[8,8,1024]{2,1,0:T(8,128)S(1)}, f32[8,8,1024]{2,1,0:T(8,128)}, u32[]{:S(2)}) copy-start(f32[8,8,1024]{2,1,0:T(8,128)} %refs_7_.3) | copy-start | bytes 786436
  68.4 10.2 %collective-permute-start.6 = (f32[8,32,128]{2,1,0:T(8,128)S(1)}, f32[8,32,128]{2,1,0:T(8,128)S(1)}, u32[]{:S(2)}, u32[]{:S(2)}) collective-permute-start(f32[8,32,128]{2,1,0:T(8,128)S(1)} %all_to_all.25), channel_id=1, source_target_pairs={{0,1},{1,2},{2,3},{3,4},{4,5},{5,6},{6,7},{7,8},{8,9},{9,10},{10,1... | collective-permute-start | bytes 393224 | tf_op jit(solution)/shard_map/ppermute | solution.py:575

commit v4 on v3

--- a/solution.py
+++ b/solution.py
@@ -142,6 +142,7 @@
 
 
 ANYWHERE = pl.BlockSpec(memory_space=pl.ANY)
+IN_VMEM = pl.BlockSpec(memory_space=pltpu.VMEM)
 
 
 def pack_measured(measured, dst_row, back_shift, tile_index, psf_z, psf_y, psf_x, psf_mix):
@@ -163,13 +164,7 @@
     )(*operands)
 
 
-def pack_estimate_kernel(field_in, moves_in, out_ref, field, moves, out, sems):
-    fetches = [
-        pltpu.make_async_copy(field_in, field, sems.at[0]),
-        pltpu.make_async_copy(moves_in, moves, sems.at[1]),
-    ]
-    start_all(fetches)
-    wait_all(fetches)
+def pack_estimate_kernel(field, moves, out):
     lane = lanes_of((ROWS, LANE))
     for plane in range(2):
         strips = [field[plane, :, place * LANE : (place + 1) * LANE] for place in range(VIEWS)]
@@ -177,22 +172,14 @@
         for place in range(VIEWS):
             out[place, plane] = jnp.where(lane < 2 * VIEWS, moves[...], tiles[place])
             out[place, 2 + plane] = tiles[place + 1]
-    wait_all(start_all([pltpu.make_async_copy(out, out_ref, sems.at[2])]))
 
 
 def pack_estimate(field, moves):
-    shape = (VIEWS, 4, ROWS, LANE)
     return pl.pallas_call(
         pack_estimate_kernel,
-        out_shape=jax.ShapeDtypeStruct(shape, F32),
-        in_specs=[ANYWHERE] * 2,
-        out_specs=ANYWHERE,
-        scratch_shapes=[
-            pltpu.VMEM(field.shape, F32),
-            pltpu.VMEM(moves.shape, F32),
-            pltpu.VMEM(shape, F32),
-            pltpu.SemaphoreType.DMA((3,)),
-        ],
+        out_shape=jax.ShapeDtypeStruct((VIEWS, 4, ROWS, LANE), F32),
+        in_specs=[IN_VMEM] * 2,
+        out_specs=IN_VMEM,
         cost_estimate=pl.CostEstimate(
             flops=40_000_000_000, bytes_accessed=100_000_000, transcendentals=0
         ),
@@ -221,31 +208,19 @@
     )(*arrays)
 
 
-def pack_field_kernel(field_in, out_ref, field, out, sems):
-    fetch = pltpu.make_async_copy(field_in, field, sems.at[0])
-    fetch.start()
-    fetch.wait()
+def pack_field_kernel(field, out):
     tiles = windows_of([field[place] for place in range(VIEWS)])
     for place in range(VIEWS):
         out[place, 0:2] = tiles[place].reshape(2, ROWS, LANE)
         out[place, 2:4] = tiles[place + 1].reshape(2, ROWS, LANE)
-    send = pltpu.make_async_copy(out, out_ref, sems.at[1])
-    send.start()
-    send.wait()
 
 
 def pack_field(field):
-    shape = (VIEWS, 4, ROWS, LANE)
     return pl.pallas_call(
         pack_field_kernel,
-        out_shape=jax.ShapeDtypeStruct(shape, F32),
-        in_specs=[ANYWHERE],
-        out_specs=ANYWHERE,
-        scratch_shapes=[
-            pltpu.VMEM(field.shape, F32),
-            pltpu.VMEM(shape, F32),
-            pltpu.SemaphoreType.DMA((2,)),
-        ],
+        out_shape=jax.ShapeDtypeStruct((VIEWS, 4, ROWS, LANE), F32),
+        in_specs=[IN_VMEM],
+        out_specs=IN_VMEM,
         compiler_params=pltpu.CompilerParams(vmem_limit_bytes=SMALL_LIMIT),
         name="pack_field",
     )(field)
@@ -266,7 +241,7 @@
     above = tap_index(rows_of(shape) - lanes_of(shape) + RADIUS - ROWS)
     for view in range(VIEWS):
         for term in range(RANK):
-            taps = received[view, 6 + term : 7 + term, :]
+            taps = received[view, 6 + term : 7 + term, SEEN:]
             band = halves(look_up(jnp.broadcast_to(taps, square.shape), square))
             lower = halves(look_up(jnp.broadcast_to(taps, below.shape), below))
             upper = halves(look_up(jnp.broadcast_to(taps, above.shape), above))
@@ -343,47 +318,32 @@
 
     forward = mode != "adjoint"
     backward = mode != "forward"
-    received_in, field_in = take(2)
-    moves_in = take(1)[0] if mode == "both" else None
-    blurred_in = take(1)[0] if mode == "adjoint" else None
+    received, field = take(2)
+    moves = take(1)[0] if mode == "both" else field
+    blurred = take(1)[0] if mode == "adjoint" else None
     if backward:
         sides = take(4)
-        sides.insert(2, received_in.at[:, :, pl.ds(0, SEEN)])
-        (tiles_in,) = take(1)
+        sides.insert(2, received)
+        tiles, col_high, col_low = take(3)
+    if mode == "both":
+        row_high, row_low, turned_high, turned_low = take(4)
     (out,) = take(1)
-    received, field, moves, col_high, col_low = take(5)
+    if mode == "forward":
+        col_high, col_low, row_high, row_low = take(4)
+    if mode == "adjoint":
+        turned_high, turned_low = take(2)
     if forward:
-        row_high, row_low, x_high, x_low, rows_lane = take(5)
-    if backward:
-        turned_high, turned_low, measured, tiles, result_ref = take(5)
-    if mode != "both":
-        (blurred_ref,) = take(1)
-    (sems,) = take(1)
+        x_high, x_low, rows_lane = take(3)
 
     strip = lax.axis_index("view")
     block = lax.axis_index("blk")
     first_column = pl.multiple_of(strip * LANE, LANE)
-    number = 0
-
-    def copy(source, target):
-        nonlocal number
-        number += 1
-        return pltpu.make_async_copy(source, target, sems.at[number - 1])
-
-    for_taps = start_all([copy(received_in.at[:, :, pl.ds(SEEN, LANE)], received)])
-    others = [copy(field_in, field)]
-    if mode == "both":
-        others.append(copy(moves_in.at[:, pl.ds(0, 2)], moves))
-    if mode == "adjoint":
-        others.append(copy(blurred_in, blurred_ref))
-    if backward:
-        for place, source in enumerate(sides):
-            others.append(copy(source, measured.at[place]))
-        others.append(copy(tiles_in.at[:, :, pl.ds(first_column, LANE)], tiles))
-    start_all(others)
-    wait_all(for_taps)
-    build_column_bands(received, col_high, col_low)
-    wait_all(others)
+
+    def stash(view):
+        return received[view, :, SEEN:]
+
+    if mode == "forward":
+        build_column_bands(received, col_high, col_low)
 
     lane = lanes_of((2 * ROWS, LANE))
     column = lane + strip * LANE - HALF
@@ -396,29 +356,29 @@
     wide_column = wide + strip * LANE - HALF
     kept = (wide >= Q_FIRST) & (wide <= Q_LAST) & (wide_column >= 0) & (wide_column < columns)
 
-    if mode != "both":
-        moves[...] = field[:, 0:2]
     if forward:
-        rows_lane[...] = jnp.transpose(moves[...].reshape(VIEWS * 2 * ROWS, LANE))
+        if mode == "forward":
+            rows_lane[...] = jnp.transpose(moves[:, 0:2].reshape(VIEWS * 2 * ROWS, LANE))
         unused = slice((OWN + 1) * 2 * ROWS, VIEWS * 2 * ROWS)
         x_high[:, unused, :] = jnp.zeros((VIEWS, 2 * ROWS, 2 * LANE), BF16)
         x_low[:, unused, :] = jnp.zeros((VIEWS, 2 * ROWS, 2 * LANE), BF16)
 
     def prepare(view):
-        own_dst = pick_lane(moves[OWN].reshape(2 * ROWS, LANE), view)
+        own_dst = pick_lane(moves[OWN, 0:2].reshape(2 * ROWS, LANE), view)
         last = jnp.max(own_dst) - ROW_MARK
         phase = (last >= ((block + 1) * ROWS).astype(F32)).astype(jnp.int32)
         first_row = (block - 2 + phase) * ROWS
-        shift = pick_lane(moves[OWN].reshape(2 * ROWS, LANE), VIEWS + view).astype(jnp.int32)
-        if backward:
+        shift = pick_lane(moves[OWN, 0:2].reshape(2 * ROWS, LANE), VIEWS + view).astype(jnp.int32)
+        if mode == "adjoint":
             build_turned_bands(
-                view, first_row, received[view], own_dst[:ROWS], turned_high, turned_low
+                view, first_row, stash(view), own_dst[:ROWS], turned_high, turned_low
             )
         if not forward:
             return phase, shift
-        build_row_bands(view, first_row, received[view], rows_lane, row_high, row_low)
+        if mode == "forward":
+            build_row_bands(view, first_row, stash(view), rows_lane, row_high, row_low)
         for slot in range(OWN + 1):
-            step = pick_lane(moves[slot].reshape(2 * ROWS, LANE), VIEWS + view)
+            step = pick_lane(moves[slot, 0:2].reshape(2 * ROWS, LANE), VIEWS + view)
             where = lane + step.astype(jnp.int32)
             index = where & (LANE - 1)
             left = look_up(field[slot, 0:2].reshape(2 * ROWS, LANE), index)
@@ -449,8 +409,8 @@
             seen = [
                 jnp.where(
                     phase == 1,
-                    measured[place + 1, view, :, tile * LANE : (tile + 1) * LANE],
-                    measured[place, view, :, tile * LANE : (tile + 1) * LANE],
+                    sides[place + 1][view, :, tile * LANE : (tile + 1) * LANE],
+                    sides[place][view, :, tile * LANE : (tile + 1) * LANE],
                 )
                 for tile in range(3)
             ]
@@ -486,10 +446,10 @@
             adjoint = part if adjoint is None else adjoint + part
         source = column + HALF + shift
         returned = jnp.where((source >= 0) & (source < columns), adjoint, 0.0)
-        chosen = pick_lane(received[view], TILE_LANE)
+        chosen = pick_lane(stash(view), TILE_LANE)
         weight = jnp.zeros((ROWS, LANE), F32)
         for tile in range(tiles.shape[0]):
-            tall = jnp.concatenate([tiles[tile]] * 2, axis=0)
+            tall = jnp.concatenate([tiles[tile, :, pl.ds(first_column, LANE)]] * 2, axis=0)
             weight = jnp.where(chosen == tile, tall, weight)
         weight = jnp.concatenate([weight, weight], axis=0)
         return weight * returned, weight
@@ -499,63 +459,47 @@
     weight_total = jnp.zeros((2 * ROWS, LANE), F32)
     for view in range(VIEWS):
         phase, shift = prepare(view)
-        blurred = blur(view) if forward else blurred_ref[view]
+        now = blur(view) if forward else blurred[view]
         if not backward:
-            blurred_ref[view] = blurred
+            out[view] = now
             continue
-        more, weight = finish(view, blurred, phase, shift)
+        more, weight = finish(view, now, phase, shift)
         total = total + more
         weight_total = weight_total + weight
 
     if not backward:
-        wait_all(start_all([copy(blurred_ref, out)]))
         return
     lower = pltpu.roll(field[OWN, 0:2].reshape(2 * ROWS, LANE), HALF, 1)
     upper = pltpu.roll(field[OWN, 2:4].reshape(2 * ROWS, LANE), HALF, 1)
     own = jnp.where(lane < HALF, lower, upper)
-    result_ref[...] = own * total / weight_total
-    wait_all(start_all([copy(result_ref, out.at[place]) for place in range(VIEWS)]))
-
-
-def iteration(mode, operands, weight_tiles=None):
+    result = own * total / weight_total
+    for place in range(VIEWS):
+        out[place] = result
+
+
+def iteration(mode, operands):
     rows = 2 * ROWS
-    strips = (VIEWS, rows, LANE)
-    blurred = (VIEWS, 8 * ROWS, 2 * LANE)
-    col_shape = (VIEWS, RANK, 2 * LANE, 2 * LANE)
-    row_shape = (VIEWS, RANK * 8 * ROWS, 2 * LANE)
-    turned_shape = (VIEWS, RANK * 2 * ROWS, LANE)
-    scratch = [
-        pltpu.VMEM((VIEWS, ROWS, LANE), F32),
-        pltpu.VMEM((VIEWS, 4, ROWS, LANE), F32),
-        pltpu.VMEM((VIEWS, 2, ROWS, LANE), F32),
-        pltpu.VMEM(col_shape, BF16),
-        pltpu.VMEM(col_shape, BF16),
-    ]
+    blurred = jax.ShapeDtypeStruct((VIEWS, 8 * ROWS, 2 * LANE), F32)
+    col_band = jax.ShapeDtypeStruct((VIEWS, RANK, 2 * LANE, 2 * LANE), BF16)
+    row_band = jax.ShapeDtypeStruct((VIEWS, RANK * 8 * ROWS, 2 * LANE), BF16)
+    turned_band = jax.ShapeDtypeStruct((VIEWS, RANK * 2 * ROWS, LANE), BF16)
+    outs = [jax.ShapeDtypeStruct((VIEWS, rows, LANE), F32)]
+    scratch = []
+    if mode == "forward":
+        outs = [blurred, col_band, col_band, row_band, row_band]
+    if mode == "adjoint":
+        outs += [turned_band, turned_band]
     if mode != "adjoint":
-        scratch += [
-            pltpu.VMEM(row_shape, BF16),
-            pltpu.VMEM(row_shape, BF16),
+        scratch = [
             pltpu.VMEM((VIEWS, 2 * LANE, 2 * LANE), BF16),
             pltpu.VMEM((VIEWS, 2 * LANE, 2 * LANE), BF16),
             pltpu.VMEM((LANE, 2 * LANE), F32),
         ]
-    if mode != "forward":
-        operands = [*operands, weight_tiles]
-        scratch += [
-            pltpu.VMEM(turned_shape, BF16),
-            pltpu.VMEM(turned_shape, BF16),
-            pltpu.VMEM((5, VIEWS, ROWS, SEEN), F32),
-            pltpu.VMEM(weight_tiles.shape[:2] + (LANE,), F32),
-            pltpu.VMEM((rows, LANE), F32),
-        ]
-    if mode != "both":
-        scratch.append(pltpu.VMEM(blurred, F32))
-    scratch.append(pltpu.SemaphoreType.DMA((24,)))
     return pl.pallas_call(
         lambda *refs: iteration_kernel(mode, *refs),
-        out_shape=jax.ShapeDtypeStruct(blurred if mode == "forward" else strips, F32),
-        in_specs=[ANYWHERE] * len(operands),
-        out_specs=ANYWHERE,
+        out_shape=outs,
+        in_specs=[IN_VMEM] * len(operands),
+        out_specs=[IN_VMEM] * len(outs),
         scratch_shapes=scratch,
         compiler_params=pltpu.CompilerParams(vmem_limit_bytes=VMEM_LIMIT),
         cost_estimate=pl.CostEstimate(
@@ -613,11 +557,16 @@
     sides = [far[0], near[0], near[1], far[1]]
     field = over_views(packed)
     moves = field
-    blurred = iteration("forward", [received, field])
-    strips = iteration("adjoint", [received, field, blurred, *sides], weight_tiles)
+    blurred, *bands = iteration("forward", [received, field])
+    strips, *turned = iteration(
+        "adjoint", [received, field, blurred, *sides, weight_tiles, *bands[:2]]
+    )
+    bands += turned
     for _ in range(ITERS - 1):
         field = over_views(pack_field(step_by_view(over_views(strips))))
-        strips = iteration("both", [received, field, moves, *sides], weight_tiles)
+        (strips,) = iteration(
+            "both", [received, field, moves, *sides, weight_tiles, *bands]
+        )
     strips = over_views(strips).reshape(VIEWS, planes, row_count, LANE)
     return jnp.transpose(strips, (1, 2, 0, 3)).reshape(planes, row_count, col_count)
 

time: 112 us -> 105 us (0.938)
  Pallas kernels: 27.7 us -> 19.7 us
    pallas_call x5, Pallas kernels: 25.6 us -> 17.5 us  [the longest x3 16.6 us: iteration(): pl.pallas_call(lambda *refs: iteration_kernel(mode, *refs), out_shape=out...]
  transfers between devices with their start and end apart: 9 -> 9, of which waited for: 3 -> 3; matrix products, arithmetic and copies ran while one was open for 0% -> 0% of each run, Pallas kernels for 7% -> 6%
where the time goes in v4:
time: 105 us; the launch traced here: 104 us
  starting transfers between devices  36 us (34%)
  blocking collectives  30.9 us (29%)
  Pallas kernels  19.7 us (19%)
  waiting for transfers between devices  16.6 us (16%)
    all_to_all x3, blocking collectives, over_views(): return lax.all_to_all(values, 'view', 0, 0)  30.9 us
    pallas_call x3, Pallas kernels, iteration(): pl.pallas_call(lambda *refs: iteration_kernel(mode, *refs), out_shape=out...  16.6 us
    ppermute x4, starting transfers between devices, from_block(): return lax.ppermute(values, 'blk', route)  16 us
    all_to_all x2, starting transfers between devices, over_views(): return lax.all_to_all(values, 'view', 0, 0)  11.1 us
    ppermute x3, starting transfers between devices, step_by_view(): return lax.ppermute(values, ('view', 'blk'), route)  8.87 us
    ppermute x3, waiting for transfers between devices, step_by_view(): return lax.ppermute(values, ('view', 'blk'), route)  8.26 us
    ppermute x4, waiting for transfers between devices, from_block(): return lax.ppermute(values, 'blk', route)  4.3 us
    all_to_all x2, waiting for transfers between devices, over_views(): return lax.all_to_all(values, 'view', 0, 0)  4.06 us
  transfers between devices with their start and end apart: 9, of which 3 were waited for; matrix products, arithmetic and copies ran while one was open for 0% of the time, Pallas kernels for 6%

profile of v4, /device:TPU:256, one launch (start us, length us, event | category | flops | bytes accessed | tf_op | source)
XLA Modules:
  0.0 104.1 jit_solution(7750356452890754036)
XLA Ops:
  0.0 2.1 %pack_measured.1 = f32[8,16,512]{2,1,0:T(8,128)} custom-call(f32[1,2,16,1024]{3,2,1,0:T(8,128)} %measured.1, s32[1,16]{1,0:T(1,128)} %dst_row.1, s32[1,16]{1,0:T(1,128)} %back_shift.1, s32[1,2]{1,0:T(1,128)} %tile_index.1, f32[3,1,31]{2,1,0:T(1,128)} %bitcast.11, f32[3,1,31]{2,1,0:T(1,128)} %bitcast.12, f32[3,1,31]{2,1,0:T(1,128)} %bitcast.13, f32[1,3]{1,0:T(1,128)} %psf_mix.1), custom_call_target="tpu_custom_call" | custom-call | tf_op jit(solution)/shard_map/pack_measured/pallas_call | solution.py:152
  2.2 4.3 %all-to-all-start = ((f32[8,16,512]{2,1,0:T(8,128)}), f32[8,16,512]{2,1,0:T(8,128)S(1)}, u32[]{:S(2)}, u32[]{:S(2)}) async-start(f32[8,16,512]{2,1,0:T(8,128)} %pack_measured.1), calls=%async_computation | async-start | bytes 524288 | tf_op jit(solution)/shard_map/all_to_all | solution.py:529
  6.5 3.5 %collective-permute-start = (f32[2,16,1024]{2,1,0:T(8,128)}, f32[2,16,1024]{2,1,0:T(8,128)S(1)}, u32[]{:S(2)}, u32[]{:S(2)}) collective-permute-start(f32[2,16,1024]{2,1,0:T(8,128)} %param.12), channel_id=1, source_target_pairs={{0,1},{1,2},{2,3},{3,4},{4,5},{5,6},{6,7},{7,8},{8,9},{9,10},{10,1... | collective-permute-start | bytes 393224 | tf_op jit(solution)/shard_map/ppermute | solution.py:519
  10.0 4.1 %all-to-all-done.refs_0_ = f32[8,16,512]{2,1,0:T(8,128)S(1)} async-done(((f32[8,16,512]{2,1,0:T(8,128)}), f32[8,16,512]{2,1,0:T(8,128)S(1)}, u32[]{:S(2)}, u32[]{:S(2)}) %all-to-all-start) | async-done | bytes 262176 | tf_op jit(solution)/shard_map/all_to_all | solution.py:529
  14.1 3.5 %collective-permute-start.1 = (f32[16,128]{1,0:T(8,128)S(1)}, f32[16,128]{1,0:T(8,128)S(1)}, u32[]{:S(2)}, u32[]{:S(2)}) collective-permute-start(f32[16,128]{1,0:T(8,128)S(1)} %slice_reduce_fusion), channel_id=1, source_target_pairs={{0,1},{1,2},{2,3},{3,4},{4,5},{5,6},{6,7},{7,8},{8,9},{9,10},{10,1... | collective-permute-start | bytes 24584 | tf_op jit(solution)/shard_map/ppermute | solution.py:519
  17.5 4.4 %collective-permute-start.3 = (f32[8,16,384]{2,1,0:T(8,128)S(1)}, f32[8,16,384]{2,1,0:T(8,128)S(1)}, u32[]{:S(2)}, u32[]{:S(2)}) collective-permute-start(f32[8,16,384]{2,1,0:T(8,128)S(1)} %slice.9), channel_id=1, source_target_pairs={{2,0},{3,1},{4,2},{5,3},{6,4},{7,5},{8,6},{9,7},{10,8},{11,9},{12,... | collective-permute-start | bytes 589832 | tf_op jit(solution)/shard_map/ppermute | solution.py:525
  21.9 2.4 %collective-permute-start.2 = (f32[8,16,384]{2,1,0:T(8,128)S(1)}, f32[8,16,384]{2,1,0:T(8,128)S(1)}, u32[]{:S(2)}, u32[]{:S(2)}) collective-permute-start(f32[8,16,384]{2,1,0:T(8,128)S(1)} %slice.9), channel_id=1, source_target_pairs={{0,2},{1,3},{2,4},{3,5},{4,6},{5,7},{6,8},{7,9},{8,10},{9,11},{10,... | collective-permute-start | bytes 589832 | tf_op jit(solution)/shard_map/ppermute | solution.py:525
  24.3 0.0 collective-permute-done.field
  24.3 0.0 collective-permute-done.1.moves
  24.3 0.8 pack_estimate.1
  25.1 6.8 %all-to-all-start.1 = ((f32[8,4,16,128]{3,2,1,0:T(8,128)}), f32[8,4,16,128]{3,2,1,0:T(8,128)S(1)}, u32[]{:S(2)}, u32[]{:S(2)}) async-start(f32[8,4,16,128]{3,2,1,0:T(8,128)} %pack_estimate.1), calls=%async_computation.1 | async-start | bytes 524288 | tf_op jit(solution)/shard_map/all_to_all | solution.py:529
  31.9 7.3 %collective-permute-start.5 = (f32[8,16,384]{2,1,0:T(8,128)S(1)}, f32[8,16,384]{2,1,0:T(8,128)S(1)}, u32[]{:S(2)}, u32[]{:S(2)}) collective-permute-start(f32[8,16,384]{2,1,0:T(8,128)S(1)} %slice.9), channel_id=1, source_target_pairs={{1,0},{2,1},{3,2},{4,3},{5,4},{6,5},{7,6},{8,7},{9,8},{10,9},{11,1... | collective-permute-start | bytes 589832 | tf_op jit(solution)/shard_map/ppermute | solution.py:525
  39.2 1.9 %collective-permute-start.4 = (f32[8,16,384]{2,1,0:T(8,128)S(1)}, f32[8,16,384]{2,1,0:T(8,128)S(1)}, u32[]{:S(2)}, u32[]{:S(2)}) collective-permute-start(f32[8,16,384]{2,1,0:T(8,128)S(1)} %slice.9), channel_id=1, source_target_pairs={{0,1},{1,2},{2,3},{3,4},{4,5},{5,6},{6,7},{7,8},{8,9},{9,10},{10,1... | collective-permute-start | bytes 589832 | tf_op jit(solution)/shard_map/ppermute | solution.py:525
  41.2 0.0 collective-permute-done.3.refs_1_
  41.2 0.0 collective-permute-done.2.refs_0_
  41.2 0.0 copy-start
  41.2 0.0 all-to-all-done.1.refs_1_.refs_2_
  41.2 6.0 %iteration_forward.1 = (f32[8,128,256]{2,1,0:T(8,128)S(1)}, bf16[8,3,256,256]{3,2,1,0:T(8,128)(2,1)S(1)}, bf16[8,3,256,256]{3,2,1,0:T(8,128)(2,1)S(1)}, bf16[8,3...) custom-call(f32[8,16,512]{2,1,0:T(8,128)S(1)} %all-to-all-done.refs_0_, f32[8,4,16,128]{3,2,1,0:T(8,128)S(1)} %all-to-all-done.1.refs_1_.refs_2_), custom_call_target="tpu_custom_call" | custom-call | flops 8000000000 | bytes 1000000 | tf_op jit(solution)/shard_map/iteration_forward/pallas_call | solution.py:498
  47.2 0.0 collective-permute-done.5.refs_5_
  47.2 4.3 %collective-permute-done.4.refs_4_ = f32[8,16,384]{2,1,0:T(8,128)S(1)} collective-permute-done((f32[8,16,384]{2,1,0:T(8,128)S(1)}, f32[8,16,384]{2,1,0:T(8,128)S(1)}, u32[]{:S(2)}, u32[]{:S(2)}) %collective-permute-start.4) | collective-permute-done | bytes 196640 | tf_op jit(solution)/shard_map/ppermute | solution.py:525
  51.5 0.0 copy-done
  51.5 3.0 %iteration_adjoint.1 = (f32[8,32,128]{2,1,0:T(8,128)S(1)}, bf16[8,96,128]{2,1,0:T(8,128)(2,1)S(1)}, bf16[8,96,128]{2,1,0:T(8,128)(2,1)S(1)}) custom-call(f32[8,16,512]{2,1,0:T(8,128)S(1)} %all-to-all-done.refs_0_, f32[8,4,16,128]{3,2,1,0:T(8,128)S(1)} %all-to-all-done.1.refs_1_.refs_2_, f32[8,128,256]{2,1,0:T(8,128)S(1)} %get-tuple-element.22.refs_2_, ...), custom_call_target="tpu_custom_call" | custom-call | flops 8000000000 | bytes 1000000 | tf_op jit(solution)/shard_map/iteration_adjoint/pallas_call | solution.py:498
  54.5 10.4 %all_to_all.25 = f32[8,32,128]{2,1,0:T(8,128)S(1)} all-to-all(f32[8,32,128]{2,1,0:T(8,128)S(1)} %get-tuple-element.28), channel_id=1, replica_groups=mesh['view'=8,'blk'=64] {'view'}, dimensions={0} | all-to-all | bytes 262144 | tf_op jit(solution)/shard_map/all_to_all | solution.py:529
  64.8 1.9 %collective-permute-start.6 = (f32[8,32,128]{2,1,0:T(8,128)S(1)}, f32[8,32,128]{2,1,0:T(8,128)S(1)}, u32[]{:S(2)}, u32[]{:S(2)}) collective-permute-start(f32[8,32,128]{2,1,0:T(8,128)S(1)} %all_to_all.25), channel_id=1, source_target_pairs={{0,1},{1,2},{2,3},{3,4},{4,5},{5,6},{6,7},{7,8},{8,9},{9,10},{10,1... | collective-permute-start | bytes 393224 | tf_op jit(solution)/shard_map/ppermute | solution.py:519
  66.7 8.3 %collective-permute-done.6.field = f32[8,32,128]{2,1,0:T(8,128)S(1)} collective-permute-done((f32[8,32,128]{2,1,0:T(8,128)S(1)}, f32[8,32,128]{2,1,0:T(8,128)S(1)}, u32[]{:S(2)}, u32[]{:S(2)}) %collective-permute-start.6) | collective-permute-done | bytes 131104 | tf_op jit(solution)/shard_map/ppermute | solution.py:519
  75.0 0.1 pack_field.1
  75.1 12.0 %all_to_all.26.refs_1_ = f32[8,4,16,128]{3,2,1,0:T(8,128)S(1)} all-to-all(f32[8,4,16,128]{3,2,1,0:T(8,128)S(1)} %pack_field.1), channel_id=1, replica_groups=mesh['view'=8,'blk'=64] {'view'}, dimensions={0} | all-to-all | bytes 524288 | tf_op jit(solution)/shard_map/all_to_all | solution.py:529
  87.1 7.7 %iteration_both.1 = f32[8,32,128]{2,1,0:T(8,128)S(1)} custom-call(f32[8,16,512]{2,1,0:T(8,128)S(1)} %all-to-all-done.refs_0_, f32[8,4,16,128]{3,2,1,0:T(8,128)S(1)} %all_to_all.26.refs_1_, f32[8,4,16,128]{3,2,1,0:T(8,128)S(1)} %all-to-all-done.1.refs_1_.refs_2_, f32[8,16,384]{2,1,0:T(8,128)S(1)} %get-tuple-element.23.refs_3_, ...), custom_call_target="tpu_custom_call" | custom-call | flops 8000000000 | bytes 1000000 | tf_op jit(solution)/shard_map/iteration_both/pallas_call | solution.py:498
  94.9 8.5 %all_to_all.27 = f32[8,32,128]{2,1,0:T(8,128)S(1)} all-to-all(f32[8,32,128]{2,1,0:T(8,128)S(1)} %iteration_both.1), channel_id=1, replica_groups=mesh['view'=8,'blk'=64] {'view'}, dimensions={0} | all-to-all | bytes 262144 | tf_op jit(solution)/shard_map/all_to_all | solution.py:529
  103.4 0.7 copy.16
  (3 shorter events, 0.0 us)
Async XLA Ops:
  2.2 11.9 %all-to-all-start = ((f32[8,16,512]{2,1,0:T(8,128)}), f32[8,16,512]{2,1,0:T(8,128)S(1)}, u32[]{:S(2)}, u32[]{:S(2)}) async-start(f32[8,16,512]{2,1,0:T(8,128)} %pack_measured.1), calls=%async_computation | async-start | bytes 524288 | tf_op jit(solution)/shard_map/all_to_all | solution.py:529
  6.5 17.8 %collective-permute-start = (f32[2,16,1024]{2,1,0:T(8,128)}, f32[2,16,1024]{2,1,0:T(8,128)S(1)}, u32[]{:S(2)}, u32[]{:S(2)}) collective-permute-start(f32[2,16,1024]{2,1,0:T(8,128)} %param.12), channel_id=1, source_target_pairs={{0,1},{1,2},{2,3},{3,4},{4,5},{5,6},{6,7},{7,8},{8,9},{9,10},{10,1... | collective-permute-start | bytes 393224 | tf_op jit(solution)/shard_map/ppermute | solution.py:519
  14.1 10.3 %collective-permute-start.1 = (f32[16,128]{1,0:T(8,128)S(1)}, f32[16,128]{1,0:T(8,128)S(1)}, u32[]{:S(2)}, u32[]{:S(2)}) collective-permute-start(f32[16,128]{1,0:T(8,128)S(1)} %slice_reduce_fusion), channel_id=1, source_target_pairs={{0,1},{1,2},{2,3},{3,4},{4,5},{5,6},{6,7},{7,8},{8,9},{9,10},{10,1... | collective-permute-start | bytes 24584 | tf_op jit(solution)/shard_map/ppermute | solution.py:519
  17.5 23.6 %collective-permute-start.3 = (f32[8,16,384]{2,1,0:T(8,128)S(1)}, f32[8,16,384]{2,1,0:T(8,128)S(1)}, u32[]{:S(2)}, u32[]{:S(2)}) collective-permute-start(f32[8,16,384]{2,1,0:T(8,128)S(1)} %slice.9), channel_id=1, source_target_pairs={{2,0},{3,1},{4,2},{5,3},{6,4},{7,5},{8,6},{9,7},{10,8},{11,9},{12,... | collective-permute-start | bytes 589832 | tf_op jit(solution)/shard_map/ppermute | solution.py:525
  21.9 19.3 %collective-permute-start.2 = (f32[8,16,384]{2,1,0:T(8,128)S(1)}, f32[8,16,384]{2,1,0:T(8,128)S(1)}, u32[]{:S(2)}, u32[]{:S(2)}) collective-permute-start(f32[8,16,384]{2,1,0:T(8,128)S(1)} %slice.9), channel_id=1, source_target_pairs={{0,2},{1,3},{2,4},{3,5},{4,6},{5,7},{6,8},{7,9},{8,10},{9,11},{10,... | collective-permute-start | bytes 589832 | tf_op jit(solution)/shard_map/ppermute | solution.py:525
  25.1 16.1 %all-to-all-start.1 = ((f32[8,4,16,128]{3,2,1,0:T(8,128)}), f32[8,4,16,128]{3,2,1,0:T(8,128)S(1)}, u32[]{:S(2)}, u32[]{:S(2)}) async-start(f32[8,4,16,128]{3,2,1,0:T(8,128)} %pack_estimate.1), calls=%async_computation.1 | async-start | bytes 524288 | tf_op jit(solution)/shard_map/all_to_all | solution.py:529
  31.9 15.3 %collective-permute-start.5 = (f32[8,16,384]{2,1,0:T(8,128)S(1)}, f32[8,16,384]{2,1,0:T(8,128)S(1)}, u32[]{:S(2)}, u32[]{:S(2)}) collective-permute-start(f32[8,16,384]{2,1,0:T(8,128)S(1)} %slice.9), channel_id=1, source_target_pairs={{1,0},{2,1},{3,2},{4,3},{5,4},{6,5},{7,6},{8,7},{9,8},{10,9},{11,1... | collective-permute-start | bytes 589832 | tf_op jit(solution)/shard_map/ppermute | solution.py:525
  39.2 12.2 %collective-permute-start.4 = (f32[8,16,384]{2,1,0:T(8,128)S(1)}, f32[8,16,384]{2,1,0:T(8,128)S(1)}, u32[]{:S(2)}, u32[]{:S(2)}) collective-permute-start(f32[8,16,384]{2,1,0:T(8,128)S(1)} %slice.9), channel_id=1, source_target_pairs={{0,1},{1,2},{2,3},{3,4},{4,5},{5,6},{6,7},{7,8},{8,9},{9,10},{10,1... | collective-permute-start | bytes 589832 | tf_op jit(solution)/shard_map/ppermute | solution.py:525
  41.2 10.3 %copy-start = (f32[8,8,1024]{2,1,0:T(8,128)S(1)}, f32[8,8,1024]{2,1,0:T(8,128)}, u32[]{:S(2)}) copy-start(f32[8,8,1024]{2,1,0:T(8,128)} %refs_7_.3) | copy-start | bytes 786436
  64.8 10.2 %collective-permute-start.6 = (f32[8,32,128]{2,1,0:T(8,128)S(1)}, f32[8,32,128]{2,1,0:T(8,128)S(1)}, u32[]{:S(2)}, u32[]{:S(2)}) collective-permute-start(f32[8,32,128]{2,1,0:T(8,128)S(1)} %all_to_all.25), channel_id=1, source_target_pairs={{0,1},{1,2},{2,3},{3,4},{4,5},{5,6},{6,7},{7,8},{8,9},{9,10},{10,1... | collective-permute-start | bytes 393224 | tf_op jit(solution)/shard_map/ppermute | solution.py:519

commit v5 on v4

--- a/solution.py
+++ b/solution.py
@@ -26,10 +26,6 @@
 SMALL_LIMIT = 4 * 1024 * 1024
 
 
-def whole(shape):
-    return pl.BlockSpec(tuple(shape), lambda i: (0,) * len(shape))
-
-
 def start_all(copies):
     for copy in copies:
         copy.start()
@@ -91,9 +87,18 @@
     return tiles
 
 
-def pack_measured_kernel(
-    measured, dst_row, back_shift, tile_index, psf_z, psf_y, psf_x, psf_mix, out_ref, table, out, sems
-):
+def pack_measured_kernel(*refs):
+    sources, out, table = refs[:8], refs[8], refs[9]
+    targets, sems = refs[10:18], refs[18]
+    wait_all(
+        start_all(
+            [
+                pltpu.make_async_copy(source, target, sems.at[number])
+                for number, (source, target) in enumerate(zip(sources, targets))
+            ]
+        )
+    )
+    measured, dst_row, back_shift, tile_index, psf_z, psf_y, psf_x, psf_mix = targets
     rows = 2 * ROWS
     view = lax.axis_index("view")
     table[...] = jnp.zeros_like(table)
@@ -138,7 +143,6 @@
         turned = [pltpu.roll(row[place], HALF, 1) for row in strips]
         for number, tile in enumerate((turned[0], turned[1], edges, stash)):
             out[place, :, number * LANE : (number + 1) * LANE] = tile
-    wait_all(start_all([pltpu.make_async_copy(out, out_ref, sems.at[0])]))
 
 
 ANYWHERE = pl.BlockSpec(memory_space=pl.ANY)
@@ -148,17 +152,15 @@
 def pack_measured(measured, dst_row, back_shift, tile_index, psf_z, psf_y, psf_x, psf_mix):
     turned = [jnp.transpose(psf, (1, 0, 2)) for psf in (psf_z, psf_y, psf_x)]
     operands = (measured, dst_row, back_shift, tile_index, *turned, psf_mix)
-    shape = (VIEWS, ROWS, 4 * LANE)
     return pl.pallas_call(
         pack_measured_kernel,
-        out_shape=jax.ShapeDtypeStruct(shape, F32),
-        grid=(1,),
-        in_specs=[whole(operand.shape) for operand in operands],
-        out_specs=ANYWHERE,
+        out_shape=jax.ShapeDtypeStruct((VIEWS, ROWS, 4 * LANE), F32),
+        in_specs=[ANYWHERE] * len(operands),
+        out_specs=IN_VMEM,
         scratch_shapes=[
             pltpu.VMEM((LANE, LANE), F32),
-            pltpu.VMEM(shape, F32),
-            pltpu.SemaphoreType.DMA((1,)),
+            *[pltpu.VMEM(operand.shape, operand.dtype) for operand in operands],
+            pltpu.SemaphoreType.DMA((len(operands),)),
         ],
         name="pack_measured",
     )(*operands)
@@ -308,6 +310,9 @@
             low[view, start : start + ROWS, :] = band_low
 
 
+LAGS = (0, 1, 2, 4, 6)
+
+
 def iteration_kernel(mode, *refs):
     refs = list(refs)
 
@@ -391,18 +396,20 @@
                 x_low[view, rows, part * LANE : (part + 1) * LANE] = low
         return phase, shift
 
-    def blur(view):
+    def row_stage(view):
         xh, xl = x_high[view], x_low[view]
-        layers = triple(row_high[view], row_low[view], xh, xl, dot)
+        return halves(triple(row_high[view], row_low[view], xh, xl, dot))
+
+    def column_stage(view, layers):
         blurred = None
         height = 8 * ROWS
         for term in range(RANK):
-            high, low = halves(layers[term * height : (term + 1) * height])
+            high, low = [half[term * height : (term + 1) * height] for half in layers]
             part = triple(high, low, col_high[view, term], col_low[view, term], dot)
             blurred = part if blurred is None else blurred + part
         return blurred
 
-    def finish(view, blurred, phase, shift):
+    def turned_stage(view, blurred, phase):
         quotients = [None] * 8
         lower = lanes_of((ROWS, LANE)) < HALF
         for place in range(4):
@@ -427,7 +434,9 @@
                 quotients[plane * 4 + place] = jnp.where(fine, ratio, 0.0)
         quotient = jnp.concatenate(quotients, axis=0)
         high, low = halves(quotient)
-        layers = triple(turned_high[view], turned_low[view], high, low, dot)
+        return triple(turned_high[view], turned_low[view], high, low, dot)
+
+    def last_stage(view, layers, shift):
         where = lane + shift
         index = where & (LANE - 1)
         adjoint = None
@@ -457,16 +466,36 @@
 
     total = jnp.zeros((2 * ROWS, LANE), F32)
     weight_total = jnp.zeros((2 * ROWS, LANE), F32)
-    for view in range(VIEWS):
-        phase, shift = prepare(view)
-        now = blur(view) if forward else blurred[view]
-        if not backward:
-            out[view] = now
-            continue
-        more, weight = finish(view, now, phase, shift)
-        total = total + more
-        weight_total = weight_total + weight
-
+    known = [None] * VIEWS
+    values = [None] * VIEWS
+    stages = []
+    if forward:
+        stages += ["prepare", "rows", "columns"]
+    else:
+        stages += ["prepare"]
+    if backward:
+        stages += ["turned", "last"]
+    for step in range(VIEWS + LAGS[len(stages) - 1]):
+        for stage, lag in zip(stages, LAGS):
+            view = step - lag
+            if not 0 <= view < VIEWS:
+                continue
+            if stage == "prepare":
+                known[view] = prepare(view)
+                if not forward:
+                    values[view] = blurred[view]
+            elif stage == "rows":
+                values[view] = row_stage(view)
+            elif stage == "columns":
+                values[view] = column_stage(view, values[view])
+                if not backward:
+                    out[view] = values[view]
+            elif stage == "turned":
+                values[view] = turned_stage(view, values[view], known[view][0])
+            else:
+                more, weight = last_stage(view, values[view], known[view][1])
+                total = total + more
+                weight_total = weight_total + weight
     if not backward:
         return
     lower = pltpu.roll(field[OWN, 0:2].reshape(2 * ROWS, LANE), HALF, 1)

time: 105 us -> 101 us (0.962)
  Pallas kernels: 19.7 us -> 16.1 us
    pallas_call x3, Pallas kernels: 16.6 us -> 13 us  [iteration(): pl.pallas_call(lambda *refs: iteration_kernel(mode, *refs), out_shape=out...]
  transfers between devices with their start and end apart: 9 -> 9, of which waited for: 3 -> 3; matrix products, arithmetic and copies ran while one was open for 0% -> 0% of each run, Pallas kernels for 6% -> 7%
where the time goes in v5:
time: 101 us; the launch traced here: 100 us
  starting transfers between devices  36 us (36%)
  blocking collectives  31 us (31%)
  waiting for transfers between devices  16.5 us (16%)
  Pallas kernels  16.1 us (16%)
    all_to_all x3, blocking collectives, over_views(): return lax.all_to_all(values, 'view', 0, 0)  31 us
    ppermute x4, starting transfers between devices, from_block(): return lax.ppermute(values, 'blk', route)  16 us
    pallas_call x3, Pallas kernels, iteration(): pl.pallas_call(lambda *refs: iteration_kernel(mode, *refs), out_shape=out...  13 us
    all_to_all x2, starting transfers between devices, over_views(): return lax.all_to_all(values, 'view', 0, 0)  11.1 us
    ppermute x3, starting transfers between devices, step_by_view(): return lax.ppermute(values, ('view', 'blk'), route)  8.87 us
    ppermute x3, waiting for transfers between devices, step_by_view(): return lax.ppermute(values, ('view', 'blk'), route)  8.26 us
    ppermute x4, waiting for transfers between devices, from_block(): return lax.ppermute(values, 'blk', route)  4.18 us
    all_to_all x2, waiting for transfers between devices, over_views(): return lax.all_to_all(values, 'view', 0, 0)  4.06 us
  transfers between devices with their start and end apart: 9, of which 3 were waited for; matrix products, arithmetic and copies ran while one was open for 0% of the time, Pallas kernels for 7%

profile of v5, /device:TPU:256, one launch (start us, length us, event | category | flops | bytes accessed | tf_op | source)
XLA Modules:
  0.0 100.4 jit_solution(6828151804897367076)
XLA Ops:
  0.0 2.2 %pack_measured.1 = f32[8,16,512]{2,1,0:T(8,128)} custom-call(f32[1,2,16,1024]{3,2,1,0:T(8,128)} %refs_0_.1, s32[1,16]{1,0:T(1,128)} %refs_1_.1, s32[1,16]{1,0:T(1,128)} %refs_2_.1, s32[1,2]{1,0:T(1,128)} %refs_3_.1, f32[3,1,31]{2,1,0:T(1,128)} %bitcast.11, f32[3,1,31]{2,1,0:T(1,128)} %bitcast.12, f32[3,1,31]{2,1,0:T(1,128)} %bitcast.13, f32[1,3]{1,0:T(1,128)} %refs_7_.3), custom_call_target="tpu_custom_call" | custom-call | tf_op jit(solution)/shard_map/pack_measured/pallas_call | solution.py:155
  2.2 4.3 %all-to-all-start = ((f32[8,16,512]{2,1,0:T(8,128)}), f32[8,16,512]{2,1,0:T(8,128)S(1)}, u32[]{:S(2)}, u32[]{:S(2)}) async-start(f32[8,16,512]{2,1,0:T(8,128)} %pack_measured.1), calls=%async_computation | async-start | bytes 524288 | tf_op jit(solution)/shard_map/all_to_all | solution.py:558
  6.5 3.5 %collective-permute-start = (f32[2,16,1024]{2,1,0:T(8,128)}, f32[2,16,1024]{2,1,0:T(8,128)S(1)}, u32[]{:S(2)}, u32[]{:S(2)}) collective-permute-start(f32[2,16,1024]{2,1,0:T(8,128)} %param.12), channel_id=1, source_target_pairs={{0,1},{1,2},{2,3},{3,4},{4,5},{5,6},{6,7},{7,8},{8,9},{9,10},{10,1... | collective-permute-start | bytes 393224 | tf_op jit(solution)/shard_map/ppermute | solution.py:548
  10.0 4.1 %all-to-all-done.refs_0_ = f32[8,16,512]{2,1,0:T(8,128)S(1)} async-done(((f32[8,16,512]{2,1,0:T(8,128)}), f32[8,16,512]{2,1,0:T(8,128)S(1)}, u32[]{:S(2)}, u32[]{:S(2)}) %all-to-all-start) | async-done | bytes 262176 | tf_op jit(solution)/shard_map/all_to_all | solution.py:558
  14.1 3.5 %collective-permute-start.1 = (f32[16,128]{1,0:T(8,128)S(1)}, f32[16,128]{1,0:T(8,128)S(1)}, u32[]{:S(2)}, u32[]{:S(2)}) collective-permute-start(f32[16,128]{1,0:T(8,128)S(1)} %slice_reduce_fusion), channel_id=1, source_target_pairs={{0,1},{1,2},{2,3},{3,4},{4,5},{5,6},{6,7},{7,8},{8,9},{9,10},{10,1... | collective-permute-start | bytes 24584 | tf_op jit(solution)/shard_map/ppermute | solution.py:548
  17.6 4.4 %collective-permute-start.3 = (f32[8,16,384]{2,1,0:T(8,128)S(1)}, f32[8,16,384]{2,1,0:T(8,128)S(1)}, u32[]{:S(2)}, u32[]{:S(2)}) collective-permute-start(f32[8,16,384]{2,1,0:T(8,128)S(1)} %slice.9), channel_id=1, source_target_pairs={{2,0},{3,1},{4,2},{5,3},{6,4},{7,5},{8,6},{9,7},{10,8},{11,9},{12,... | collective-permute-start | bytes 589832 | tf_op jit(solution)/shard_map/ppermute | solution.py:554
  21.9 2.4 %collective-permute-start.2 = (f32[8,16,384]{2,1,0:T(8,128)S(1)}, f32[8,16,384]{2,1,0:T(8,128)S(1)}, u32[]{:S(2)}, u32[]{:S(2)}) collective-permute-start(f32[8,16,384]{2,1,0:T(8,128)S(1)} %slice.9), channel_id=1, source_target_pairs={{0,2},{1,3},{2,4},{3,5},{4,6},{5,7},{6,8},{7,9},{8,10},{9,11},{10,... | collective-permute-start | bytes 589832 | tf_op jit(solution)/shard_map/ppermute | solution.py:554
  24.3 0.0 collective-permute-done.field
  24.3 0.0 collective-permute-done.1.moves
  24.3 0.8 pack_estimate.1
  25.1 6.8 %all-to-all-start.1 = ((f32[8,4,16,128]{3,2,1,0:T(8,128)}), f32[8,4,16,128]{3,2,1,0:T(8,128)S(1)}, u32[]{:S(2)}, u32[]{:S(2)}) async-start(f32[8,4,16,128]{3,2,1,0:T(8,128)} %pack_estimate.1), calls=%async_computation.1 | async-start | bytes 524288 | tf_op jit(solution)/shard_map/all_to_all | solution.py:558
  31.9 7.3 %collective-permute-start.5 = (f32[8,16,384]{2,1,0:T(8,128)S(1)}, f32[8,16,384]{2,1,0:T(8,128)S(1)}, u32[]{:S(2)}, u32[]{:S(2)}) collective-permute-start(f32[8,16,384]{2,1,0:T(8,128)S(1)} %slice.9), channel_id=1, source_target_pairs={{1,0},{2,1},{3,2},{4,3},{5,4},{6,5},{7,6},{8,7},{9,8},{10,9},{11,1... | collective-permute-start | bytes 589832 | tf_op jit(solution)/shard_map/ppermute | solution.py:554
  39.3 1.9 %collective-permute-start.4 = (f32[8,16,384]{2,1,0:T(8,128)S(1)}, f32[8,16,384]{2,1,0:T(8,128)S(1)}, u32[]{:S(2)}, u32[]{:S(2)}) collective-permute-start(f32[8,16,384]{2,1,0:T(8,128)S(1)} %slice.9), channel_id=1, source_target_pairs={{0,1},{1,2},{2,3},{3,4},{4,5},{5,6},{6,7},{7,8},{8,9},{9,10},{10,1... | collective-permute-start | bytes 589832 | tf_op jit(solution)/shard_map/ppermute | solution.py:554
  41.2 0.0 collective-permute-done.3.refs_1_
  41.2 0.0 collective-permute-done.2.refs_0_
  41.2 0.0 copy-start
  41.2 0.0 all-to-all-done.1.refs_1_.refs_2_
  41.2 6.1 %iteration_forward.1 = (f32[8,128,256]{2,1,0:T(8,128)S(1)}, bf16[8,3,256,256]{3,2,1,0:T(8,128)(2,1)S(1)}, bf16[8,3,256,256]{3,2,1,0:T(8,128)(2,1)S(1)}, bf16[8,3...) custom-call(f32[8,16,512]{2,1,0:T(8,128)S(1)} %all-to-all-done.refs_0_, f32[8,4,16,128]{3,2,1,0:T(8,128)S(1)} %all-to-all-done.1.refs_1_.refs_2_), custom_call_target="tpu_custom_call" | custom-call | flops 8000000000 | bytes 1000000 | tf_op jit(solution)/shard_map/iteration_forward/pallas_call | solution.py:527
  47.3 0.0 collective-permute-done.5.refs_5_
  47.3 4.2 %collective-permute-done.4.refs_4_ = f32[8,16,384]{2,1,0:T(8,128)S(1)} collective-permute-done((f32[8,16,384]{2,1,0:T(8,128)S(1)}, f32[8,16,384]{2,1,0:T(8,128)S(1)}, u32[]{:S(2)}, u32[]{:S(2)}) %collective-permute-start.4) | collective-permute-done | bytes 196640 | tf_op jit(solution)/shard_map/ppermute | solution.py:554
  51.5 0.0 copy-done
  51.5 2.5 %iteration_adjoint.1 = (f32[8,32,128]{2,1,0:T(8,128)S(1)}, bf16[8,96,128]{2,1,0:T(8,128)(2,1)S(1)}, bf16[8,96,128]{2,1,0:T(8,128)(2,1)S(1)}) custom-call(f32[8,16,512]{2,1,0:T(8,128)S(1)} %all-to-all-done.refs_0_, f32[8,4,16,128]{3,2,1,0:T(8,128)S(1)} %all-to-all-done.1.refs_1_.refs_2_, f32[8,128,256]{2,1,0:T(8,128)S(1)} %get-tuple-element.22.refs_2_, ...), custom_call_target="tpu_custom_call" | custom-call | flops 8000000000 | bytes 1000000 | tf_op jit(solution)/shard_map/iteration_adjoint/pallas_call | solution.py:527
  54.0 10.4 %all_to_all.25 = f32[8,32,128]{2,1,0:T(8,128)S(1)} all-to-all(f32[8,32,128]{2,1,0:T(8,128)S(1)} %get-tuple-element.28), channel_id=1, replica_groups=mesh['view'=8,'blk'=64] {'view'}, dimensions={0} | all-to-all | bytes 262144 | tf_op jit(solution)/shard_map/all_to_all | solution.py:558
  64.4 1.9 %collective-permute-start.6 = (f32[8,32,128]{2,1,0:T(8,128)S(1)}, f32[8,32,128]{2,1,0:T(8,128)S(1)}, u32[]{:S(2)}, u32[]{:S(2)}) collective-permute-start(f32[8,32,128]{2,1,0:T(8,128)S(1)} %all_to_all.25), channel_id=1, source_target_pairs={{0,1},{1,2},{2,3},{3,4},{4,5},{5,6},{6,7},{7,8},{8,9},{9,10},{10,1... | collective-permute-start | bytes 393224 | tf_op jit(solution)/shard_map/ppermute | solution.py:548
  66.3 8.3 %collective-permute-done.6.field = f32[8,32,128]{2,1,0:T(8,128)S(1)} collective-permute-done((f32[8,32,128]{2,1,0:T(8,128)S(1)}, f32[8,32,128]{2,1,0:T(8,128)S(1)}, u32[]{:S(2)}, u32[]{:S(2)}) %collective-permute-start.6) | collective-permute-done | bytes 131104 | tf_op jit(solution)/shard_map/ppermute | solution.py:548
  74.6 0.1 pack_field.1
  74.7 12.1 %all_to_all.26.refs_1_ = f32[8,4,16,128]{3,2,1,0:T(8,128)S(1)} all-to-all(f32[8,4,16,128]{3,2,1,0:T(8,128)S(1)} %pack_field.1), channel_id=1, replica_groups=mesh['view'=8,'blk'=64] {'view'}, dimensions={0} | all-to-all | bytes 524288 | tf_op jit(solution)/shard_map/all_to_all | solution.py:558
  86.8 4.4 %iteration_both.1 = f32[8,32,128]{2,1,0:T(8,128)S(1)} custom-call(f32[8,16,512]{2,1,0:T(8,128)S(1)} %all-to-all-done.refs_0_, f32[8,4,16,128]{3,2,1,0:T(8,128)S(1)} %all_to_all.26.refs_1_, f32[8,4,16,128]{3,2,1,0:T(8,128)S(1)} %all-to-all-done.1.refs_1_.refs_2_, f32[8,16,384]{2,1,0:T(8,128)S(1)} %get-tuple-element.23.refs_3_, ...), custom_call_target="tpu_custom_call" | custom-call | flops 8000000000 | bytes 1000000 | tf_op jit(solution)/shard_map/iteration_both/pallas_call | solution.py:527
  91.3 8.5 %all_to_all.27 = f32[8,32,128]{2,1,0:T(8,128)S(1)} all-to-all(f32[8,32,128]{2,1,0:T(8,128)S(1)} %iteration_both.1), channel_id=1, replica_groups=mesh['view'=8,'blk'=64] {'view'}, dimensions={0} | all-to-all | bytes 262144 | tf_op jit(solution)/shard_map/all_to_all | solution.py:558
  99.8 0.7 copy.16
  (3 shorter events, 0.0 us)
Async XLA Ops:
  2.2 11.9 %all-to-all-start = ((f32[8,16,512]{2,1,0:T(8,128)}), f32[8,16,512]{2,1,0:T(8,128)S(1)}, u32[]{:S(2)}, u32[]{:S(2)}) async-start(f32[8,16,512]{2,1,0:T(8,128)} %pack_measured.1), calls=%async_computation | async-start | bytes 524288 | tf_op jit(solution)/shard_map/all_to_all | solution.py:558
  6.5 17.8 %collective-permute-start = (f32[2,16,1024]{2,1,0:T(8,128)}, f32[2,16,1024]{2,1,0:T(8,128)S(1)}, u32[]{:S(2)}, u32[]{:S(2)}) collective-permute-start(f32[2,16,1024]{2,1,0:T(8,128)} %param.12), channel_id=1, source_target_pairs={{0,1},{1,2},{2,3},{3,4},{4,5},{5,6},{6,7},{7,8},{8,9},{9,10},{10,1... | collective-permute-start | bytes 393224 | tf_op jit(solution)/shard_map/ppermute | solution.py:548
  14.1 10.3 %collective-permute-start.1 = (f32[16,128]{1,0:T(8,128)S(1)}, f32[16,128]{1,0:T(8,128)S(1)}, u32[]{:S(2)}, u32[]{:S(2)}) collective-permute-start(f32[16,128]{1,0:T(8,128)S(1)} %slice_reduce_fusion), channel_id=1, source_target_pairs={{0,1},{1,2},{2,3},{3,4},{4,5},{5,6},{6,7},{7,8},{8,9},{9,10},{10,1... | collective-permute-start | bytes 24584 | tf_op jit(solution)/shard_map/ppermute | solution.py:548
  17.6 23.6 %collective-permute-start.3 = (f32[8,16,384]{2,1,0:T(8,128)S(1)}, f32[8,16,384]{2,1,0:T(8,128)S(1)}, u32[]{:S(2)}, u32[]{:S(2)}) collective-permute-start(f32[8,16,384]{2,1,0:T(8,128)S(1)} %slice.9), channel_id=1, source_target_pairs={{2,0},{3,1},{4,2},{5,3},{6,4},{7,5},{8,6},{9,7},{10,8},{11,9},{12,... | collective-permute-start | bytes 589832 | tf_op jit(solution)/shard_map/ppermute | solution.py:554
  21.9 19.3 %collective-permute-start.2 = (f32[8,16,384]{2,1,0:T(8,128)S(1)}, f32[8,16,384]{2,1,0:T(8,128)S(1)}, u32[]{:S(2)}, u32[]{:S(2)}) collective-permute-start(f32[8,16,384]{2,1,0:T(8,128)S(1)} %slice.9), channel_id=1, source_target_pairs={{0,2},{1,3},{2,4},{3,5},{4,6},{5,7},{6,8},{7,9},{8,10},{9,11},{10,... | collective-permute-start | bytes 589832 | tf_op jit(solution)/shard_map/ppermute | solution.py:554
  25.1 16.1 %all-to-all-start.1 = ((f32[8,4,16,128]{3,2,1,0:T(8,128)}), f32[8,4,16,128]{3,2,1,0:T(8,128)S(1)}, u32[]{:S(2)}, u32[]{:S(2)}) async-start(f32[8,4,16,128]{3,2,1,0:T(8,128)} %pack_estimate.1), calls=%async_computation.1 | async-start | bytes 524288 | tf_op jit(solution)/shard_map/all_to_all | solution.py:558
  31.9 15.4 %collective-permute-start.5 = (f32[8,16,384]{2,1,0:T(8,128)S(1)}, f32[8,16,384]{2,1,0:T(8,128)S(1)}, u32[]{:S(2)}, u32[]{:S(2)}) collective-permute-start(f32[8,16,384]{2,1,0:T(8,128)S(1)} %slice.9), channel_id=1, source_target_pairs={{1,0},{2,1},{3,2},{4,3},{5,4},{6,5},{7,6},{8,7},{9,8},{10,9},{11,1... | collective-permute-start | bytes 589832 | tf_op jit(solution)/shard_map/ppermute | solution.py:554
  39.3 12.2 %collective-permute-start.4 = (f32[8,16,384]{2,1,0:T(8,128)S(1)}, f32[8,16,384]{2,1,0:T(8,128)S(1)}, u32[]{:S(2)}, u32[]{:S(2)}) collective-permute-start(f32[8,16,384]{2,1,0:T(8,128)S(1)} %slice.9), channel_id=1, source_target_pairs={{0,1},{1,2},{2,3},{3,4},{4,5},{5,6},{6,7},{7,8},{8,9},{9,10},{10,1... | collective-permute-start | bytes 589832 | tf_op jit(solution)/shard_map/ppermute | solution.py:554
  41.2 10.3 %copy-start = (f32[8,8,1024]{2,1,0:T(8,128)S(1)}, f32[8,8,1024]{2,1,0:T(8,128)}, u32[]{:S(2)}) copy-start(f32[8,8,1024]{2,1,0:T(8,128)} %refs_7_.5) | copy-start | bytes 786436
  64.4 10.2 %collective-permute-start.6 = (f32[8,32,128]{2,1,0:T(8,128)S(1)}, f32[8,32,128]{2,1,0:T(8,128)S(1)}, u32[]{:S(2)}, u32[]{:S(2)}) collective-permute-start(f32[8,32,128]{2,1,0:T(8,128)S(1)} %all_to_all.25), channel_id=1, source_target_pairs={{0,1},{1,2},{2,3},{3,4},{4,5},{5,6},{6,7},{7,8},{8,9},{9,10},{10,1... | collective-permute-start | bytes 393224 | tf_op jit(solution)/shard_map/ppermute | solution.py:548

commit v6 on v5

--- a/solution.py
+++ b/solution.py
@@ -580,9 +580,10 @@
     moves = jnp.sum(received[:, :, SEEN:], axis=0)
     moves, seen = lax.optimization_barrier((moves, received[:, :, :SEEN]))
     packed = pack_estimate(stepped, step_by_view(moves))
-    far = hand_on([from_block(seen, offset) for offset in (-2, 2)])
-    packed, seen = lax.optimization_barrier((packed, seen))
     near = [from_block(seen, offset) for offset in (-1, 1)]
+    near = hand_on(near)
+    _, *relayed = lax.optimization_barrier((packed, *near))
+    far = [from_block(values, offset) for values, offset in zip(relayed, (-1, 1))]
     sides = [far[0], near[0], near[1], far[1]]
     field = over_views(packed)
     moves = field

time: 101 us -> 99.6 us (0.986)
  waiting for transfers between devices: 16.5 us -> 15.3 us
    all_to_all x2, starting transfers between devices: 11.1 us -> 9.44 us  [over_views(): return lax.all_to_all(values, 'view', 0, 0)]
    ppermute x4, waiting for transfers between devices: 4.18 us -> 3 us  [from_block(): return lax.ppermute(values, 'blk', route)]
where the time goes in v6:
time: 99.6 us; the launch traced here: 99 us
  starting transfers between devices  35.2 us (35%)
  blocking collectives  31.5 us (32%)
  Pallas kernels  16.1 us (16%)
  waiting for transfers between devices  15.3 us (15%)
    all_to_all x3, blocking collectives, over_views(): return lax.all_to_all(values, 'view', 0, 0)  31.5 us
    ppermute x4, starting transfers between devices, from_block(): return lax.ppermute(values, 'blk', route)  16.9 us
    pallas_call x3, Pallas kernels, iteration(): pl.pallas_call(lambda *refs: iteration_kernel(mode, *refs), out_shape=out...  13 us
    all_to_all x2, starting transfers between devices, over_views(): return lax.all_to_all(values, 'view', 0, 0)  9.44 us
    ppermute x3, starting transfers between devices, step_by_view(): return lax.ppermute(values, ('view', 'blk'), route)  8.87 us
    ppermute x3, waiting for transfers between devices, step_by_view(): return lax.ppermute(values, ('view', 'blk'), route)  8.26 us
    all_to_all x2, waiting for transfers between devices, over_views(): return lax.all_to_all(values, 'view', 0, 0)  4.06 us
    ppermute x4, waiting for transfers between devices, from_block(): return lax.ppermute(values, 'blk', route)  3 us
  transfers between devices with their start and end apart: 9, of which 3 were waited for; matrix products, arithmetic and copies ran while one was open for 0% of the time, Pallas kernels for 7%

profile of v6, /device:TPU:256, one launch (start us, length us, event | category | flops | bytes accessed | tf_op | source)
XLA Modules:
  0.0 99.0 jit_solution(5443484748123597656)
XLA Ops:
  0.0 2.2 %pack_measured.1 = f32[8,16,512]{2,1,0:T(8,128)} custom-call(f32[1,2,16,1024]{3,2,1,0:T(8,128)} %refs_0_.1, s32[1,16]{1,0:T(1,128)} %refs_1_.1, s32[1,16]{1,0:T(1,128)} %refs_2_.1, s32[1,2]{1,0:T(1,128)} %refs_3_.1, f32[3,1,31]{2,1,0:T(1,128)} %bitcast.11, f32[3,1,31]{2,1,0:T(1,128)} %bitcast.12, f32[3,1,31]{2,1,0:T(1,128)} %bitcast.13, f32[1,3]{1,0:T(1,128)} %refs_7_.3), custom_call_target="tpu_custom_call" | custom-call | tf_op jit(solution)/shard_map/pack_measured/pallas_call | solution.py:155
  2.2 4.3 %all-to-all-start = ((f32[8,16,512]{2,1,0:T(8,128)}), f32[8,16,512]{2,1,0:T(8,128)S(1)}, u32[]{:S(2)}, u32[]{:S(2)}) async-start(f32[8,16,512]{2,1,0:T(8,128)} %pack_measured.1), calls=%async_computation | async-start | bytes 524288 | tf_op jit(solution)/shard_map/all_to_all | solution.py:558
  6.5 3.5 %collective-permute-start = (f32[2,16,1024]{2,1,0:T(8,128)}, f32[2,16,1024]{2,1,0:T(8,128)S(1)}, u32[]{:S(2)}, u32[]{:S(2)}) collective-permute-start(f32[2,16,1024]{2,1,0:T(8,128)} %param.12), channel_id=1, source_target_pairs={{0,1},{1,2},{2,3},{3,4},{4,5},{5,6},{6,7},{7,8},{8,9},{9,10},{10,1... | collective-permute-start | bytes 393224 | tf_op jit(solution)/shard_map/ppermute | solution.py:548
  10.0 4.1 %all-to-all-done.refs_0_ = f32[8,16,512]{2,1,0:T(8,128)S(1)} async-done(((f32[8,16,512]{2,1,0:T(8,128)}), f32[8,16,512]{2,1,0:T(8,128)S(1)}, u32[]{:S(2)}, u32[]{:S(2)}) %all-to-all-start) | async-done | bytes 262176 | tf_op jit(solution)/shard_map/all_to_all | solution.py:558
  14.1 3.5 %collective-permute-start.1 = (f32[16,128]{1,0:T(8,128)S(1)}, f32[16,128]{1,0:T(8,128)S(1)}, u32[]{:S(2)}, u32[]{:S(2)}) collective-permute-start(f32[16,128]{1,0:T(8,128)S(1)} %slice_reduce_fusion), channel_id=1, source_target_pairs={{0,1},{1,2},{2,3},{3,4},{4,5},{5,6},{6,7},{7,8},{8,9},{9,10},{10,1... | collective-permute-start | bytes 24584 | tf_op jit(solution)/shard_map/ppermute | solution.py:548
  17.6 5.7 %collective-permute-start.3 = (f32[8,16,384]{2,1,0:T(8,128)S(1)}, f32[8,16,384]{2,1,0:T(8,128)S(1)}, u32[]{:S(2)}, u32[]{:S(2)}) collective-permute-start(f32[8,16,384]{2,1,0:T(8,128)S(1)} %slice.9), channel_id=1, source_target_pairs={{1,0},{2,1},{3,2},{4,3},{5,4},{6,5},{7,6},{8,7},{9,8},{10,9},{11,1... | collective-permute-start | bytes 589832 | tf_op jit(solution)/shard_map/ppermute | solution.py:554
  23.2 1.9 %collective-permute-start.2 = (f32[8,16,384]{2,1,0:T(8,128)S(1)}, f32[8,16,384]{2,1,0:T(8,128)S(1)}, u32[]{:S(2)}, u32[]{:S(2)}) collective-permute-start(f32[8,16,384]{2,1,0:T(8,128)S(1)} %slice.9), channel_id=1, source_target_pairs={{0,1},{1,2},{2,3},{3,4},{4,5},{5,6},{6,7},{7,8},{8,9},{9,10},{10,1... | collective-permute-start | bytes 589832 | tf_op jit(solution)/shard_map/ppermute | solution.py:554
  25.2 0.0 collective-permute-done.field
  25.2 0.0 collective-permute-done.1.moves
  25.2 0.8 pack_estimate.1
  26.0 5.1 %all-to-all-start.1 = ((f32[8,4,16,128]{3,2,1,0:T(8,128)}), f32[8,4,16,128]{3,2,1,0:T(8,128)S(1)}, u32[]{:S(2)}, u32[]{:S(2)}) async-start(f32[8,4,16,128]{3,2,1,0:T(8,128)} %pack_estimate.1), calls=%async_computation.1 | async-start | bytes 524288 | tf_op jit(solution)/shard_map/all_to_all | solution.py:558
  31.1 0.0 collective-permute-done.3.refs_1_
  31.1 3.0 %collective-permute-done.2.refs_0_ = f32[8,16,384]{2,1,0:T(8,128)S(1)} collective-permute-done((f32[8,16,384]{2,1,0:T(8,128)S(1)}, f32[8,16,384]{2,1,0:T(8,128)S(1)}, u32[]{:S(2)}, u32[]{:S(2)}) %collective-permute-start.2) | collective-permute-done | bytes 196640 | tf_op jit(solution)/shard_map/ppermute | solution.py:554
  34.1 0.0 copy-start
  34.1 2.0 %collective-permute-start.4 = (f32[8,16,384]{2,1,0:T(8,128)S(1)}, f32[8,16,384]{2,1,0:T(8,128)S(1)}, u32[]{:S(2)}, u32[]{:S(2)}) collective-permute-start(f32[8,16,384]{2,1,0:T(8,128)S(1)} %get-tuple-element.24.refs_4_), channel_id=1, source_target_pairs={{0,1},{1,2},{2,3},{3,4},{4,5},{5,6},{6,7},{7,8},{8,9},{9,10},{10,1... | collective-permute-start | bytes 589832 | tf_op jit(solution)/shard_map/ppermute | solution.py:554
  36.2 7.2 %collective-permute-start.5 = (f32[8,16,384]{2,1,0:T(8,128)S(1)}, f32[8,16,384]{2,1,0:T(8,128)S(1)}, u32[]{:S(2)}, u32[]{:S(2)}) collective-permute-start(f32[8,16,384]{2,1,0:T(8,128)S(1)} %get-tuple-element.25.refs_5_), channel_id=1, source_target_pairs={{1,0},{2,1},{3,2},{4,3},{5,4},{6,5},{7,6},{8,7},{9,8},{10,9},{11,1... | collective-permute-start | bytes 589832 | tf_op jit(solution)/shard_map/ppermute | solution.py:554
  43.4 0.0 all-to-all-done.1.refs_1_.refs_2_
  43.4 6.1 %iteration_forward.1 = (f32[8,128,256]{2,1,0:T(8,128)S(1)}, bf16[8,3,256,256]{3,2,1,0:T(8,128)(2,1)S(1)}, bf16[8,3,256,256]{3,2,1,0:T(8,128)(2,1)S(1)}, bf16[8,3...) custom-call(f32[8,16,512]{2,1,0:T(8,128)S(1)} %all-to-all-done.refs_0_, f32[8,4,16,128]{3,2,1,0:T(8,128)S(1)} %all-to-all-done.1.refs_1_.refs_2_), custom_call_target="tpu_custom_call" | custom-call | flops 8000000000 | bytes 1000000 | tf_op jit(solution)/shard_map/iteration_forward/pallas_call | solution.py:527
  49.5 0.0 collective-permute-done.4.refs_3_
  49.5 0.0 collective-permute-done.5.refs_6_
  49.5 0.0 copy-done
  49.6 2.5 %iteration_adjoint.1 = (f32[8,32,128]{2,1,0:T(8,128)S(1)}, bf16[8,96,128]{2,1,0:T(8,128)(2,1)S(1)}, bf16[8,96,128]{2,1,0:T(8,128)(2,1)S(1)}) custom-call(f32[8,16,512]{2,1,0:T(8,128)S(1)} %all-to-all-done.refs_0_, f32[8,4,16,128]{3,2,1,0:T(8,128)S(1)} %all-to-all-done.1.refs_1_.refs_2_, f32[8,128,256]{2,1,0:T(8,128)S(1)} %get-tuple-element.20.refs_2_, ...), custom_call_target="tpu_custom_call" | custom-call | flops 8000000000 | bytes 1000000 | tf_op jit(solution)/shard_map/iteration_adjoint/pallas_call | solution.py:527
  52.1 11.1 %all_to_all.25 = f32[8,32,128]{2,1,0:T(8,128)S(1)} all-to-all(f32[8,32,128]{2,1,0:T(8,128)S(1)} %get-tuple-element.28), channel_id=1, replica_groups=mesh['view'=8,'blk'=64] {'view'}, dimensions={0} | all-to-all | bytes 262144 | tf_op jit(solution)/shard_map/all_to_all | solution.py:558
  63.2 1.9 %collective-permute-start.6 = (f32[8,32,128]{2,1,0:T(8,128)S(1)}, f32[8,32,128]{2,1,0:T(8,128)S(1)}, u32[]{:S(2)}, u32[]{:S(2)}) collective-permute-start(f32[8,32,128]{2,1,0:T(8,128)S(1)} %all_to_all.25), channel_id=1, source_target_pairs={{0,1},{1,2},{2,3},{3,4},{4,5},{5,6},{6,7},{7,8},{8,9},{9,10},{10,1... | collective-permute-start | bytes 393224 | tf_op jit(solution)/shard_map/ppermute | solution.py:548
  65.1 8.3 %collective-permute-done.6.field = f32[8,32,128]{2,1,0:T(8,128)S(1)} collective-permute-done((f32[8,32,128]{2,1,0:T(8,128)S(1)}, f32[8,32,128]{2,1,0:T(8,128)S(1)}, u32[]{:S(2)}, u32[]{:S(2)}) %collective-permute-start.6) | collective-permute-done | bytes 131104 | tf_op jit(solution)/shard_map/ppermute | solution.py:548
  73.3 0.1 pack_field.1
  73.4 11.9 %all_to_all.26.refs_1_ = f32[8,4,16,128]{3,2,1,0:T(8,128)S(1)} all-to-all(f32[8,4,16,128]{3,2,1,0:T(8,128)S(1)} %pack_field.1), channel_id=1, replica_groups=mesh['view'=8,'blk'=64] {'view'}, dimensions={0} | all-to-all | bytes 524288 | tf_op jit(solution)/shard_map/all_to_all | solution.py:558
  85.4 4.4 %iteration_both.1 = f32[8,32,128]{2,1,0:T(8,128)S(1)} custom-call(f32[8,16,512]{2,1,0:T(8,128)S(1)} %all-to-all-done.refs_0_, f32[8,4,16,128]{3,2,1,0:T(8,128)S(1)} %all_to_all.26.refs_1_, f32[8,4,16,128]{3,2,1,0:T(8,128)S(1)} %all-to-all-done.1.refs_1_.refs_2_, f32[8,16,384]{2,1,0:T(8,128)S(1)} %collective-permute-done.4.refs_3_, ...), custom_call_target="tpu_custom_call" | custom-call | flops 8000000000 | bytes 1000000 | tf_op jit(solution)/shard_map/iteration_both/pallas_call | solution.py:527
  89.8 8.5 %all_to_all.27 = f32[8,32,128]{2,1,0:T(8,128)S(1)} all-to-all(f32[8,32,128]{2,1,0:T(8,128)S(1)} %iteration_both.1), channel_id=1, replica_groups=mesh['view'=8,'blk'=64] {'view'}, dimensions={0} | all-to-all | bytes 262144 | tf_op jit(solution)/shard_map/all_to_all | solution.py:558
  98.3 0.7 copy.16
  (3 shorter events, 0.0 us)
Async XLA Ops:
  2.2 11.9 %all-to-all-start = ((f32[8,16,512]{2,1,0:T(8,128)}), f32[8,16,512]{2,1,0:T(8,128)S(1)}, u32[]{:S(2)}, u32[]{:S(2)}) async-start(f32[8,16,512]{2,1,0:T(8,128)} %pack_measured.1), calls=%async_computation | async-start | bytes 524288 | tf_op jit(solution)/shard_map/all_to_all | solution.py:558
  6.5 18.7 %collective-permute-start = (f32[2,16,1024]{2,1,0:T(8,128)}, f32[2,16,1024]{2,1,0:T(8,128)S(1)}, u32[]{:S(2)}, u32[]{:S(2)}) collective-permute-start(f32[2,16,1024]{2,1,0:T(8,128)} %param.12), channel_id=1, source_target_pairs={{0,1},{1,2},{2,3},{3,4},{4,5},{5,6},{6,7},{7,8},{8,9},{9,10},{10,1... | collective-permute-start | bytes 393224 | tf_op jit(solution)/shard_map/ppermute | solution.py:548
  14.1 11.1 %collective-permute-start.1 = (f32[16,128]{1,0:T(8,128)S(1)}, f32[16,128]{1,0:T(8,128)S(1)}, u32[]{:S(2)}, u32[]{:S(2)}) collective-permute-start(f32[16,128]{1,0:T(8,128)S(1)} %slice_reduce_fusion), channel_id=1, source_target_pairs={{0,1},{1,2},{2,3},{3,4},{4,5},{5,6},{6,7},{7,8},{8,9},{9,10},{10,1... | collective-permute-start | bytes 24584 | tf_op jit(solution)/shard_map/ppermute | solution.py:548
  17.6 13.6 %collective-permute-start.3 = (f32[8,16,384]{2,1,0:T(8,128)S(1)}, f32[8,16,384]{2,1,0:T(8,128)S(1)}, u32[]{:S(2)}, u32[]{:S(2)}) collective-permute-start(f32[8,16,384]{2,1,0:T(8,128)S(1)} %slice.9), channel_id=1, source_target_pairs={{1,0},{2,1},{3,2},{4,3},{5,4},{6,5},{7,6},{8,7},{9,8},{10,9},{11,1... | collective-permute-start | bytes 589832 | tf_op jit(solution)/shard_map/ppermute | solution.py:554
  23.2 10.9 %collective-permute-start.2 = (f32[8,16,384]{2,1,0:T(8,128)S(1)}, f32[8,16,384]{2,1,0:T(8,128)S(1)}, u32[]{:S(2)}, u32[]{:S(2)}) collective-permute-start(f32[8,16,384]{2,1,0:T(8,128)S(1)} %slice.9), channel_id=1, source_target_pairs={{0,1},{1,2},{2,3},{3,4},{4,5},{5,6},{6,7},{7,8},{8,9},{9,10},{10,1... | collective-permute-start | bytes 589832 | tf_op jit(solution)/shard_map/ppermute | solution.py:554
  26.0 17.4 %all-to-all-start.1 = ((f32[8,4,16,128]{3,2,1,0:T(8,128)}), f32[8,4,16,128]{3,2,1,0:T(8,128)S(1)}, u32[]{:S(2)}, u32[]{:S(2)}) async-start(f32[8,4,16,128]{3,2,1,0:T(8,128)} %pack_estimate.1), calls=%async_computation.1 | async-start | bytes 524288 | tf_op jit(solution)/shard_map/all_to_all | solution.py:558
  34.1 15.4 %copy-start = (f32[8,8,1024]{2,1,0:T(8,128)S(1)}, f32[8,8,1024]{2,1,0:T(8,128)}, u32[]{:S(2)}) copy-start(f32[8,8,1024]{2,1,0:T(8,128)} %refs_7_.5) | copy-start | bytes 786436
  34.1 15.4 %collective-permute-start.4 = (f32[8,16,384]{2,1,0:T(8,128)S(1)}, f32[8,16,384]{2,1,0:T(8,128)S(1)}, u32[]{:S(2)}, u32[]{:S(2)}) collective-permute-start(f32[8,16,384]{2,1,0:T(8,128)S(1)} %get-tuple-element.24.refs_4_), channel_id=1, source_target_pairs={{0,1},{1,2},{2,3},{3,4},{4,5},{5,6},{6,7},{7,8},{8,9},{9,10},{10,1... | collective-permute-start | bytes 589832 | tf_op jit(solution)/shard_map/ppermute | solution.py:554
  36.2 13.4 %collective-permute-start.5 = (f32[8,16,384]{2,1,0:T(8,128)S(1)}, f32[8,16,384]{2,1,0:T(8,128)S(1)}, u32[]{:S(2)}, u32[]{:S(2)}) collective-permute-start(f32[8,16,384]{2,1,0:T(8,128)S(1)} %get-tuple-element.25.refs_5_), channel_id=1, source_target_pairs={{1,0},{2,1},{3,2},{4,3},{5,4},{6,5},{7,6},{8,7},{9,8},{10,9},{11,1... | collective-permute-start | bytes 589832 | tf_op jit(solution)/shard_map/ppermute | solution.py:554
  63.2 10.2 %collective-permute-start.6 = (f32[8,32,128]{2,1,0:T(8,128)S(1)}, f32[8,32,128]{2,1,0:T(8,128)S(1)}, u32[]{:S(2)}, u32[]{:S(2)}) collective-permute-start(f32[8,32,128]{2,1,0:T(8,128)S(1)} %all_to_all.25), channel_id=1, source_target_pairs={{0,1},{1,2},{2,3},{3,4},{4,5},{5,6},{6,7},{7,8},{8,9},{9,10},{10,1... | collective-permute-start | bytes 393224 | tf_op jit(solution)/shard_map/ppermute | solution.py:548

commit v7 on v6

--- a/solution.py
+++ b/solution.py
@@ -342,6 +342,7 @@
 
     strip = lax.axis_index("view")
     block = lax.axis_index("blk")
+    even = block % 2 == 0
     first_column = pl.multiple_of(strip * LANE, LANE)
 
     def stash(view):
@@ -413,14 +414,24 @@
         quotients = [None] * 8
         lower = lanes_of((ROWS, LANE)) < HALF
         for place in range(4):
-            seen = [
-                jnp.where(
-                    phase == 1,
-                    sides[place + 1][view, :, tile * LANE : (tile + 1) * LANE],
-                    sides[place][view, :, tile * LANE : (tile + 1) * LANE],
+            seen = []
+            for tile in range(3):
+                columns = slice(tile * LANE, (tile + 1) * LANE)
+                seen.append(
+                    jnp.where(
+                        even,
+                        jnp.where(
+                            phase == 1,
+                            sides[place + 1][view, :, columns],
+                            sides[place][view, :, columns],
+                        ),
+                        jnp.where(
+                            phase == 1,
+                            sides[3 - place][view, :, columns],
+                            sides[4 - place][view, :, columns],
+                        ),
+                    )
                 )
-                for tile in range(3)
-            ]
             edges = (seen[2], pltpu.roll(seen[2], HALF, 1))
             row_block = block - 2 + phase + place
             fine = kept & (row_block >= 0) & (row_block < VIEWS * 8)
@@ -548,9 +559,11 @@
     return lax.ppermute(values, ("view", "blk"), route)
 
 
-def from_block(values, offset):
+def with_neighbour(values, first):
     blocks = lax.axis_size("blk")
-    route = [(b + offset, b) for b in range(blocks) if 0 <= b + offset < blocks]
+    route = []
+    for block in range(first, blocks - 1, 2):
+        route += [(block, block + 1), (block + 1, block)]
     return lax.ppermute(values, "blk", route)
 
 
@@ -580,11 +593,10 @@
     moves = jnp.sum(received[:, :, SEEN:], axis=0)
     moves, seen = lax.optimization_barrier((moves, received[:, :, :SEEN]))
     packed = pack_estimate(stepped, step_by_view(moves))
-    near = [from_block(seen, offset) for offset in (-1, 1)]
-    near = hand_on(near)
+    near = hand_on([with_neighbour(seen, first) for first in (0, 1)])
     _, *relayed = lax.optimization_barrier((packed, *near))
-    far = [from_block(values, offset) for values, offset in zip(relayed, (-1, 1))]
-    sides = [far[0], near[0], near[1], far[1]]
+    far = [with_neighbour(relayed[1 - first], first) for first in (0, 1)]
+    sides = [far[1], near[1], near[0], far[0]]
     field = over_views(packed)
     moves = field
     blurred, *bands = iteration("forward", [received, field])

time: 99.6 us -> 94.9 us (0.953)
  the two profiles are of different devices: /device:TPU:256 before, /device:TPU:264 now
where the time goes in v7:
time: 94.9 us; the launch traced here: 94.3 us
  blocking collectives  34.5 us (36%)
  starting transfers between devices  33.7 us (36%)
  Pallas kernels  16.1 us (17%)
  waiting for transfers between devices  9.14 us (10%)
    all_to_all x3, blocking collectives, over_views(): return lax.all_to_all(values, 'view', 0, 0)  34.5 us
    ppermute x4, starting transfers between devices, with_neighbour(): return lax.ppermute(values, 'blk', route)  14.2 us
    pallas_call x3, Pallas kernels, iteration(): pl.pallas_call(lambda *refs: iteration_kernel(mode, *refs), out_shape=out...  13.1 us
    ppermute x3, starting transfers between devices, step_by_view(): return lax.ppermute(values, ('view', 'blk'), route)  10 us
    all_to_all x2, starting transfers between devices, over_views(): return lax.all_to_all(values, 'view', 0, 0)  9.44 us
    all_to_all x2, waiting for transfers between devices, over_views(): return lax.all_to_all(values, 'view', 0, 0)  5.34 us
    ppermute x3, waiting for transfers between devices, step_by_view(): return lax.ppermute(values, ('view', 'blk'), route)  3.79 us
    pallas_call x1, Pallas kernels, pack_measured(): pl.pallas_call(pack_measured_kernel, out_shape=jax.ShapeDtypeStruct((VIEW...  2.16 us
  transfers between devices with their start and end apart: 9, of which 3 were waited for; matrix products, arithmetic and copies ran while one was open for 0% of the time, Pallas kernels for 7%

profile of v7, /device:TPU:264, one launch (start us, length us, event | category | flops | bytes accessed | tf_op | source)
XLA Modules:
  0.0 94.3 jit_solution(10275835956964844696)
XLA Ops:
  0.0 2.2 %pack_measured.1 = f32[8,16,512]{2,1,0:T(8,128)} custom-call(f32[1,2,16,1024]{3,2,1,0:T(8,128)} %refs_0_.1, s32[1,16]{1,0:T(1,128)} %refs_1_.1, s32[1,16]{1,0:T(1,128)} %refs_2_.1, s32[1,2]{1,0:T(1,128)} %refs_3_.1, f32[3,1,31]{2,1,0:T(1,128)} %bitcast.11, f32[3,1,31]{2,1,0:T(1,128)} %bitcast.12, f32[3,1,31]{2,1,0:T(1,128)} %bitcast.13, f32[1,3]{1,0:T(1,128)} %refs_7_.3), custom_call_target="tpu_custom_call" | custom-call | tf_op jit(solution)/shard_map/pack_measured/pallas_call | solution.py:155
  2.2 4.3 %all-to-all-start = ((f32[8,16,512]{2,1,0:T(8,128)}), f32[8,16,512]{2,1,0:T(8,128)S(1)}, u32[]{:S(2)}, u32[]{:S(2)}) async-start(f32[8,16,512]{2,1,0:T(8,128)} %pack_measured.1), calls=%async_computation | async-start | bytes 524288 | tf_op jit(solution)/shard_map/all_to_all | solution.py:571
  6.5 3.5 %collective-permute-start = (f32[2,16,1024]{2,1,0:T(8,128)}, f32[2,16,1024]{2,1,0:T(8,128)S(1)}, u32[]{:S(2)}, u32[]{:S(2)}) collective-permute-start(f32[2,16,1024]{2,1,0:T(8,128)} %param.12), channel_id=1, source_target_pairs={{0,1},{1,2},{2,3},{3,4},{4,5},{5,6},{6,7},{7,8},{8,9},{9,10},{10,1... | collective-permute-start | bytes 393224 | tf_op jit(solution)/shard_map/ppermute | solution.py:559
  10.0 4.1 %all-to-all-done.refs_0_ = f32[8,16,512]{2,1,0:T(8,128)S(1)} async-done(((f32[8,16,512]{2,1,0:T(8,128)}), f32[8,16,512]{2,1,0:T(8,128)S(1)}, u32[]{:S(2)}, u32[]{:S(2)}) %all-to-all-start) | async-done | bytes 262176 | tf_op jit(solution)/shard_map/all_to_all | solution.py:571
  14.1 3.5 %collective-permute-start.1 = (f32[16,128]{1,0:T(8,128)S(1)}, f32[16,128]{1,0:T(8,128)S(1)}, u32[]{:S(2)}, u32[]{:S(2)}) collective-permute-start(f32[16,128]{1,0:T(8,128)S(1)} %slice_reduce_fusion), channel_id=1, source_target_pairs={{0,1},{1,2},{2,3},{3,4},{4,5},{5,6},{6,7},{7,8},{8,9},{9,10},{10,1... | collective-permute-start | bytes 24584 | tf_op jit(solution)/shard_map/ppermute | solution.py:559
  17.6 3.5 %collective-permute-start.3 = (f32[8,16,384]{2,1,0:T(8,128)S(1)}, f32[8,16,384]{2,1,0:T(8,128)S(1)}, u32[]{:S(2)}, u32[]{:S(2)}) collective-permute-start(f32[8,16,384]{2,1,0:T(8,128)S(1)} %slice.9), channel_id=1, source_target_pairs={{1,2},{2,1},{3,4},{4,3},{5,6},{6,5},{7,8},{8,7},{9,10},{10,9},{11,... | collective-permute-start | bytes 589832 | tf_op jit(solution)/shard_map/ppermute | solution.py:567
  21.1 4.6 %collective-permute-start.2 = (f32[8,16,384]{2,1,0:T(8,128)S(1)}, f32[8,16,384]{2,1,0:T(8,128)S(1)}, u32[]{:S(2)}, u32[]{:S(2)}) collective-permute-start(f32[8,16,384]{2,1,0:T(8,128)S(1)} %slice.9), channel_id=1, source_target_pairs={{0,1},{1,0},{2,3},{3,2},{4,5},{5,4},{6,7},{7,6},{8,9},{9,8},{10,11... | collective-permute-start | bytes 589832 | tf_op jit(solution)/shard_map/ppermute | solution.py:567
  25.6 0.0 collective-permute-done.field
  25.6 0.0 collective-permute-done.1.moves
  25.6 0.8 pack_estimate.1
  26.4 5.1 %all-to-all-start.1 = ((f32[8,4,16,128]{3,2,1,0:T(8,128)}), f32[8,4,16,128]{3,2,1,0:T(8,128)S(1)}, u32[]{:S(2)}, u32[]{:S(2)}) async-start(f32[8,4,16,128]{3,2,1,0:T(8,128)} %pack_estimate.1), calls=%async_computation.1 | async-start | bytes 524288 | tf_op jit(solution)/shard_map/all_to_all | solution.py:571
  31.6 0.0 collective-permute-done.3.refs_1_
  31.6 0.0 collective-permute-done.2.refs_0_
  31.6 0.0 copy-start
  31.6 2.1 %collective-permute-start.4 = (f32[8,16,384]{2,1,0:T(8,128)S(1)}, f32[8,16,384]{2,1,0:T(8,128)S(1)}, u32[]{:S(2)}, u32[]{:S(2)}) collective-permute-start(f32[8,16,384]{2,1,0:T(8,128)S(1)} %get-tuple-element.24.refs_5_), channel_id=1, source_target_pairs={{1,2},{2,1},{3,4},{4,3},{5,6},{6,5},{7,8},{8,7},{9,10},{10,9},{11,... | collective-permute-start | bytes 589832 | tf_op jit(solution)/shard_map/ppermute | solution.py:567
  33.7 4.1 %collective-permute-start.5 = (f32[8,16,384]{2,1,0:T(8,128)S(1)}, f32[8,16,384]{2,1,0:T(8,128)S(1)}, u32[]{:S(2)}, u32[]{:S(2)}) collective-permute-start(f32[8,16,384]{2,1,0:T(8,128)S(1)} %get-tuple-element.25.refs_4_), channel_id=1, source_target_pairs={{0,1},{1,0},{2,3},{3,2},{4,5},{5,4},{6,7},{7,6},{8,9},{9,8},{10,11... | collective-permute-start | bytes 589832 | tf_op jit(solution)/shard_map/ppermute | solution.py:567
  37.8 1.3 %all-to-all-done.1.refs_1_.refs_2_ = f32[8,4,16,128]{3,2,1,0:T(8,128)S(1)} async-done(((f32[8,4,16,128]{3,2,1,0:T(8,128)}), f32[8,4,16,128]{3,2,1,0:T(8,128)S(1)}, u32[]{:S(2)}, u32[]{:S(2)}) %all-to-all-start.1) | async-done | bytes 262176 | tf_op jit(solution)/shard_map/all_to_all | solution.py:571
  39.1 6.1 %iteration_forward.1 = (f32[8,128,256]{2,1,0:T(8,128)S(1)}, bf16[8,3,256,256]{3,2,1,0:T(8,128)(2,1)S(1)}, bf16[8,3,256,256]{3,2,1,0:T(8,128)(2,1)S(1)}, bf16[8,3...) custom-call(f32[8,16,512]{2,1,0:T(8,128)S(1)} %all-to-all-done.refs_0_, f32[8,4,16,128]{3,2,1,0:T(8,128)S(1)} %all-to-all-done.1.refs_1_.refs_2_), custom_call_target="tpu_custom_call" | custom-call | flops 8000000000 | bytes 1000000 | tf_op jit(solution)/shard_map/iteration_forward/pallas_call | solution.py:538
  45.2 0.0 collective-permute-done.4.refs_3_
  45.2 0.0 collective-permute-done.5.refs_6_
  45.2 0.0 copy-done
  45.2 2.6 %iteration_adjoint.1 = (f32[8,32,128]{2,1,0:T(8,128)S(1)}, bf16[8,96,128]{2,1,0:T(8,128)(2,1)S(1)}, bf16[8,96,128]{2,1,0:T(8,128)(2,1)S(1)}) custom-call(f32[8,16,512]{2,1,0:T(8,128)S(1)} %all-to-all-done.refs_0_, f32[8,4,16,128]{3,2,1,0:T(8,128)S(1)} %all-to-all-done.1.refs_1_.refs_2_, f32[8,128,256]{2,1,0:T(8,128)S(1)} %get-tuple-element.20.refs_2_, ...), custom_call_target="tpu_custom_call" | custom-call | flops 8000000000 | bytes 1000000 | tf_op jit(solution)/shard_map/iteration_adjoint/pallas_call | solution.py:538
  47.8 8.6 %all_to_all.25 = f32[8,32,128]{2,1,0:T(8,128)S(1)} all-to-all(f32[8,32,128]{2,1,0:T(8,128)S(1)} %get-tuple-element.28), channel_id=1, replica_groups=mesh['view'=8,'blk'=64] {'view'}, dimensions={0} | all-to-all | bytes 262144 | tf_op jit(solution)/shard_map/all_to_all | solution.py:571
  56.4 3.1 %collective-permute-start.6 = (f32[8,32,128]{2,1,0:T(8,128)S(1)}, f32[8,32,128]{2,1,0:T(8,128)S(1)}, u32[]{:S(2)}, u32[]{:S(2)}) collective-permute-start(f32[8,32,128]{2,1,0:T(8,128)S(1)} %all_to_all.25), channel_id=1, source_target_pairs={{0,1},{1,2},{2,3},{3,4},{4,5},{5,6},{6,7},{7,8},{8,9},{9,10},{10,1... | collective-permute-start | bytes 393224 | tf_op jit(solution)/shard_map/ppermute | solution.py:559
  59.5 3.8 %collective-permute-done.6.field = f32[8,32,128]{2,1,0:T(8,128)S(1)} collective-permute-done((f32[8,32,128]{2,1,0:T(8,128)S(1)}, f32[8,32,128]{2,1,0:T(8,128)S(1)}, u32[]{:S(2)}, u32[]{:S(2)}) %collective-permute-start.6) | collective-permute-done | bytes 131104 | tf_op jit(solution)/shard_map/ppermute | solution.py:559
  63.2 0.1 pack_field.1
  63.3 17.4 %all_to_all.26.refs_1_ = f32[8,4,16,128]{3,2,1,0:T(8,128)S(1)} all-to-all(f32[8,4,16,128]{3,2,1,0:T(8,128)S(1)} %pack_field.1), channel_id=1, replica_groups=mesh['view'=8,'blk'=64] {'view'}, dimensions={0} | all-to-all | bytes 524288 | tf_op jit(solution)/shard_map/all_to_all | solution.py:571
  80.7 4.4 %iteration_both.1 = f32[8,32,128]{2,1,0:T(8,128)S(1)} custom-call(f32[8,16,512]{2,1,0:T(8,128)S(1)} %all-to-all-done.refs_0_, f32[8,4,16,128]{3,2,1,0:T(8,128)S(1)} %all_to_all.26.refs_1_, f32[8,4,16,128]{3,2,1,0:T(8,128)S(1)} %all-to-all-done.1.refs_1_.refs_2_, f32[8,16,384]{2,1,0:T(8,128)S(1)} %collective-permute-done.4.refs_3_, ...), custom_call_target="tpu_custom_call" | custom-call | flops 8000000000 | bytes 1000000 | tf_op jit(solution)/shard_map/iteration_both/pallas_call | solution.py:538
  85.1 8.5 %all_to_all.27 = f32[8,32,128]{2,1,0:T(8,128)S(1)} all-to-all(f32[8,32,128]{2,1,0:T(8,128)S(1)} %iteration_both.1), channel_id=1, replica_groups=mesh['view'=8,'blk'=64] {'view'}, dimensions={0} | all-to-all | bytes 262144 | tf_op jit(solution)/shard_map/all_to_all | solution.py:571
  93.6 0.7 copy.16
  (3 shorter events, 0.0 us)
Async XLA Ops:
  2.2 11.9 %all-to-all-start = ((f32[8,16,512]{2,1,0:T(8,128)}), f32[8,16,512]{2,1,0:T(8,128)S(1)}, u32[]{:S(2)}, u32[]{:S(2)}) async-start(f32[8,16,512]{2,1,0:T(8,128)} %pack_measured.1), calls=%async_computation | async-start | bytes 524288 | tf_op jit(solution)/shard_map/all_to_all | solution.py:571
  6.5 19.1 %collective-permute-start = (f32[2,16,1024]{2,1,0:T(8,128)}, f32[2,16,1024]{2,1,0:T(8,128)S(1)}, u32[]{:S(2)}, u32[]{:S(2)}) collective-permute-start(f32[2,16,1024]{2,1,0:T(8,128)} %param.12), channel_id=1, source_target_pairs={{0,1},{1,2},{2,3},{3,4},{4,5},{5,6},{6,7},{7,8},{8,9},{9,10},{10,1... | collective-permute-start | bytes 393224 | tf_op jit(solution)/shard_map/ppermute | solution.py:559
  14.1 11.6 %collective-permute-start.1 = (f32[16,128]{1,0:T(8,128)S(1)}, f32[16,128]{1,0:T(8,128)S(1)}, u32[]{:S(2)}, u32[]{:S(2)}) collective-permute-start(f32[16,128]{1,0:T(8,128)S(1)} %slice_reduce_fusion), channel_id=1, source_target_pairs={{0,1},{1,2},{2,3},{3,4},{4,5},{5,6},{6,7},{7,8},{8,9},{9,10},{10,1... | collective-permute-start | bytes 24584 | tf_op jit(solution)/shard_map/ppermute | solution.py:559
  17.6 14.0 %collective-permute-start.3 = (f32[8,16,384]{2,1,0:T(8,128)S(1)}, f32[8,16,384]{2,1,0:T(8,128)S(1)}, u32[]{:S(2)}, u32[]{:S(2)}) collective-permute-start(f32[8,16,384]{2,1,0:T(8,128)S(1)} %slice.9), channel_id=1, source_target_pairs={{1,2},{2,1},{3,4},{4,3},{5,6},{6,5},{7,8},{8,7},{9,10},{10,9},{11,... | collective-permute-start | bytes 589832 | tf_op jit(solution)/shard_map/ppermute | solution.py:567
  21.1 10.5 %collective-permute-start.2 = (f32[8,16,384]{2,1,0:T(8,128)S(1)}, f32[8,16,384]{2,1,0:T(8,128)S(1)}, u32[]{:S(2)}, u32[]{:S(2)}) collective-permute-start(f32[8,16,384]{2,1,0:T(8,128)S(1)} %slice.9), channel_id=1, source_target_pairs={{0,1},{1,0},{2,3},{3,2},{4,5},{5,4},{6,7},{7,6},{8,9},{9,8},{10,11... | collective-permute-start | bytes 589832 | tf_op jit(solution)/shard_map/ppermute | solution.py:567
  26.4 12.7 %all-to-all-start.1 = ((f32[8,4,16,128]{3,2,1,0:T(8,128)}), f32[8,4,16,128]{3,2,1,0:T(8,128)S(1)}, u32[]{:S(2)}, u32[]{:S(2)}) async-start(f32[8,4,16,128]{3,2,1,0:T(8,128)} %pack_estimate.1), calls=%async_computation.1 | async-start | bytes 524288 | tf_op jit(solution)/shard_map/all_to_all | solution.py:571
  31.6 13.6 %copy-start = (f32[8,8,1024]{2,1,0:T(8,128)S(1)}, f32[8,8,1024]{2,1,0:T(8,128)}, u32[]{:S(2)}) copy-start(f32[8,8,1024]{2,1,0:T(8,128)} %refs_7_.5) | copy-start | bytes 786436
  31.6 13.6 %collective-permute-start.4 = (f32[8,16,384]{2,1,0:T(8,128)S(1)}, f32[8,16,384]{2,1,0:T(8,128)S(1)}, u32[]{:S(2)}, u32[]{:S(2)}) collective-permute-start(f32[8,16,384]{2,1,0:T(8,128)S(1)} %get-tuple-element.24.refs_5_), channel_id=1, source_target_pairs={{1,2},{2,1},{3,4},{4,3},{5,6},{6,5},{7,8},{8,7},{9,10},{10,9},{11,... | collective-permute-start | bytes 589832 | tf_op jit(solution)/shard_map/ppermute | solution.py:567
  33.7 11.5 %collective-permute-start.5 = (f32[8,16,384]{2,1,0:T(8,128)S(1)}, f32[8,16,384]{2,1,0:T(8,128)S(1)}, u32[]{:S(2)}, u32[]{:S(2)}) collective-permute-start(f32[8,16,384]{2,1,0:T(8,128)S(1)} %get-tuple-element.25.refs_4_), channel_id=1, source_target_pairs={{0,1},{1,0},{2,3},{3,2},{4,5},{5,4},{6,7},{7,6},{8,9},{9,8},{10,11... | collective-permute-start | bytes 589832 | tf_op jit(solution)/shard_map/ppermute | solution.py:567
  56.4 6.8 %collective-permute-start.6 = (f32[8,32,128]{2,1,0:T(8,128)S(1)}, f32[8,32,128]{2,1,0:T(8,128)S(1)}, u32[]{:S(2)}, u32[]{:S(2)}) collective-permute-start(f32[8,32,128]{2,1,0:T(8,128)S(1)} %all_to_all.25), channel_id=1, source_target_pairs={{0,1},{1,2},{2,3},{3,4},{4,5},{5,6},{6,7},{7,8},{8,9},{9,10},{10,1... | collective-permute-start | bytes 393224 | tf_op jit(solution)/shard_map/ppermute | solution.py:559

commit v8 on v7

--- a/solution.py
+++ b/solution.py
@@ -17,7 +17,7 @@
 TILE_LANE = 2 * 8
 ROW_MARK = 1024
 Q_FIRST, Q_LAST = 41, 214
-STEPS = (1, -1, 2, -2, 3, -3, 0, 0)
+STEPS = (1, 1, 2, 2, 3, 3, 0, 0)
 OWN = 6
 SEEN = 3 * LANE
 F32 = jnp.float32
@@ -553,9 +553,13 @@
     blocks = lax.axis_size("blk")
     route = []
     for view, step in enumerate(STEPS):
-        for block in range(blocks):
-            if 0 <= block + step < blocks:
-                route.append((view * blocks + block, view * blocks + block + step))
+        here = view * blocks
+        if step == 0:
+            route += [(here + block, here + block) for block in range(blocks)]
+            continue
+        for block in range(blocks - step):
+            if (block // step) % 2 == view % 2:
+                route += [(here + block, here + block + step), (here + block + step, here + block)]
     return lax.ppermute(values, ("view", "blk"), route)
 
 

time: 94.9 us -> 94.4 us (level)
  the two profiles are of different devices: /device:TPU:264 before, /device:TPU:240 now
where the time goes in v8:
time: 94.4 us; the launch traced here: 93.8 us
  blocking collectives  34.8 us (37%)
  starting transfers between devices  32.2 us (34%)
  Pallas kernels  16.1 us (17%)
  waiting for transfers between devices  9.8 us (10%)
    all_to_all x3, blocking collectives, over_views(): return lax.all_to_all(values, 'view', 0, 0)  34.8 us
    ppermute x4, starting transfers between devices, with_neighbour(): return lax.ppermute(values, 'blk', route)  16.6 us
    pallas_call x3, Pallas kernels, iteration(): pl.pallas_call(lambda *refs: iteration_kernel(mode, *refs), out_shape=out...  13.1 us
    all_to_all x2, starting transfers between devices, over_views(): return lax.all_to_all(values, 'view', 0, 0)  8.01 us
    ppermute x3, starting transfers between devices, step_by_view(): return lax.ppermute(values, ('view', 'blk'), route)  7.58 us
    all_to_all x2, waiting for transfers between devices, over_views(): return lax.all_to_all(values, 'view', 0, 0)  4.96 us
    ppermute x3, waiting for transfers between devices, step_by_view(): return lax.ppermute(values, ('view', 'blk'), route)  4.43 us
    pallas_call x1, Pallas kernels, pack_measured(): pl.pallas_call(pack_measured_kernel, out_shape=jax.ShapeDtypeStruct((VIEW...  2.16 us
  transfers between devices with their start and end apart: 9, of which 3 were waited for; matrix products, arithmetic and copies ran while one was open for 0% of the time, Pallas kernels for 7%

profile of v8, /device:TPU:240, one launch (start us, length us, event | category | flops | bytes accessed | tf_op | source)
XLA Modules:
  0.0 93.8 jit_solution(12788900840856666626)
XLA Ops:
  0.0 2.2 %pack_measured.1 = f32[8,16,512]{2,1,0:T(8,128)} custom-call(f32[1,2,16,1024]{3,2,1,0:T(8,128)} %refs_0_.1, s32[1,16]{1,0:T(1,128)} %refs_1_.1, s32[1,16]{1,0:T(1,128)} %refs_2_.1, s32[1,2]{1,0:T(1,128)} %refs_3_.1, f32[3,1,31]{2,1,0:T(1,128)} %bitcast.11, f32[3,1,31]{2,1,0:T(1,128)} %bitcast.12, f32[3,1,31]{2,1,0:T(1,128)} %bitcast.13, f32[1,3]{1,0:T(1,128)} %refs_7_.3), custom_call_target="tpu_custom_call" | custom-call | tf_op jit(solution)/shard_map/pack_measured/pallas_call | solution.py:155
  2.2 4.3 %all-to-all-start = ((f32[8,16,512]{2,1,0:T(8,128)}), f32[8,16,512]{2,1,0:T(8,128)S(1)}, u32[]{:S(2)}, u32[]{:S(2)}) async-start(f32[8,16,512]{2,1,0:T(8,128)} %pack_measured.1), calls=%async_computation | async-start | bytes 524288 | tf_op jit(solution)/shard_map/all_to_all | solution.py:575
  6.5 2.6 %collective-permute-start = (f32[2,16,1024]{2,1,0:T(8,128)}, f32[2,16,1024]{2,1,0:T(8,128)S(1)}, u32[]{:S(2)}, u32[]{:S(2)}) collective-permute-start(f32[2,16,1024]{2,1,0:T(8,128)} %param.12), channel_id=1, source_target_pairs={{0,1},{1,0},{2,3},{3,2},{4,5},{5,4},{6,7},{7,6},{8,9},{9,8},{10,11... | collective-permute-start | bytes 393224 | tf_op jit(solution)/shard_map/ppermute | solution.py:563
  9.1 5.0 %all-to-all-done.refs_0_ = f32[8,16,512]{2,1,0:T(8,128)S(1)} async-done(((f32[8,16,512]{2,1,0:T(8,128)}), f32[8,16,512]{2,1,0:T(8,128)S(1)}, u32[]{:S(2)}, u32[]{:S(2)}) %all-to-all-start) | async-done | bytes 262176 | tf_op jit(solution)/shard_map/all_to_all | solution.py:575
  14.1 2.6 %collective-permute-start.1 = (f32[16,128]{1,0:T(8,128)S(1)}, f32[16,128]{1,0:T(8,128)S(1)}, u32[]{:S(2)}, u32[]{:S(2)}) collective-permute-start(f32[16,128]{1,0:T(8,128)S(1)} %slice_reduce_fusion), channel_id=1, source_target_pairs={{0,1},{1,0},{2,3},{3,2},{4,5},{5,4},{6,7},{7,6},{8,9},{9,8},{10,11... | collective-permute-start | bytes 24584 | tf_op jit(solution)/shard_map/ppermute | solution.py:563
  16.7 3.9 %collective-permute-start.3 = (f32[8,16,384]{2,1,0:T(8,128)S(1)}, f32[8,16,384]{2,1,0:T(8,128)S(1)}, u32[]{:S(2)}, u32[]{:S(2)}) collective-permute-start(f32[8,16,384]{2,1,0:T(8,128)S(1)} %slice.9), channel_id=1, source_target_pairs={{1,2},{2,1},{3,4},{4,3},{5,6},{6,5},{7,8},{8,7},{9,10},{10,9},{11,... | collective-permute-start | bytes 589832 | tf_op jit(solution)/shard_map/ppermute | solution.py:571
  20.6 4.3 %collective-permute-start.2 = (f32[8,16,384]{2,1,0:T(8,128)S(1)}, f32[8,16,384]{2,1,0:T(8,128)S(1)}, u32[]{:S(2)}, u32[]{:S(2)}) collective-permute-start(f32[8,16,384]{2,1,0:T(8,128)S(1)} %slice.9), channel_id=1, source_target_pairs={{0,1},{1,0},{2,3},{3,2},{4,5},{5,4},{6,7},{7,6},{8,9},{9,8},{10,11... | collective-permute-start | bytes 589832 | tf_op jit(solution)/shard_map/ppermute | solution.py:571
  24.9 0.0 collective-permute-done.field
  24.9 0.0 collective-permute-done.1.moves
  24.9 0.8 pack_estimate.1
  25.7 3.7 %all-to-all-start.1 = ((f32[8,4,16,128]{3,2,1,0:T(8,128)}), f32[8,4,16,128]{3,2,1,0:T(8,128)S(1)}, u32[]{:S(2)}, u32[]{:S(2)}) async-start(f32[8,4,16,128]{3,2,1,0:T(8,128)} %pack_estimate.1), calls=%async_computation.1 | async-start | bytes 524288 | tf_op jit(solution)/shard_map/all_to_all | solution.py:575
  29.4 0.0 collective-permute-done.3.refs_1_
  29.4 0.4 collective-permute-done.2.refs_0_
  29.8 0.0 copy-start
  29.8 2.0 %collective-permute-start.4 = (f32[8,16,384]{2,1,0:T(8,128)S(1)}, f32[8,16,384]{2,1,0:T(8,128)S(1)}, u32[]{:S(2)}, u32[]{:S(2)}) collective-permute-start(f32[8,16,384]{2,1,0:T(8,128)S(1)} %get-tuple-element.24.refs_5_), channel_id=1, source_target_pairs={{1,2},{2,1},{3,4},{4,3},{5,6},{6,5},{7,8},{8,7},{9,10},{10,9},{11,... | collective-permute-start | bytes 589832 | tf_op jit(solution)/shard_map/ppermute | solution.py:571
  31.9 6.4 %collective-permute-start.5 = (f32[8,16,384]{2,1,0:T(8,128)S(1)}, f32[8,16,384]{2,1,0:T(8,128)S(1)}, u32[]{:S(2)}, u32[]{:S(2)}) collective-permute-start(f32[8,16,384]{2,1,0:T(8,128)S(1)} %get-tuple-element.25.refs_4_), channel_id=1, source_target_pairs={{0,1},{1,0},{2,3},{3,2},{4,5},{5,4},{6,7},{7,6},{8,9},{9,8},{10,11... | collective-permute-start | bytes 589832 | tf_op jit(solution)/shard_map/ppermute | solution.py:571
  38.3 0.0 all-to-all-done.1.refs_1_.refs_2_
  38.3 6.1 %iteration_forward.1 = (f32[8,128,256]{2,1,0:T(8,128)S(1)}, bf16[8,3,256,256]{3,2,1,0:T(8,128)(2,1)S(1)}, bf16[8,3,256,256]{3,2,1,0:T(8,128)(2,1)S(1)}, bf16[8,3...) custom-call(f32[8,16,512]{2,1,0:T(8,128)S(1)} %all-to-all-done.refs_0_, f32[8,4,16,128]{3,2,1,0:T(8,128)S(1)} %all-to-all-done.1.refs_1_.refs_2_), custom_call_target="tpu_custom_call" | custom-call | flops 8000000000 | bytes 1000000 | tf_op jit(solution)/shard_map/iteration_forward/pallas_call | solution.py:538
  44.4 0.0 collective-permute-done.4.refs_3_
  44.4 0.0 collective-permute-done.5.refs_6_
  44.4 0.0 copy-done
  44.4 2.6 %iteration_adjoint.1 = (f32[8,32,128]{2,1,0:T(8,128)S(1)}, bf16[8,96,128]{2,1,0:T(8,128)(2,1)S(1)}, bf16[8,96,128]{2,1,0:T(8,128)(2,1)S(1)}) custom-call(f32[8,16,512]{2,1,0:T(8,128)S(1)} %all-to-all-done.refs_0_, f32[8,4,16,128]{3,2,1,0:T(8,128)S(1)} %all-to-all-done.1.refs_1_.refs_2_, f32[8,128,256]{2,1,0:T(8,128)S(1)} %get-tuple-element.20.refs_2_, ...), custom_call_target="tpu_custom_call" | custom-call | flops 8000000000 | bytes 1000000 | tf_op jit(solution)/shard_map/iteration_adjoint/pallas_call | solution.py:538
  47.0 10.1 %all_to_all.25 = f32[8,32,128]{2,1,0:T(8,128)S(1)} all-to-all(f32[8,32,128]{2,1,0:T(8,128)S(1)} %get-tuple-element.28), channel_id=1, replica_groups=mesh['view'=8,'blk'=64] {'view'}, dimensions={0} | all-to-all | bytes 262144 | tf_op jit(solution)/shard_map/all_to_all | solution.py:575
  57.0 2.4 %collective-permute-start.6 = (f32[8,32,128]{2,1,0:T(8,128)S(1)}, f32[8,32,128]{2,1,0:T(8,128)S(1)}, u32[]{:S(2)}, u32[]{:S(2)}) collective-permute-start(f32[8,32,128]{2,1,0:T(8,128)S(1)} %all_to_all.25), channel_id=1, source_target_pairs={{0,1},{1,0},{2,3},{3,2},{4,5},{5,4},{6,7},{7,6},{8,9},{9,8},{10,11... | collective-permute-start | bytes 393224 | tf_op jit(solution)/shard_map/ppermute | solution.py:563
  59.5 4.4 %collective-permute-done.6.field = f32[8,32,128]{2,1,0:T(8,128)S(1)} collective-permute-done((f32[8,32,128]{2,1,0:T(8,128)S(1)}, f32[8,32,128]{2,1,0:T(8,128)S(1)}, u32[]{:S(2)}, u32[]{:S(2)}) %collective-permute-start.6) | collective-permute-done | bytes 131104 | tf_op jit(solution)/shard_map/ppermute | solution.py:563
  63.9 0.1 pack_field.1
  64.0 16.2 %all_to_all.26.refs_1_ = f32[8,4,16,128]{3,2,1,0:T(8,128)S(1)} all-to-all(f32[8,4,16,128]{3,2,1,0:T(8,128)S(1)} %pack_field.1), channel_id=1, replica_groups=mesh['view'=8,'blk'=64] {'view'}, dimensions={0} | all-to-all | bytes 524288 | tf_op jit(solution)/shard_map/all_to_all | solution.py:575
  80.2 4.4 %iteration_both.1 = f32[8,32,128]{2,1,0:T(8,128)S(1)} custom-call(f32[8,16,512]{2,1,0:T(8,128)S(1)} %all-to-all-done.refs_0_, f32[8,4,16,128]{3,2,1,0:T(8,128)S(1)} %all_to_all.26.refs_1_, f32[8,4,16,128]{3,2,1,0:T(8,128)S(1)} %all-to-all-done.1.refs_1_.refs_2_, f32[8,16,384]{2,1,0:T(8,128)S(1)} %collective-permute-done.4.refs_3_, ...), custom_call_target="tpu_custom_call" | custom-call | flops 8000000000 | bytes 1000000 | tf_op jit(solution)/shard_map/iteration_both/pallas_call | solution.py:538
  84.6 8.5 %all_to_all.27 = f32[8,32,128]{2,1,0:T(8,128)S(1)} all-to-all(f32[8,32,128]{2,1,0:T(8,128)S(1)} %iteration_both.1), channel_id=1, replica_groups=mesh['view'=8,'blk'=64] {'view'}, dimensions={0} | all-to-all | bytes 262144 | tf_op jit(solution)/shard_map/all_to_all | solution.py:575
  93.1 0.7 copy.16
  (3 shorter events, 0.0 us)
Async XLA Ops:
  2.2 11.9 %all-to-all-start = ((f32[8,16,512]{2,1,0:T(8,128)}), f32[8,16,512]{2,1,0:T(8,128)S(1)}, u32[]{:S(2)}, u32[]{:S(2)}) async-start(f32[8,16,512]{2,1,0:T(8,128)} %pack_measured.1), calls=%async_computation | async-start | bytes 524288 | tf_op jit(solution)/shard_map/all_to_all | solution.py:575
  6.5 18.4 %collective-permute-start = (f32[2,16,1024]{2,1,0:T(8,128)}, f32[2,16,1024]{2,1,0:T(8,128)S(1)}, u32[]{:S(2)}, u32[]{:S(2)}) collective-permute-start(f32[2,16,1024]{2,1,0:T(8,128)} %param.12), channel_id=1, source_target_pairs={{0,1},{1,0},{2,3},{3,2},{4,5},{5,4},{6,7},{7,6},{8,9},{9,8},{10,11... | collective-permute-start | bytes 393224 | tf_op jit(solution)/shard_map/ppermute | solution.py:563
  14.1 10.8 %collective-permute-start.1 = (f32[16,128]{1,0:T(8,128)S(1)}, f32[16,128]{1,0:T(8,128)S(1)}, u32[]{:S(2)}, u32[]{:S(2)}) collective-permute-start(f32[16,128]{1,0:T(8,128)S(1)} %slice_reduce_fusion), channel_id=1, source_target_pairs={{0,1},{1,0},{2,3},{3,2},{4,5},{5,4},{6,7},{7,6},{8,9},{9,8},{10,11... | collective-permute-start | bytes 24584 | tf_op jit(solution)/shard_map/ppermute | solution.py:563
  16.7 12.7 %collective-permute-start.3 = (f32[8,16,384]{2,1,0:T(8,128)S(1)}, f32[8,16,384]{2,1,0:T(8,128)S(1)}, u32[]{:S(2)}, u32[]{:S(2)}) collective-permute-start(f32[8,16,384]{2,1,0:T(8,128)S(1)} %slice.9), channel_id=1, source_target_pairs={{1,2},{2,1},{3,4},{4,3},{5,6},{6,5},{7,8},{8,7},{9,10},{10,9},{11,... | collective-permute-start | bytes 589832 | tf_op jit(solution)/shard_map/ppermute | solution.py:571
  20.6 9.2 %collective-permute-start.2 = (f32[8,16,384]{2,1,0:T(8,128)S(1)}, f32[8,16,384]{2,1,0:T(8,128)S(1)}, u32[]{:S(2)}, u32[]{:S(2)}) collective-permute-start(f32[8,16,384]{2,1,0:T(8,128)S(1)} %slice.9), channel_id=1, source_target_pairs={{0,1},{1,0},{2,3},{3,2},{4,5},{5,4},{6,7},{7,6},{8,9},{9,8},{10,11... | collective-permute-start | bytes 589832 | tf_op jit(solution)/shard_map/ppermute | solution.py:571
  25.7 12.6 %all-to-all-start.1 = ((f32[8,4,16,128]{3,2,1,0:T(8,128)}), f32[8,4,16,128]{3,2,1,0:T(8,128)S(1)}, u32[]{:S(2)}, u32[]{:S(2)}) async-start(f32[8,4,16,128]{3,2,1,0:T(8,128)} %pack_estimate.1), calls=%async_computation.1 | async-start | bytes 524288 | tf_op jit(solution)/shard_map/all_to_all | solution.py:575
  29.8 14.6 %copy-start = (f32[8,8,1024]{2,1,0:T(8,128)S(1)}, f32[8,8,1024]{2,1,0:T(8,128)}, u32[]{:S(2)}) copy-start(f32[8,8,1024]{2,1,0:T(8,128)} %refs_7_.5) | copy-start | bytes 786436
  29.8 14.6 %collective-permute-start.4 = (f32[8,16,384]{2,1,0:T(8,128)S(1)}, f32[8,16,384]{2,1,0:T(8,128)S(1)}, u32[]{:S(2)}, u32[]{:S(2)}) collective-permute-start(f32[8,16,384]{2,1,0:T(8,128)S(1)} %get-tuple-element.24.refs_5_), channel_id=1, source_target_pairs={{1,2},{2,1},{3,4},{4,3},{5,6},{6,5},{7,8},{8,7},{9,10},{10,9},{11,... | collective-permute-start | bytes 589832 | tf_op jit(solution)/shard_map/ppermute | solution.py:571
  31.9 12.5 %collective-permute-start.5 = (f32[8,16,384]{2,1,0:T(8,128)S(1)}, f32[8,16,384]{2,1,0:T(8,128)S(1)}, u32[]{:S(2)}, u32[]{:S(2)}) collective-permute-start(f32[8,16,384]{2,1,0:T(8,128)S(1)} %get-tuple-element.25.refs_4_), channel_id=1, source_target_pairs={{0,1},{1,0},{2,3},{3,2},{4,5},{5,4},{6,7},{7,6},{8,9},{9,8},{10,11... | collective-permute-start | bytes 589832 | tf_op jit(solution)/shard_map/ppermute | solution.py:571
  57.0 6.8 %collective-permute-start.6 = (f32[8,32,128]{2,1,0:T(8,128)S(1)}, f32[8,32,128]{2,1,0:T(8,128)S(1)}, u32[]{:S(2)}, u32[]{:S(2)}) collective-permute-start(f32[8,32,128]{2,1,0:T(8,128)S(1)} %all_to_all.25), channel_id=1, source_target_pairs={{0,1},{1,0},{2,3},{3,2},{4,5},{5,4},{6,7},{7,6},{8,9},{9,8},{10,11... | collective-permute-start | bytes 393224 | tf_op jit(solution)/shard_map/ppermute | solution.py:563
